TPU v7x, 256 devices: a whole 4x4x8 slice. The times are simulated.
256 devices in a mesh: dp: 16 (over x_lo, z), sp: 16 (over x_hi, y, core).
Axes of the slice: x: 4 (x_hi: 2, x_lo: 2; x = x_hi * 2 + x_lo), y: 4, z: 8, core: 2. Of those that a mesh axis runs over, the one named last changes fastest.
Arguments:
- tokens: bfloat16 [16, 2048, 1536], P('dp', 'sp'), may hold values from -8 to 8
- norm_gain: bfloat16 [1536], replicated, may hold values from 0.099609375 to 1.8984375
- qkv_weight: bfloat16 [1536, 2304], P('sp', 'dp'), may hold values from -2 to 2
- d_context: bfloat16 [16, 2048, 768], P('dp', 'sp'), may hold values from -6 to 6
Outputs:
- context: bfloat16 [16, 2048, 768], P('dp', 'sp')
- d_tokens: bfloat16 [16, 2048, 1536], P('dp', 'sp')
- weight_grad: float32 [1536, 2304], P('sp', 'dp')
- gain_grad: float32 [1536], replicated
All inputs are finite; a program needn't handle non-finite values.
Results may differ from a plain program's by a relative error of at most 0.03.
Values may be sent and summed in bfloat16 or wider, within the bound.
A program may use at most 128 MiB of HBM per device.

v0:
```python
import math

import jax
import jax.numpy as jnp
from jax import lax
from jax.sharding import PartitionSpec as P

HEADS = 12
HEAD = 64


EPS = 1e-05


def layer_norm(values, gain_wide):
    centred = values - jnp.mean(values, axis=-1, keepdims=True)
    spread = jnp.mean(centred * centred, axis=-1, keepdims=True)
    return centred * lax.rsqrt(spread + EPS) * gain_wide


def rounded(values):
    return lax.optimization_barrier(values.astype(jnp.bfloat16)).astype(jnp.float32)


def shards(tokens, norm_gain, qkv_weight, d_context):
    row_count = tokens.shape[1]
    inner_width = d_context.shape[2]
    score_scale = HEAD ** (-0.5)
    columns = lax.all_gather(qkv_weight, "dp", axis=1, tiled=True)
    weights = lax.all_gather(columns, "sp", axis=0, tiled=True)
    inputs = tokens[0].astype(jnp.float32)
    gain_wide = norm_gain.astype(jnp.float32)
    normed = layer_norm(inputs, gain_wide).astype(jnp.bfloat16)
    projected = jnp.dot(normed, weights, preferred_element_type=jnp.float32).astype(jnp.bfloat16)
    queries = projected[:, :inner_width]
    keys_own = projected[:, inner_width : 2 * inner_width]
    values_own = projected[:, 2 * inner_width :]
    keys_all, values_all = (
        lax.all_gather(keys_own, "sp", axis=0, tiled=True),
        lax.all_gather(values_own, "sp", axis=0, tiled=True),
    )
    query_heads = queries.reshape(row_count, HEADS, HEAD)
    key_heads = keys_all.reshape(-1, HEADS, HEAD)
    value_heads = values_all.reshape(-1, HEADS, HEAD)
    cot_heads = d_context[0].reshape(row_count, HEADS, HEAD)
    scores = (
        jnp.einsum("thd,shd->hts", query_heads, key_heads, preferred_element_type=jnp.float32)
        * score_scale
    )
    row_top = jnp.max(scores, axis=-1, keepdims=True)
    exponent = jnp.exp(scores - row_top)
    attention = exponent / jnp.sum(exponent, axis=-1, keepdims=True)
    attention_low = attention.astype(jnp.bfloat16)
    context = jnp.einsum(
        "hts,shd->thd", attention_low, value_heads, preferred_element_type=jnp.float32
    )
    context = context.astype(jnp.bfloat16).reshape(row_count, inner_width)
    d_attn = jnp.einsum("thd,shd->hts", cot_heads, value_heads, preferred_element_type=jnp.float32)
    row_dot = jnp.sum(attention * d_attn, axis=-1, keepdims=True)
    slopes = (attention * (d_attn - row_dot)).astype(jnp.bfloat16)
    d_query = score_scale * jnp.einsum(
        "hts,shd->thd", slopes, key_heads, preferred_element_type=jnp.float32
    )
    d_query = d_query.astype(jnp.bfloat16).reshape(row_count, inner_width)
    d_key = score_scale * jnp.einsum(
        "hts,thd->shd", slopes, query_heads, preferred_element_type=jnp.float32
    )
    d_value = jnp.einsum(
        "hts,thd->shd", attention_low, cot_heads, preferred_element_type=jnp.float32
    )
    key_sums = lax.psum_scatter(
        rounded(
            jnp.concatenate(
                [
                    d_key.reshape(row_count * lax.axis_size("sp"), inner_width),
                    d_value.reshape(row_count * lax.axis_size("sp"), inner_width),
                ],
                axis=1,
            )
        ).astype(jnp.bfloat16),
        "sp",
        scatter_dimension=0,
        tiled=True,
    )
    d_proj = jnp.concatenate([d_query, key_sums], axis=1)
    d_normed = lax.dot_general(
        d_proj, weights, (((1,), (1,)), ((), ())), preferred_element_type=jnp.float32
    )
    _, pullback = jax.vjp(layer_norm, inputs, gain_wide)
    d_inputs, d_gain_local = pullback(d_normed)
    token_total = lax.axis_size("dp") * lax.axis_size("sp") * row_count
    factor = 1.0 / math.sqrt(token_total)
    slab_sums = lax.psum_scatter(
        rounded(
            lax.dot_general(
                normed, d_proj, (((0,), (0,)), ((), ())), preferred_element_type=jnp.float32
            )
        ).astype(jnp.bfloat16),
        "sp",
        scatter_dimension=0,
        tiled=True,
    )
    weight_grad = (
        lax.psum_scatter(slab_sums, "dp", scatter_dimension=1, tiled=True).astype(jnp.float32)
        * factor
    )
    gain_grad = lax.psum(d_gain_local, ("dp", "sp")) * factor
    return (context[None], d_inputs.astype(jnp.bfloat16)[None], weight_grad, gain_grad)


def solution(mesh):
    in_specs = (P("dp", "sp", None), P(), P("sp", "dp"), P("dp", "sp", None))
    out_specs = (P("dp", "sp", None), P("dp", "sp", None), P("sp", "dp"), P())
    return jax.shard_map(shards, mesh=mesh, in_specs=in_specs, out_specs=out_specs, check_vma=False)
```

profile of v0, /device:TPU:2, one launch (start us, length us, event | category | flops | bytes accessed | tf_op | source)
XLA Modules:
  0.0 557.8 jit_solution(10452537941667597884)
XLA Ops:
  7.2 39.2 %all_gather.12 = bf16[96,2304]{0,1:T(8,128)(2,1)S(1)} all-gather(bf16[96,144]{0,1:T(8,128)(2,1)} %param.6), channel_id=1, replica_groups=mesh['dp'=16,'sp'=16] {'dp'}, dimensions={1}, use_global_device_ids=true | all-gather | bytes 470016 | tf_op jit(solution)/shard_map/all_gather | solution.py:29
  50.6 65.5 %all-gather.4.cloned.1.call-done = bf16[1536,2304]{1,0:T(8,128)(2,1)} async-done(((bf16[96,2304]{1,0:T(8,128)(2,1)}), bf16[1536,2304]{1,0:T(8,128)(2,1)}) %all-gather.4.cloned.1.call-update) | async-done | bytes 7077904 | tf_op jit(solution)/shard_map/all_gather | solution.py:30
  116.1 4.3 convolution_convert_fusion.1
  122.4 52.6 %all-gather.8.cloned.1.call-done = bf16[2048,768]{1,0:T(8,128)(2,1)} async-done(((bf16[128,768]{1,0:T(8,128)(2,1)}), bf16[2048,768]{1,0:T(8,128)(2,1)}) %all-gather.8.cloned.1.call-update) | async-done | bytes 3145744 | tf_op jit(solution)/shard_map/all_gather | solution.py:39
  175.1 3.2 copy.37
  178.3 7.2 %fusion.38 = (f32[12,128]{1,0:T(8,128)}, f32[12,128,2048]{2,1,0:T(8,128)}) fusion(bf16[128,12,64]{0,2,1:T(8,128)(2,1)S(1)} %bitcast.82, bf16[2048,12,64]{0,2,1:T(8,128)(2,1)S(1)} %bitcast.75), kind=kOutput, calls=%fused_computation.53 | convolution fusion | flops 412092416 | bytes 15931392 | tf_op jit(solution)/shard_map/sub | solution.py:51
  185.4 7.3 %convolution_convert_fusion.2 = bf16[12,2048,64]{1,2,0:T(8,128)(2,1)} fusion(bf16[128,12,64]{0,2,1:T(8,128)(2,1)S(1)} %bitcast.86, f32[12,128,2048]{2,1,0:T(8,128)} %get-tuple-element.28, f32[12,128]{1,0:T(8,128)} %get-tuple-element.27), kind=kOutput, calls=%fused_computation.15 | convolution fusion | flops 410517504 | bytes 15931392 | tf_op jit(solution)/shard_map/hts,thd->shd/dot_general | solution.py:68
  192.8 40.3 %all-gather.6.cloned.1.call-done = bf16[2048,768]{1,0:T(8,128)(2,1)} async-done(((bf16[128,768]{1,0:T(8,128)(2,1)}), bf16[2048,768]{1,0:T(8,128)(2,1)}) %all-gather.6.cloned.1.call-update) | async-done | bytes 3145744 | tf_op jit(solution)/shard_map/all_gather | solution.py:40
  233.1 4.7 copy.35
  237.8 12.4 %fusion.1 = (f32[12,128]{1,0:T(8,128)S(1)}, f32[12,2048,128]{1,2,0:T(8,128)}) fusion(f32[12,128,2048]{2,1,0:T(8,128)} %get-tuple-element.28, f32[12,128]{1,0:T(8,128)} %get-tuple-element.27, bf16[2048,12,64]{0,2,1:T(8,128)(2,1)} %bitcast.78, bf16[128,12,64]{0,2,1:T(8,128)(2,1)S(1)} %bitcast.87), kind=kOutput, calls=%fused_computation.3 | convolution fusion | flops 412088832 | bytes 28520448 | tf_op jit(solution)/shard_map/thd,shd->hts/dot_general | solution.py:58
  250.2 5.8 %fusion.3 = bf16[12,128,2048]{2,1,0:T(8,128)(2,1)S(1)} fusion(f32[12,2048,128]{1,2,0:T(8,128)} %get-tuple-element.30, f32[12,128]{1,0:T(8,128)S(1)} %get-tuple-element.29, f32[12,128,2048]{2,1,0:T(8,128)S(1)} %bitcast.74, f32[12,128]{1,0:T(8,128)S(1)} %copy-done.6), kind=kLoop, calls=%fused_computation.5 | loop fusion | flops 12582912 | bytes 31469568 | tf_op jit(solution)/shard_map/convert_element_type | solution.py:60
  256.0 2.6 copy-done
  260.5 3.9 pad_maximum_fusion
  264.4 8.7 %copy.43 = bf16[2048,1536]{1,0:T(8,128)(2,1)} copy(bf16[2048,1536]{0,1:T(8,128)(2,1)} %pad_maximum_fusion) | data formatting | bytes 12582912
  273.3 5.7 %fusion.13 = bf16[12,64,128]{2,1,0:T(8,128)(2,1)} fusion(bf16[2048,12,64]{0,2,1:T(8,128)(2,1)S(1)} %bitcast.76, bf16[12,128,2048]{2,1,0:T(8,128)(2,1)} %copy-done), kind=kOutput, calls=%fused_computation.22 | convolution fusion | flops 402849792 | bytes 9633792 | tf_op jit(solution)/shard_map/hts,shd->thd/dot_general | solution.py:61
  279.0 90.4 %reduce-scatter.10.cloned.1.call-done = bf16[128,1536]{1,0:T(8,128)(2,1)} async-done(((bf16[2048,1536]{1,0:T(8,128)(2,1)}), bf16[128,1536]{1,0:T(8,128)(2,1)}) %reduce-scatter.10.cloned.1.call-update) | async-done | bytes 393232
  371.4 5.9 %convolution_convert_fusion = bf16[1536,2304]{1,0:T(8,128)(2,1)} fusion(bf16[128,1536]{0,1:T(8,128)(2,1)S(1)} %copy.44, bf16[128,768]{0,1:T(8,128)(2,1)} %bitcast.84, bf16[1,128,1536]{2,1,0:T(8,128)(2,1)S(1)} %copy-done.1, f32[1536]{0:T(1024)S(1)} %convert_element_type.49, f32[128]{0:T(128)S(1)} %fusion.30, f32[128]{0:T(128)S(1)} %broadcast_multiply_fusion.1), kind=kOutput, calls=%fused_computation.7 | convolution fusion | flops 911671296 | bytes 8068096 | tf_op jit(solution)/shard_map/dot_general | solution.py:95
  377.4 1.8 copy-done.2
  379.3 7.6 %fusion.14 = bf16[12,64,128]{2,1,0:T(8,128)(2,1)} fusion(bf16[2048,12,64]{0,2,1:T(8,128)(2,1)S(1)} %bitcast.79, f32[12,128,2048]{2,1,0:T(8,128)} %get-tuple-element.28, f32[12,128]{1,0:T(8,128)} %get-tuple-element.27), kind=kOutput, calls=%fused_computation.23 | convolution fusion | flops 409042944 | bytes 15931392 | tf_op jit(solution)/shard_map/hts,shd->thd/dot_general | solution.py:54
  388.6 6.4 %fusion.25 = (f32[1536]{0:T(1024)S(1)}, f32[128]{0:T(128)S(1)}, f32[128,1536]{1,0:T(8,128)S(1)}) fusion(bf16[1,128,1536]{2,1,0:T(8,128)(2,1)S(1)} %copy-done.1, f32[128]{0:T(128)S(1)} %fusion.30, f32[128]{0:T(128)S(1)} %broadcast_multiply_fusion.1, f32[1536]{0:T(1024)S(1)} %convert_element_type.49, bf16[1536,2304]{1,0:T(8,128)(2,1)} %all-gather.4.cloned.1.call-done, ...), kind=kOutput, calls=%fused_computation.34 | convolution fusion | flops 908720512 | bytes 8861184 | tf_op jit(solution)/shard_map/dot_general | solution.py:86
  395.1 77.0 %psum.7 = f32[1536]{0:T(1024)S(1)} all-reduce(f32[1536]{0:T(1024)S(1)} %get-tuple-element.20), channel_id=1, replica_groups=mesh['dp'=16,'sp'=16] {'dp','sp'}, use_global_device_ids=true, to_apply=%region_11.0 | all-reduce | flops 1536 | bytes 12288 | tf_op jit(solution)/shard_map/psum | solution.py:107
  472.4 5.2 reduce-scatter.8.cloned.1.call-done
  477.6 2.1 copy.45
  481.2 68.1 %reduce-scatter.12.cloned.1.call-done = bf16[144,96]{1,0:T(8,128)(2,1)} async-done(((bf16[2304,96]{1,0:T(8,128)(2,1)}), bf16[144,96]{1,0:T(8,128)(2,1)}) %reduce-scatter.12.cloned.1.call-update) | async-done | bytes 27664
  (55 shorter events, 15.4 us)
Async XLA Ops:
  7.2 114.9 %copy-start.5 = (bf16[1,128,768]{2,1,0:T(8,128)(2,1)S(1)}, bf16[1,128,768]{2,1,0:T(8,128)(2,1)}, u32[]{:S(2)}) copy-start(bf16[1,128,768]{2,1,0:T(8,128)(2,1)} %param.7) | copy-start | bytes 589828
  7.2 109.0 %all-gather.4.cloned.1.call-start = ((), (), s32[]{:S(2)}) async-start(), calls=%async_computation.3 | async-start | bytes 7520256 | tf_op jit(solution)/shard_map/all_gather | solution.py:30
  47.5 127.6 %all-gather.8.cloned.1.call-start = ((), (), s32[]{:S(2)}) async-start(), calls=%async_computation.5 | async-start | bytes 3342336 | tf_op jit(solution)/shard_map/all_gather | solution.py:39
  50.6 71.8 %copy-start.7 = (f32[128]{0:T(128)}, f32[128]{0:T(128)S(1)}, u32[]{:S(2)}) copy-start(f32[128]{0:T(128)S(1)} %fusion.26) | copy-start | bytes 1540
  121.3 111.8 %all-gather.6.cloned.1.call-start = ((), (), s32[]{:S(2)}) async-start(), calls=%async_computation.4 | async-start | bytes 3342336 | tf_op jit(solution)/shard_map/all_gather | solution.py:40
  122.0 247.4 %reduce-scatter.10.cloned.1.call-start = ((), (), s32[]{:S(2)}) async-start(), calls=%async_computation.7 | async-start | bytes 6684672
  237.8 12.4 %slice-start = ((s8[12582912]{0:T(1024)(128)(4,1)}), s8[4194304]{0:T(1024)(128)(4,1)S(1)}, s32[]{:S(2)}) async-start(s8[12582912]{0:T(1024)(128)(4,1)} %bitcast.73), calls=%async_computation.9 | async-start | bytes 8388608
  237.8 12.4 %slice-start.1 = ((s8[12582912]{0:T(1024)(128)(4,1)}), s8[4194304]{0:T(1024)(128)(4,1)S(1)}, s32[]{:S(2)}) async-start(s8[12582912]{0:T(1024)(128)(4,1)} %bitcast.73), calls=%async_computation.10 | async-start | bytes 8388608
  237.8 12.4 %slice-start.2 = ((s8[12582912]{0:T(1024)(128)(4,1)}), s8[4194304]{0:T(1024)(128)(4,1)S(1)}, s32[]{:S(2)}) async-start(s8[12582912]{0:T(1024)(128)(4,1)} %bitcast.73), calls=%async_computation.11 | async-start | bytes 8388608
  237.8 12.4 %copy-start.6 = (f32[12,128]{1,0:T(8,128)S(1)}, f32[12,128]{1,0:T(8,128)}, u32[]{:S(2)}) copy-start(f32[12,128]{1,0:T(8,128)} %get-tuple-element.27) | copy-start | bytes 18436
  256.0 2.6 copy-start
  258.6 1.9 copy-start.3
  273.1 98.4 %copy-start.1 = (bf16[1,128,1536]{2,1,0:T(8,128)(2,1)S(1)}, bf16[1,128,1536]{2,1,0:T(8,128)(2,1)}, u32[]{:S(2)}) copy-start(bf16[1,128,1536]{2,1,0:T(8,128)(2,1)} %param.4) | copy-start | bytes 1179652
  273.1 204.6 %reduce-scatter.8.cloned.1.call-start = ((), (), s32[]{:S(2)}) async-start(), calls=%async_computation.6 | async-start | bytes 7520256 | tf_op jit(solution)/shard_map/reduce_scatter | solution.py:93
  370.7 0.7 copy-start.4
  377.4 1.9 copy-start.2
  377.4 171.9 %reduce-scatter.12.cloned.1.call-start = ((), (), s32[]{:S(2)}) async-start(), calls=%async_computation.8 | async-start | bytes 626688
  386.9 85.2 %copy-start.8 = (f32[128]{0:T(128)S(1)}, f32[128]{0:T(128)}, u32[]{:S(2)}) copy-start(f32[128]{0:T(128)} %copy-done.7) | copy-start | bytes 1540
Sparse Core Ops, SparseCore 0:
  47.6 68.5 all-gather.3
  121.4 53.6 all-gather.7
  178.4 54.5 all-gather.5
  273.2 96.2 reduce-scatter.9
  377.5 100.0 reduce-scatter.7
  480.0 69.2 reduce-scatter.11
where the time goes:
time: 560 us; the launch traced here: 558 us
  waiting for transfers between devices  323 us (58%)
  blocking collectives  116 us (21%)
  matrix products  58 us (10%)
  local copies, waits for them, and re-layouts  31.3 us (6%)
  other arithmetic  14.6 us (3%)
  between operations  14.3 us (3%)
    unnamed x8, waiting for transfers between devices  159 us
    psum x1, blocking collectives, shards(): gain_grad = lax.psum(d_gain_local, ('dp', 'sp')) * factor  77 us
    all_gather x1, waiting for transfers between devices, shards(): weights = lax.all_gather(columns, 'sp', axis=0, tiled=True)  65.5 us
    all_gather x1, waiting for transfers between devices, shards(): lax.all_gather(keys_own, 'sp', axis=0, tiled=True)  52.6 us
    all_gather x1, waiting for transfers between devices, shards(): lax.all_gather(values_own, 'sp', axis=0, tiled=True)  40.3 us
    all_gather x1, blocking collectives, shards(): columns = lax.all_gather(qkv_weight, 'dp', axis=1, tiled=True)  39.2 us
    unnamed x31, local copies, waits for them, and re-layouts  21.5 us
    dot_general x1, matrix products, shards(): jnp.einsum('thd,shd->hts', cot_heads, value_heads, preferred_element_type...  12.4 us
  transfers between devices with their start and end apart: 6, of which 6 were waited for; matrix products, arithmetic and copies ran while one was open for 8% of the time, Pallas kernels for 0%

commit v1 on v0

v1 whole, which is shorter than its diff:
```python
import functools
import math

import jax
import jax.numpy as jnp
from jax import lax
from jax.experimental import pallas as pl
from jax.experimental.pallas import tpu as pltpu
from jax.sharding import PartitionSpec as P

MESH = pl.DeviceIdType.MESH
BF = jnp.bfloat16
F32 = jnp.float32

D = 1536
HEAD = 64
OWN = 3
TOK = 128
NY = 4
NZ = 8
NA = 4
ROWS = NY * TOK
SEQ = NA * ROWS
QW = OWN * HEAD
PW = 3 * QW
SLAB = 96
BLOCK = 144
GW = NY * SLAB
EPS = 1e-05
VMEM = pl.BlockSpec(memory_space=pltpu.VMEM)


class Place:
    def __init__(self):
        d, s = lax.axis_index("dp"), lax.axis_index("sp")
        self.x_lo, self.z = d // NZ, d % NZ
        self.x_hi, self.y, self.core = s // 8, (s // 2) % NY, s % 2
        self.group = self.x_hi * 2 + self.core
        self.far_group = (1 - self.x_hi) * 2 + self.core

    def id(self, x_hi=None, x_lo=None, y=None, z=None, core=None):
        x_hi = self.x_hi if x_hi is None else x_hi
        x_lo = self.x_lo if x_lo is None else x_lo
        y = self.y if y is None else y
        z = self.z if z is None else z
        core = self.core if core is None else core
        return {"dp": x_lo * NZ + z, "sp": x_hi * 8 + y * 2 + core}

    def other_core(self):
        return self.id(core=1 - self.core)

    def mirror(self):
        return self.id(x_hi=1 - self.x_hi, x_lo=1 - self.x_lo)

    def beside(self):
        return self.id(x_lo=1 - self.x_lo)

    def far(self):
        return self.id(x_hi=1 - self.x_hi)

    def along_y(self, step):
        return self.id(y=(self.y + step) % NY)

    def along_z(self, step):
        return self.id(z=(self.z + step) % NZ)

    def along_x(self, step):
        x = (self.x_hi * 2 + self.x_lo + step) % 4
        return self.id(x_hi=x // 2, x_lo=x % 2)


def greet(partners):
    barrier = pltpu.get_barrier_semaphore()
    for partner in partners:
        pl.semaphore_signal(barrier, inc=1, device_id=partner, device_id_type=MESH)
    return functools.partial(pl.semaphore_wait, barrier, len(partners))


def remote(src, dst, send, recv, partner):
    return pltpu.make_async_remote_copy(
        src_ref=src, dst_ref=dst, send_sem=send, recv_sem=recv, device_id=partner, device_id_type=MESH
    )


def rows_at(start, size):
    return pl.ds(pl.multiple_of(start, 16), size)


def lanes_at(start, size):
    return pl.ds(pl.multiple_of(start, 128), size)


def to_grouped(wide):
    parts = []
    for x_hi in range(2):
        for core in range(2):
            for y in range(NY):
                s = x_hi * 8 + y * 2 + core
                parts.append(wide[:, s * SLAB : (s + 1) * SLAB])
    return jnp.concatenate(parts, axis=1)


def to_natural(wide):
    parts = []
    for x_hi in range(2):
        for y in range(NY):
            for core in range(2):
                s = (x_hi * 2 + core) * NY + y
                parts.append(wide[:, s * SLAB : (s + 1) * SLAB])
    return jnp.concatenate(parts, axis=1)


def wire_row(piece):
    if piece < OWN:
        return piece * HEAD
    head, which = (piece - OWN) // 2, (piece - OWN) % 2
    return QW * (1 + which) + head * HEAD


def gather_kernel(x_ref, gain_ref, w_ref, cot_ref, nall, wall, cots,
                  wd, wy, ns, nr, cs, cr, zs, zr, bs, br, ys, yr, gs, gr):
    me = Place()
    y = me.y
    partners = (
        [me.along_z(r) for r in range(1, NZ)]
        + [me.along_y(r) for r in range(1, NY)]
        + [me.beside(), me.mirror(), me.other_core()]
    )
    ready = greet(partners)
    own_rows = rows_at((me.x_lo * NZ + me.z) * BLOCK, BLOCK)
    wd[own_rows, :] = w_ref[...]
    ready()
    z_copies, b_copies = [], []
    for r in range(1, NZ):
        c = remote(wd.at[own_rows, :], wd.at[own_rows, :], zs.at[r], zr.at[r], me.along_z(r))
        c.start()
        z_copies.append(c)
    c = remote(wd.at[own_rows, :], wd.at[own_rows, :], bs.at[0], br.at[0], me.beside())
    c.start()
    b_copies.append(c)

    x = x_ref[...].astype(F32)
    centred = x - jnp.mean(x, axis=1, keepdims=True)
    spread = jnp.mean(centred * centred, axis=1, keepdims=True)
    normed = centred * lax.rsqrt(spread + EPS) * gain_ref[...]
    tok_rows = rows_at(y * TOK, TOK)
    nall[tok_rows, :] = to_grouped(normed).astype(BF)
    right, left = me.along_y(1), me.along_y(3)
    n_right = remote(nall.at[tok_rows, :], nall.at[tok_rows, :], ns.at[0], nr.at[0], right)
    n_left = remote(nall.at[tok_rows, :], nall.at[tok_rows, :], ns.at[1], nr.at[1], left)
    n_right.start()
    n_left.start()
    cot_copies = []
    cot_lanes = lanes_at(y * TOK, TOK)
    for r in range(1, NY):
        to = (y + r) % NY
        c = remote(cot_ref.at[rows_at(to * QW, QW), :], cots.at[:, cot_lanes], cs.at[r], cr.at[r], me.along_y(r))
        c.start()
        cot_copies.append(c)
    cots[:, cot_lanes] = cot_ref[rows_at(y * QW, QW), :]

    for r in (1, 7, 2, 6, 3, 5, 4):
        z_copies[r - 1].wait_recv()
        rows = rows_at((me.x_lo * NZ + (me.z + NZ - r) % NZ) * BLOCK, BLOCK)
        c = remote(wd.at[rows, :], wd.at[rows, :], bs.at[r], br.at[r], me.beside())
        c.start()
        b_copies.append(c)
    half = TOK // 2
    from_left = rows_at(((y + 3) % NY) * TOK, half)
    from_right = rows_at(((y + 1) % NY) * TOK + half, half)
    n_right.wait_recv()
    f_right = remote(nall.at[from_left, :], nall.at[from_left, :], ns.at[2], nr.at[2], right)
    f_right.start()
    n_left.wait_recv()
    f_left = remote(nall.at[from_right, :], nall.at[from_right, :], ns.at[3], nr.at[3], left)
    f_left.start()

    for c in b_copies:
        c.wait_recv()
    y_copies = []
    for r in range(1, NY):
        to = (y + r) % NY
        for k in range(3):
            c = remote(
                wd.at[rows_at(k * NY * QW + to * QW, QW), :],
                wy.at[y, pl.ds(k * QW, QW), :],
                ys.at[r, k],
                yr.at[r, k],
                me.along_y(r),
            )
            c.start()
            y_copies.append(c)
    for k in range(3):
        wy[y, k * QW : (k + 1) * QW, :] = wd[rows_at(k * NY * QW + y * QW, QW), :]
    for c in y_copies:
        c.wait_recv()
    own = lanes_at(me.group * GW, GW)
    for piece in range(3 * OWN):
        row = wire_row(piece)
        parts = [wy[k, row : row + HEAD, :][:, :SLAB].astype(F32) for k in range(NY)]
        wall[piece * HEAD : (piece + 1) * HEAD, own] = jnp.concatenate(parts, axis=1).astype(BF)
    far = lanes_at(me.far_group * GW, GW)
    g_far = remote(wall.at[:, own], wall.at[:, own], gs.at[0], gr.at[0], me.mirror())
    g_core = remote(wall.at[:, own], wall.at[:, own], gs.at[1], gr.at[1], me.other_core())
    g_far.start()
    g_core.start()
    g_far.wait_recv()
    g_pass = remote(wall.at[:, far], wall.at[:, far], gs.at[2], gr.at[2], me.other_core())
    g_pass.start()
    g_core.wait_recv()
    g_pass.wait_recv()
    f_right.wait_recv()
    f_left.wait_recv()
    for c in cot_copies:
        c.wait_recv()
    for c in (
        z_copies + b_copies + y_copies + cot_copies
        + [n_right, n_left, f_right, f_left, g_far, g_core, g_pass]
    ):
        c.wait_send()


def dma(*shape):
    return pltpu.SemaphoreType.DMA(shape)


def gather(x, gain, w, cot):
    return pl.pallas_call(
        gather_kernel,
        out_shape=(
            jax.ShapeDtypeStruct((ROWS, D), BF),
            jax.ShapeDtypeStruct((PW, D), BF),
            jax.ShapeDtypeStruct((QW, ROWS), BF),
        ),
        in_specs=[VMEM] * 4,
        out_specs=(VMEM,) * 3,
        scratch_shapes=[
            pltpu.VMEM((16 * BLOCK, 128), BF),
            pltpu.VMEM((NY, PW, 128), BF),
            dma(4), dma(4), dma(4), dma(4), dma(8), dma(8), dma(8), dma(8),
            dma(4, 3), dma(4, 3), dma(3), dma(3),
        ],
        compiler_params=pltpu.CompilerParams(
            collective_id=0, has_side_effects=True, vmem_limit_bytes=48 * 2**20
        ),
        name="gather",
    )(x, gain, w, cot)


def keys_kernel(kv_ref, kvall, ss, rs):
    me = Place()
    ready = greet([me.far(), me.other_core()])
    own = rows_at(me.group * ROWS, ROWS)
    far = rows_at(me.far_group * ROWS, ROWS)
    ready()
    c_far = remote(kv_ref, kvall.at[own, :], ss.at[0], rs.at[0], me.far())
    c_core = remote(kv_ref, kvall.at[own, :], ss.at[1], rs.at[1], me.other_core())
    c_far.start()
    c_core.start()
    kvall[own, :] = kv_ref[...]
    c_far.wait_recv()
    c_pass = remote(kvall.at[far, :], kvall.at[far, :], ss.at[2], rs.at[2], me.other_core())
    c_pass.start()
    c_core.wait_recv()
    c_pass.wait_recv()
    for c in (c_far, c_core, c_pass):
        c.wait_send()


def keys(kv):
    return pl.pallas_call(
        keys_kernel,
        out_shape=jax.ShapeDtypeStruct((SEQ, 2 * QW), BF),
        in_specs=[VMEM],
        out_specs=VMEM,
        scratch_shapes=[dma(3), dma(3)],
        compiler_params=pltpu.CompilerParams(
            collective_id=1, has_side_effects=True, vmem_limit_bytes=48 * 2**20
        ),
        name="keys",
    )(kv)


CHUNK = 256


def attention_kernel(kv_ref, q_ref, cot_ref, ctx_ref, dq_ref, dkv_ref, s_buf, e_buf):
    chunks = SEQ // CHUNK
    q = q_ref[...] * jnp.asarray(HEAD**-0.5, BF)
    zeros = jnp.zeros((HEAD, ROWS), BF)
    q_pad = jnp.concatenate([q, zeros], axis=0)
    top = jnp.full((8, ROWS), -jnp.inf, F32)
    for i in range(chunks):
        rows = slice(i * CHUNK, (i + 1) * CHUNK)
        s = jnp.dot(kv_ref[rows, :], q_pad, preferred_element_type=F32)
        s_buf[rows, :] = s
        top = jnp.maximum(top, jnp.max(s.reshape(CHUNK // 8, 8, ROWS), axis=0))
    top = jnp.max(top, axis=0, keepdims=True)
    total = jnp.zeros((8, ROWS), F32)
    ctx = jnp.zeros((HEAD, ROWS), F32)
    for i in range(chunks):
        rows = slice(i * CHUNK, (i + 1) * CHUNK)
        e = jnp.exp(s_buf[rows, :] - top)
        total = total + jnp.sum(e.reshape(CHUNK // 8, 8, ROWS), axis=0)
        e_low = e.astype(BF)
        e_buf[rows, :] = e_low
        v_t = kv_ref[rows, :].T[HEAD:, :]
        ctx = ctx + jnp.dot(v_t, e_low, preferred_element_type=F32)
    inverse = 1.0 / jnp.sum(total, axis=0, keepdims=True)
    ctx = ctx * inverse
    ctx_ref[...] = ctx.astype(BF)
    cot = (cot_ref[...].astype(F32) * inverse).astype(BF)
    row_dot = jnp.sum(cot.astype(F32) * ctx, axis=0, keepdims=True)
    cot_pad = jnp.concatenate([zeros, cot], axis=0)
    q_side = jnp.concatenate([q, zeros], axis=0).T
    cot_side = cot_pad.T
    dq = jnp.zeros((HEAD, ROWS), F32)
    for i in range(chunks):
        rows = slice(i * CHUNK, (i + 1) * CHUNK)
        d_attn = jnp.dot(kv_ref[rows, :], cot_pad, preferred_element_type=F32)
        e_low = e_buf[rows, :]
        slopes = (e_low.astype(F32) * (d_attn - row_dot)).astype(BF)
        k_t = kv_ref[rows, :].T[:HEAD, :]
        dq = dq + jnp.dot(k_t, slopes, preferred_element_type=F32)
        dkv_ref[rows, :] = (
            jnp.dot(slopes, q_side, preferred_element_type=F32)
            + jnp.dot(e_low, cot_side, preferred_element_type=F32)
        ).astype(BF)
    dq_ref[...] = (dq * HEAD**-0.5).astype(BF)


def attend(kv, q, cot):
    return pl.pallas_call(
        attention_kernel,
        grid=(OWN,),
        out_shape=(
            jax.ShapeDtypeStruct((QW, ROWS), BF),
            jax.ShapeDtypeStruct((QW, ROWS), BF),
            jax.ShapeDtypeStruct((SEQ, 2 * QW), BF),
        ),
        in_specs=[
            pl.BlockSpec((SEQ, 128), lambda h: (0, h)),
            pl.BlockSpec((HEAD, ROWS), lambda h: (h, 0)),
            pl.BlockSpec((HEAD, ROWS), lambda h: (h, 0)),
        ],
        out_specs=(
            pl.BlockSpec((HEAD, ROWS), lambda h: (h, 0)),
            pl.BlockSpec((HEAD, ROWS), lambda h: (h, 0)),
            pl.BlockSpec((SEQ, 128), lambda h: (0, h)),
        ),
        scratch_shapes=[pltpu.VMEM((SEQ, ROWS), F32), pltpu.VMEM((SEQ, ROWS), BF)],
        compiler_params=pltpu.CompilerParams(vmem_limit_bytes=48 * 2**20),
        name="attention",
    )(kv, q, cot)


def key_sums_kernel(dkv_ref, ctx_ref, out_ref, ctx_out, r1, mid, r2, ss, rs, cs, cr):
    me = Place()
    y = me.y
    ready = greet([me.far(), me.other_core()] + [me.along_y(r) for r in range(1, NY)])
    own = rows_at(me.group * ROWS, ROWS)
    far = rows_at(me.far_group * ROWS, ROWS)
    own_there = rows_at((me.x_hi * 2 + 1 - me.core) * ROWS, ROWS)
    far_there = rows_at(((1 - me.x_hi) * 2 + 1 - me.core) * ROWS, ROWS)
    ready()
    c_far = remote(dkv_ref.at[far_there, :], r1.at[0], ss.at[0], rs.at[0], me.other_core())
    c_own = remote(dkv_ref.at[own_there, :], r1.at[1], ss.at[1], rs.at[1], me.other_core())
    c_far.start()
    c_own.start()
    ctx_copies = []
    mine = rows_at(y * QW, QW)
    for r in range(1, NY):
        to = (y + r) % NY
        c = remote(ctx_ref.at[:, lanes_at(to * TOK, TOK)], ctx_out.at[mine, :], cs.at[r], cr.at[r], me.along_y(r))
        c.start()
        ctx_copies.append(c)
    ctx_out[mine, :] = ctx_ref[:, lanes_at(y * TOK, TOK)]
    c_far.wait_recv()
    mid[...] = (dkv_ref[far, :].astype(F32) + r1[0].astype(F32)).astype(BF)
    c_x = remote(mid, r2, ss.at[2], rs.at[2], me.far())
    c_x.start()
    c_own.wait_recv()
    c_x.wait_recv()
    out_ref[...] = (dkv_ref[own, :].astype(F32) + r1[1].astype(F32) + r2[...].astype(F32)).astype(BF)
    for c in ctx_copies:
        c.wait_recv()
    for c in [c_far, c_own, c_x] + ctx_copies:
        c.wait_send()


def key_sums(dkv, ctx):
    return pl.pallas_call(
        key_sums_kernel,
        out_shape=(
            jax.ShapeDtypeStruct((ROWS, 2 * QW), BF),
            jax.ShapeDtypeStruct((NY * QW, TOK), BF),
        ),
        in_specs=[VMEM] * 2,
        out_specs=(VMEM,) * 2,
        scratch_shapes=[
            pltpu.VMEM((2, ROWS, 2 * QW), BF),
            pltpu.VMEM((ROWS, 2 * QW), BF),
            pltpu.VMEM((ROWS, 2 * QW), BF),
            dma(3), dma(3), dma(4), dma(4),
        ],
        compiler_params=pltpu.CompilerParams(
            collective_id=2, has_side_effects=True, vmem_limit_bytes=48 * 2**20
        ),
        name="key_sums",
    )(dkv, ctx)


def sums_kernel(dn_ref, wg_ref, gg_ref, x_ref, gain_ref, dx_ref, wout_ref, gout_ref,
                half_r, to_right, to_left, full_r, wr1, s1, wr2, wyo, wd, wb, wz, zbuf,
                gcore, gy, gx, gz,
                ns, nr, ws, wr, ys, yr, zs, zr, gs, gr):
    me = Place()
    y = me.y
    partners = (
        [me.along_z(r) for r in range(1, NZ)]
        + [me.along_y(r) for r in range(1, NY)]
        + [me.along_x(r) for r in range(1, 4)]
        + [me.other_core()]
    )
    ready = greet(partners)
    ready()
    sent = []

    def go(*args):
        c = remote(*args)
        c.start()
        sent.append(c)
        return c

    def group(x_hi, core):
        return lanes_at((x_hi * 2 + core) * GW, GW)

    other = 1 - me.core
    w_far = go(wg_ref.at[:, group(1 - me.x_hi, other)], wr1.at[0], ws.at[0], wr.at[0], me.other_core())
    w_own = go(wg_ref.at[:, group(me.x_hi, other)], wr1.at[1], ws.at[1], wr.at[1], me.other_core())
    half = TOK // 2
    right, left = me.along_y(1), me.along_y(3)
    opposite = ((y + 2) % NY) * TOK
    h_right = go(dn_ref.at[rows_at(opposite, half), :], half_r.at[0], ns.at[0], nr.at[0], right)
    h_left = go(dn_ref.at[rows_at(opposite + half, half), :], half_r.at[1], ns.at[1], nr.at[1], left)
    gcore[me.core] = gg_ref[...]
    g_core = go(gg_ref, gcore.at[me.core], gs.at[0], gr.at[0], me.other_core())

    w_far.wait_recv()
    s1[...] = (wg_ref[:, group(1 - me.x_hi, me.core)].astype(F32) + wr1[0].astype(F32)).astype(BF)
    w_x = go(s1, wr2, ws.at[2], wr.at[2], me.mirror())

    h_right.wait_recv()
    block = rows_at(((y + 1) % NY) * TOK, half)
    rest = rows_at(((y + 1) % NY) * TOK + half, half)
    to_right[:half, :] = (dn_ref[block, :].astype(F32) + half_r[0].astype(F32)).astype(BF)
    to_right[half:, :] = dn_ref[rest, :]
    f_right = go(to_right, full_r.at[0], ns.at[2], nr.at[2], right)
    h_left.wait_recv()
    block = rows_at(((y + 3) % NY) * TOK, half)
    rest = rows_at(((y + 3) % NY) * TOK + half, half)
    to_left[:half, :] = dn_ref[block, :]
    to_left[half:, :] = (dn_ref[rest, :].astype(F32) + half_r[1].astype(F32)).astype(BF)
    f_left = go(to_left, full_r.at[1], ns.at[3], nr.at[3], left)

    g_core.wait_recv()
    gy[y] = gcore[0] + gcore[1]
    g_y = [go(gy.at[y], gy.at[y], gs.at[r], gr.at[r], me.along_y(r)) for r in range(1, NY)]

    w_own.wait_recv()
    w_x.wait_recv()
    for piece in range(3 * OWN):
        rows = slice(piece * HEAD, (piece + 1) * HEAD)
        dense = wg_ref[rows, group(me.x_hi, me.core)].astype(F32) + wr1[1, rows, :].astype(F32) + wr2[rows, :].astype(F32)
        row = wire_row(piece)
        for k in range(NY):
            part = dense[:, k * SLAB : (k + 1) * SLAB]
            part = jnp.concatenate([part, jnp.zeros((HEAD, 128 - SLAB), F32)], axis=1)
            wyo[k, row : row + HEAD, :] = part.astype(BF)
    w_y = []
    for r in range(1, NY):
        to = (y + r) % NY
        for k in range(3):
            w_y.append(go(
                wyo.at[to, pl.ds(k * QW, QW), :],
                wd.at[rows_at(k * NY * QW + y * QW, QW), :],
                ys.at[r, k], yr.at[r, k], me.along_y(r),
            ))
    for k in range(3):
        wd[rows_at(k * NY * QW + y * QW, QW), :] = wyo[y, k * QW : (k + 1) * QW, :]

    for c in g_y:
        c.wait_recv()
    x_at = me.x_hi * 2 + me.x_lo
    gx[x_at] = gy[0] + gy[1] + gy[2] + gy[3]
    g_x = [go(gx.at[x_at], gx.at[x_at], gs.at[3 + r], gr.at[3 + r], me.along_x(r)) for r in range(1, 4)]

    for c in w_y:
        c.wait_recv()
    span = NZ * BLOCK
    w_b = go(wd.at[rows_at((1 - me.x_lo) * span, span), :], wb, ws.at[3], wr.at[3], me.beside())

    for c in g_x:
        c.wait_recv()
    gz[me.z] = gx[0] + gx[1] + gx[2] + gx[3]
    g_z = [go(gz.at[me.z], gz.at[me.z], gs.at[6 + r], gr.at[6 + r], me.along_z(r)) for r in range(1, NZ)]

    f_right.wait_recv()
    f_left.wait_recv()
    d_normed = (
        dn_ref[rows_at(y * TOK, TOK), :].astype(F32) + full_r[0].astype(F32) + full_r[1].astype(F32)
    )
    d_normed = to_natural(d_normed)
    x = x_ref[...].astype(F32)
    centred = x - jnp.mean(x, axis=1, keepdims=True)
    spread = jnp.mean(centred * centred, axis=1, keepdims=True)
    scale = lax.rsqrt(spread + EPS)
    hat = centred * scale
    inner = d_normed * gain_ref[...]
    first = jnp.mean(inner, axis=1, keepdims=True)
    second = jnp.mean(inner * hat, axis=1, keepdims=True)
    dx_ref[...] = (scale * (inner - first - hat * second)).astype(BF)

    w_b.wait_recv()
    for k in range(NZ):
        at = rows_at(me.x_lo * span + k * BLOCK, BLOCK)
        wz[k * BLOCK : (k + 1) * BLOCK, :] = (
            wd[at, :].astype(F32) + wb[k * BLOCK : (k + 1) * BLOCK, :].astype(F32)
        ).astype(BF)
    w_z = []
    for r in range(1, NZ):
        to = (me.z + r) % NZ
        w_z.append(go(wz.at[rows_at(to * BLOCK, BLOCK), :], zbuf.at[r], zs.at[r], zr.at[r], me.along_z(r)))
    for c in g_z:
        c.wait_recv()
    total = gz[0]
    for k in range(1, NZ):
        total = total + gz[k]
    gout_ref[...] = total
    total = wz[rows_at(me.z * BLOCK, BLOCK), :].astype(F32)
    for r in range(1, NZ):
        w_z[r - 1].wait_recv()
        total = total + zbuf[r].astype(F32)
    wout_ref[...] = total
    for c in sent:
        c.wait_send()


def sums(dn, wg, gg, x, gain):
    span = NZ * BLOCK
    return pl.pallas_call(
        sums_kernel,
        out_shape=(
            jax.ShapeDtypeStruct((TOK, D), BF),
            jax.ShapeDtypeStruct((BLOCK, 128), F32),
            jax.ShapeDtypeStruct((16, 128), F32),
        ),
        in_specs=[VMEM] * 5,
        out_specs=(VMEM,) * 3,
        scratch_shapes=[
            pltpu.VMEM((2, TOK // 2, D), BF),
            pltpu.VMEM((TOK, D), BF),
            pltpu.VMEM((TOK, D), BF),
            pltpu.VMEM((2, TOK, D), BF),
            pltpu.VMEM((2, PW, GW), BF),
            pltpu.VMEM((PW, GW), BF),
            pltpu.VMEM((PW, GW), BF),
            pltpu.VMEM((NY, PW, 128), BF),
            pltpu.VMEM((2 * span, 128), BF),
            pltpu.VMEM((span, 128), BF),
            pltpu.VMEM((span, 128), BF),
            pltpu.VMEM((NZ, BLOCK, 128), BF),
            pltpu.VMEM((2, 16, 128), F32),
            pltpu.VMEM((NY, 16, 128), F32),
            pltpu.VMEM((4, 16, 128), F32),
            pltpu.VMEM((NZ, 16, 128), F32),
            dma(4), dma(4), dma(4), dma(4), dma(4, 3), dma(4, 3), dma(8), dma(8), dma(14), dma(14),
        ],
        compiler_params=pltpu.CompilerParams(
            collective_id=3, has_side_effects=True, vmem_limit_bytes=48 * 2**20
        ),
        name="sums",
    )(dn, wg, gg, x, gain)


def shards(tokens, norm_gain, qkv_weight, d_context):
    x = tokens[0]
    gain = norm_gain.astype(F32)[None, :]
    w_own = jnp.pad(qkv_weight.T, ((0, 0), (0, 128 - SLAB)))
    normed, weights, cot = gather(x, gain, w_own, d_context[0].T)
    q = lax.dot_general(weights[:QW], normed, (((1,), (1,)), ((), ())), preferred_element_type=F32).astype(BF)
    kv = lax.dot_general(normed, weights[QW:], (((1,), (1,)), ((), ())), preferred_element_type=F32).astype(BF)
    kv_all = keys(kv)
    context, d_query, d_kv = attend(kv_all, q, cot)
    kv_sums, context = key_sums(d_kv, context)
    d_proj = jnp.concatenate([d_query.T, kv_sums], axis=1)
    d_normed = jnp.dot(d_proj, weights, preferred_element_type=F32).astype(BF)
    grad = lax.dot_general(d_proj, normed, (((0,), (0,)), ((), ())), preferred_element_type=F32)
    gain_terms = jnp.sum(grad * weights.astype(F32), axis=0)
    gain_terms = jnp.pad(gain_terms.reshape(12, 128), ((0, 4), (0, 0)))
    d_tokens, weight_sums, gain_sums = sums(d_normed, grad.astype(BF), gain_terms, x, gain)
    factor = 1.0 / math.sqrt(16 * SEQ)
    weight_grad = weight_sums[:, :SLAB].T * factor
    gain_grad = gain_sums[:12].reshape(2, 2, NY, SLAB).transpose(0, 2, 1, 3).reshape(D)
    gain_grad = gain_grad / norm_gain.astype(F32) * factor
    return (context.T[None], d_tokens[None], weight_grad, gain_grad)


def solution(mesh):
    in_specs = (P("dp", "sp", None), P(), P("sp", "dp"), P("dp", "sp", None))
    out_specs = (P("dp", "sp", None), P("dp", "sp", None), P("sp", "dp"), P())
    return jax.shard_map(shards, mesh=mesh, in_specs=in_specs, out_specs=out_specs, check_vma=False)
```

time: 560 us -> 145 us (0.26)
  waiting for transfers between devices: 323 us -> 0 us
  Pallas kernels: 0 us -> 131 us
  blocking collectives: 116 us -> 0 us
  matrix products: 58 us -> 5.79 us
  local copies, waits for them, and re-layouts: 31.3 us -> 5.92 us
  between operations: 14.3 us -> 0.76 us
  other arithmetic: 14.6 us -> 1.25 us
    unnamed x8 -> x0, waiting for transfers between devices: 159 us -> none
    all_gather x3 -> x0, waiting for transfers between devices: 158 us -> none  [the longest x1 65.5 us: shards(): weights = lax.all_gather(columns, 'sp', axis=0, tiled=True)]
    pallas_call x0 -> x5, Pallas kernels: none -> 131 us  [the longest x1 45.1 us: gather(): pl.pallas_call(gather_kernel, out_shape=(jax.ShapeDtypeStruct((ROWS, D),...]
    psum x1 -> x0, blocking collectives: 77 us -> none  [shards(): gain_grad = lax.psum(d_gain_local, ('dp', 'sp')) * factor]
    dot_general x8 -> x4, matrix products: 50.8 us -> 5.79 us  [the longest x1 2.69 us: shards(): lax.dot_general(d_proj, normed, (((0,), (0,)), ((), ())), preferred_eleme...]
    all_gather x1 -> x0, blocking collectives: 39.2 us -> none  [shards(): columns = lax.all_gather(qkv_weight, 'dp', axis=1, tiled=True)]
    unnamed x31 -> x11, local copies, waits for them, and re-layouts: 21.5 us -> 4.14 us
    all_gather x3 -> x0, local copies, waits for them, and re-layouts: 8.88 us -> none  [the longest x1 4.7 us: shards(): lax.all_gather(values_own, 'sp', axis=0, tiled=True)]
  transfers between devices with their start and end apart: 6 -> 0, of which waited for: 6 -> 0; matrix products, arithmetic and copies ran while one was open for 8% -> 0% of each run, Pallas kernels for 0% -> 0%
where the time goes in v1:
time: 145 us
  Pallas kernels  131 us (90%)
  local copies, waits for them, and re-layouts  5.92 us (4%)
  matrix products  5.79 us (4%)
    pallas_call x1, Pallas kernels, gather(): pl.pallas_call(gather_kernel, out_shape=(jax.ShapeDtypeStruct((ROWS, D),...  45.1 us
    pallas_call x1, Pallas kernels, sums(): pl.pallas_call(sums_kernel, out_shape=(jax.ShapeDtypeStruct((TOK, D), BF)...  43.5 us
    pallas_call x1, Pallas kernels, key_sums(): pl.pallas_call(key_sums_kernel, out_shape=(jax.ShapeDtypeStruct((ROWS, 2...  15.1 us
    pallas_call x1, Pallas kernels, keys(): pl.pallas_call(keys_kernel, out_shape=jax.ShapeDtypeStruct((SEQ, 2 * QW),...  14.5 us
    pallas_call x1, Pallas kernels, attend(): pl.pallas_call(attention_kernel, grid=(OWN,), out_shape=(jax.ShapeDtypeSt...  12.6 us
    unnamed x11, local copies, waits for them, and re-layouts  4.14 us

profile of v1, /device:TPU:2, one launch (start us, length us, event | category | flops | bytes accessed | tf_op | source)
XLA Modules:
  0.0 144.7 jit_solution(7327546049639333204)
XLA Ops:
  0.6 0.7 broadcast_in_dim.9.gain_ref
  1.3 0.8 pad.8.w_ref
  2.1 1.1 copy.11
  3.2 0.0 copy-start
  3.2 1.0 copy-done
  4.2 45.1 %gather.1 = (bf16[512,1536]{1,0:T(8,128)(2,1)S(1)}, bf16[576,1536]{1,0:T(8,128)(2,1)S(1)}, bf16[192,512]{1,0:T(8,128)(2,1)S(1)}) custom-call(bf16[128,1536]{1,0:T(8,128)(2,1)S(1)} %bitcast.21, f32[1,1536]{1,0:T(1,128)S(1)} %broadcast_in_dim.9.gain_ref, bf16[144,128]{1,0:T(8,128)(2,1)S(1)} %pad.8.w_ref, bf16[768,128]{1,0:T(8,128)(2,1)S(1)} %bitcast.23), custom_call_target="tpu_custom_call" | custom-call | tf_op jit(solution)/shard_map/gather/pallas_call | solution.py:228
  49.4 0.7 convolution_convert_fusion.2.q_ref
  50.0 0.5 copy-done.2
  50.5 1.0 convolution_convert_fusion.1.kv_ref
  51.5 14.5 %keys.1.kv_ref = bf16[2048,384]{1,0:T(8,128)(2,1)S(1)} custom-call(bf16[512,384]{1,0:T(8,128)(2,1)S(1)} %convolution_convert_fusion.1.kv_ref), custom_call_target="tpu_custom_call" | custom-call | tf_op jit(solution)/shard_map/keys/pallas_call | solution.py:271
  66.1 12.6 %attention.1 = (bf16[192,512]{1,0:T(8,128)(2,1)S(1)}, bf16[192,512]{1,0:T(8,128)(2,1)S(1)}, bf16[2048,384]{1,0:T(8,128)(2,1)S(1)}) custom-call(bf16[2048,384]{1,0:T(8,128)(2,1)S(1)} %keys.1.kv_ref, bf16[192,512]{1,0:T(8,128)(2,1)S(1)} %convolution_convert_fusion.2.q_ref, bf16[192,512]{1,0:T(8,128)(2,1)S(1)} %get-tuple-element.17.cot_ref), custom_call_target="tpu_custom_call" | custom-call | tf_op jit(solution)/shard_map/attention/pallas_call | solution.py:333
  78.7 15.1 %key_sums.1 = (bf16[512,384]{1,0:T(8,128)(2,1)S(1)}, bf16[768,128]{1,0:T(8,128)(2,1)S(1)}) custom-call(bf16[2048,384]{1,0:T(8,128)(2,1)S(1)} %get-tuple-element.18.dkv_ref, bf16[192,512]{1,0:T(8,128)(2,1)S(1)} %get-tuple-element.19.ctx_ref), custom_call_target="tpu_custom_call" | custom-call | tf_op jit(solution)/shard_map/key_sums/pallas_call | solution.py:392
  93.8 0.8 copy.14
  94.6 0.1 copy.12
  94.8 2.7 %multiply_reduce_fusion = (f32[1536]{0:T(1024)S(1)}, bf16[576,1536]{1,0:T(8,128)(2,1)S(1)}) fusion(bf16[576,1536]{1,0:T(8,128)(2,1)S(1)} %get-tuple-element.16, bf16[512,1536]{1,0:T(8,128)(2,1)} %copy-done.2, bf16[512,384]{1,0:T(8,128)(2,1)S(1)} %get-tuple-element.22, bf16[512,192]{1,0:T(8,128)(2,1)S(1)} %bitcast.27), kind=kOutput, calls=%fused_computation | convolution fusion | flops 910686720 | bytes 5707776 | tf_op jit(solution)/shard_map/dot_general | solution.py:598
  97.5 0.0 copy-start.1
  97.5 1.4 convolution_convert_fusion.dn_ref
  99.0 0.0 copy-start.3
  99.0 43.5 %sums.1 = (bf16[128,1536]{1,0:T(8,128)(2,1)S(1)}, f32[144,128]{1,0:T(8,128)S(1)}, f32[16,128]{1,0:T(8,128)S(1)}) custom-call(bf16[512,1536]{1,0:T(8,128)(2,1)S(1)} %convolution_convert_fusion.dn_ref, bf16[576,1536]{1,0:T(8,128)(2,1)S(1)} %get-tuple-element.35.wg_ref, f32[16,128]{1,0:T(8,128)S(1)} %pad.9.gg_ref, bf16[128,1536]{1,0:T(8,128)(2,1)S(1)} %bitcast.22, ...), custom_call_target="tpu_custom_call" | custom-call | tf_op jit(solution)/shard_map/sums/pallas_call | solution.py:551
  142.5 0.1 reshape.18
  142.6 0.1 reshape.19
  142.7 0.6 divide_multiply_fusion
  143.3 0.6 multiply_bitcast_fusion
  143.9 0.7 copy.18
  (5 shorter events, 0.0 us)
Async XLA Ops:
  3.2 1.0 copy-start
  49.4 1.2 copy-start.2
  97.5 1.5 %copy-start.1 = (bf16[1,128,1536]{2,1,0:T(8,128)(2,1)S(1)}, bf16[1,128,1536]{2,1,0:T(8,128)(2,1)}, u32[]{:S(2)}) copy-start(bf16[1,128,1536]{2,1,0:T(8,128)(2,1)} %param.4) | copy-start | bytes 1179652
  99.0 43.7 %copy-start.3 = (bf16[1536]{0:T(1024)(128)(2,1)S(1)}, bf16[1536]{0:T(1024)(128)(2,1)}, u32[]{:S(2)}) copy-start(bf16[1536]{0:T(1024)(128)(2,1)} %param.5) | copy-start | bytes 9220

commit v2 on v1

--- a/solution.py
+++ b/solution.py
@@ -247,114 +247,13 @@
     )(x, gain, w, cot)
 
 
-def keys_kernel(kv_ref, kvall, ss, rs):
-    me = Place()
-    ready = greet([me.far(), me.other_core()])
-    own = rows_at(me.group * ROWS, ROWS)
-    far = rows_at(me.far_group * ROWS, ROWS)
-    ready()
-    c_far = remote(kv_ref, kvall.at[own, :], ss.at[0], rs.at[0], me.far())
-    c_core = remote(kv_ref, kvall.at[own, :], ss.at[1], rs.at[1], me.other_core())
-    c_far.start()
-    c_core.start()
-    kvall[own, :] = kv_ref[...]
-    c_far.wait_recv()
-    c_pass = remote(kvall.at[far, :], kvall.at[far, :], ss.at[2], rs.at[2], me.other_core())
-    c_pass.start()
-    c_core.wait_recv()
-    c_pass.wait_recv()
-    for c in (c_far, c_core, c_pass):
-        c.wait_send()
-
-
-def keys(kv):
-    return pl.pallas_call(
-        keys_kernel,
-        out_shape=jax.ShapeDtypeStruct((SEQ, 2 * QW), BF),
-        in_specs=[VMEM],
-        out_specs=VMEM,
-        scratch_shapes=[dma(3), dma(3)],
-        compiler_params=pltpu.CompilerParams(
-            collective_id=1, has_side_effects=True, vmem_limit_bytes=48 * 2**20
-        ),
-        name="keys",
-    )(kv)
-
-
 CHUNK = 256
-
-
-def attention_kernel(kv_ref, q_ref, cot_ref, ctx_ref, dq_ref, dkv_ref, s_buf, e_buf):
-    chunks = SEQ // CHUNK
-    q = q_ref[...] * jnp.asarray(HEAD**-0.5, BF)
-    zeros = jnp.zeros((HEAD, ROWS), BF)
-    q_pad = jnp.concatenate([q, zeros], axis=0)
-    top = jnp.full((8, ROWS), -jnp.inf, F32)
-    for i in range(chunks):
-        rows = slice(i * CHUNK, (i + 1) * CHUNK)
-        s = jnp.dot(kv_ref[rows, :], q_pad, preferred_element_type=F32)
-        s_buf[rows, :] = s
-        top = jnp.maximum(top, jnp.max(s.reshape(CHUNK // 8, 8, ROWS), axis=0))
-    top = jnp.max(top, axis=0, keepdims=True)
-    total = jnp.zeros((8, ROWS), F32)
-    ctx = jnp.zeros((HEAD, ROWS), F32)
-    for i in range(chunks):
-        rows = slice(i * CHUNK, (i + 1) * CHUNK)
-        e = jnp.exp(s_buf[rows, :] - top)
-        total = total + jnp.sum(e.reshape(CHUNK // 8, 8, ROWS), axis=0)
-        e_low = e.astype(BF)
-        e_buf[rows, :] = e_low
-        v_t = kv_ref[rows, :].T[HEAD:, :]
-        ctx = ctx + jnp.dot(v_t, e_low, preferred_element_type=F32)
-    inverse = 1.0 / jnp.sum(total, axis=0, keepdims=True)
-    ctx = ctx * inverse
-    ctx_ref[...] = ctx.astype(BF)
-    cot = (cot_ref[...].astype(F32) * inverse).astype(BF)
-    row_dot = jnp.sum(cot.astype(F32) * ctx, axis=0, keepdims=True)
-    cot_pad = jnp.concatenate([zeros, cot], axis=0)
-    q_side = jnp.concatenate([q, zeros], axis=0).T
-    cot_side = cot_pad.T
-    dq = jnp.zeros((HEAD, ROWS), F32)
-    for i in range(chunks):
-        rows = slice(i * CHUNK, (i + 1) * CHUNK)
-        d_attn = jnp.dot(kv_ref[rows, :], cot_pad, preferred_element_type=F32)
-        e_low = e_buf[rows, :]
-        slopes = (e_low.astype(F32) * (d_attn - row_dot)).astype(BF)
-        k_t = kv_ref[rows, :].T[:HEAD, :]
-        dq = dq + jnp.dot(k_t, slopes, preferred_element_type=F32)
-        dkv_ref[rows, :] = (
-            jnp.dot(slopes, q_side, preferred_element_type=F32)
-            + jnp.dot(e_low, cot_side, preferred_element_type=F32)
-        ).astype(BF)
-    dq_ref[...] = (dq * HEAD**-0.5).astype(BF)
-
-
-def attend(kv, q, cot):
-    return pl.pallas_call(
-        attention_kernel,
-        grid=(OWN,),
-        out_shape=(
-            jax.ShapeDtypeStruct((QW, ROWS), BF),
-            jax.ShapeDtypeStruct((QW, ROWS), BF),
-            jax.ShapeDtypeStruct((SEQ, 2 * QW), BF),
-        ),
-        in_specs=[
-            pl.BlockSpec((SEQ, 128), lambda h: (0, h)),
-            pl.BlockSpec((HEAD, ROWS), lambda h: (h, 0)),
-            pl.BlockSpec((HEAD, ROWS), lambda h: (h, 0)),
-        ],
-        out_specs=(
-            pl.BlockSpec((HEAD, ROWS), lambda h: (h, 0)),
-            pl.BlockSpec((HEAD, ROWS), lambda h: (h, 0)),
-            pl.BlockSpec((SEQ, 128), lambda h: (0, h)),
-        ),
-        scratch_shapes=[pltpu.VMEM((SEQ, ROWS), F32), pltpu.VMEM((SEQ, ROWS), BF)],
-        compiler_params=pltpu.CompilerParams(vmem_limit_bytes=48 * 2**20),
-        name="attention",
-    )(kv, q, cot)
-
-
-def key_sums_kernel(dkv_ref, ctx_ref, out_ref, ctx_out, r1, mid, r2, ss, rs, cs, cr):
+STEPS = SEQ // CHUNK
+
+
+def attention_kernel(q_ref, kv_ref, cot_ref, dq_ref, out_ref, ctx_out,
+                     kvall, dkv, ctx_own, s_buf, e_buf, r1, mid, r2,
+                     ks, kr, ss, rs, cs, cr):
     me = Place()
     y = me.y
     ready = greet([me.far(), me.other_core()] + [me.along_y(r) for r in range(1, NY)])
@@ -362,52 +261,136 @@
     far = rows_at(me.far_group * ROWS, ROWS)
     own_there = rows_at((me.x_hi * 2 + 1 - me.core) * ROWS, ROWS)
     far_there = rows_at(((1 - me.x_hi) * 2 + 1 - me.core) * ROWS, ROWS)
+    mine = y * QW
     ready()
-    c_far = remote(dkv_ref.at[far_there, :], r1.at[0], ss.at[0], rs.at[0], me.other_core())
-    c_own = remote(dkv_ref.at[own_there, :], r1.at[1], ss.at[1], rs.at[1], me.other_core())
-    c_far.start()
-    c_own.start()
-    ctx_copies = []
-    mine = rows_at(y * QW, QW)
-    for r in range(1, NY):
-        to = (y + r) % NY
-        c = remote(ctx_ref.at[:, lanes_at(to * TOK, TOK)], ctx_out.at[mine, :], cs.at[r], cr.at[r], me.along_y(r))
+    sent = []
+
+    def go(*args):
+        c = remote(*args)
         c.start()
-        ctx_copies.append(c)
-    ctx_out[mine, :] = ctx_ref[:, lanes_at(y * TOK, TOK)]
-    c_far.wait_recv()
-    mid[...] = (dkv_ref[far, :].astype(F32) + r1[0].astype(F32)).astype(BF)
-    c_x = remote(mid, r2, ss.at[2], rs.at[2], me.far())
-    c_x.start()
-    c_own.wait_recv()
-    c_x.wait_recv()
-    out_ref[...] = (dkv_ref[own, :].astype(F32) + r1[1].astype(F32) + r2[...].astype(F32)).astype(BF)
+        sent.append(c)
+        return c
+
+    def head_lanes(h):
+        return slice(h * 128, (h + 1) * 128)
+
+    k_far = [go(kv_ref.at[:, head_lanes(h)], kvall.at[own, head_lanes(h)], ks.at[0, h], kr.at[0, h], me.far()) for h in range(OWN)]
+    k_core = [go(kv_ref.at[:, head_lanes(h)], kvall.at[own, head_lanes(h)], ks.at[1, h], kr.at[1, h], me.other_core()) for h in range(OWN)]
+    k_pass = []
+    kvall[own, :] = kv_ref[...]
+    d_far, d_own, d_x, ctx_copies = [], [], [], []
+
+    def pass_keys(h):
+        k_far[h].wait_recv()
+        k_pass.append(go(kvall.at[far, head_lanes(h)], kvall.at[far, head_lanes(h)], ks.at[2, h], kr.at[2, h], me.other_core()))
+
+    def pass_sums(h):
+        lanes = head_lanes(h)
+        d_far[h].wait_recv()
+        mid[:, lanes] = (dkv[far, lanes].astype(F32) + r1[0, :, lanes].astype(F32)).astype(BF)
+        d_x.append(go(mid.at[:, lanes], r2.at[:, lanes], ss.at[2, h], rs.at[2, h], me.far()))
+
+    def finish(h):
+        lanes = head_lanes(h)
+        d_own[h].wait_recv()
+        d_x[h].wait_recv()
+        out_ref[:, lanes] = (
+            dkv[own, lanes].astype(F32) + r1[1, :, lanes].astype(F32) + r2[:, lanes].astype(F32)
+        ).astype(BF)
+
+    pass_keys(0)
+    zeros = jnp.zeros((HEAD, ROWS), BF)
+    for h in range(OWN):
+        lanes = head_lanes(h)
+        head_rows = slice(h * HEAD, (h + 1) * HEAD)
+        q = q_ref[head_rows, :] * jnp.asarray(HEAD**-0.5, BF)
+        q_pad = jnp.concatenate([q, zeros], axis=0)
+        k_core[h].wait_recv()
+        k_pass[h].wait_recv()
+        top = jnp.full((8, ROWS), -jnp.inf, F32)
+        for i in range(STEPS):
+            rows = slice(i * CHUNK, (i + 1) * CHUNK)
+            s = jnp.dot(kvall[rows, lanes], q_pad, preferred_element_type=F32)
+            s_buf[rows, :] = s
+            top = jnp.maximum(top, jnp.max(s.reshape(CHUNK // 8, 8, ROWS), axis=0))
+        top = jnp.max(top, axis=0, keepdims=True)
+        total = jnp.zeros((8, ROWS), F32)
+        ctx = jnp.zeros((HEAD, ROWS), F32)
+        for i in range(STEPS):
+            rows = slice(i * CHUNK, (i + 1) * CHUNK)
+            e = jnp.exp(s_buf[rows, :] - top)
+            total = total + jnp.sum(e.reshape(CHUNK // 8, 8, ROWS), axis=0)
+            e_low = e.astype(BF)
+            e_buf[rows, :] = e_low
+            v_t = kvall[rows, lanes].T[HEAD:, :]
+            ctx = ctx + jnp.dot(v_t, e_low, preferred_element_type=F32)
+        inverse = 1.0 / jnp.sum(total, axis=0, keepdims=True)
+        ctx = ctx * inverse
+        ctx_own[head_rows, :] = ctx.astype(BF)
+        rows_there = rows_at(mine + h * HEAD, HEAD)
+        for r in range(1, NY):
+            to = lanes_at(((y + r) % NY) * TOK, TOK)
+            ctx_copies.append(go(ctx_own.at[head_rows, to], ctx_out.at[rows_there, :], cs.at[h, r], cr.at[h, r], me.along_y(r)))
+        ctx_out[rows_there, :] = ctx_own[head_rows, lanes_at(y * TOK, TOK)]
+        if h + 1 < OWN:
+            pass_keys(h + 1)
+        if h > 0:
+            pass_sums(h - 1)
+        cot = (cot_ref[head_rows, :].astype(F32) * inverse).astype(BF)
+        row_dot = jnp.sum(cot.astype(F32) * ctx, axis=0, keepdims=True)
+        cot_pad = jnp.concatenate([zeros, cot], axis=0)
+        q_side = q_pad.T
+        cot_side = cot_pad.T
+        dq = jnp.zeros((HEAD, ROWS), F32)
+        for i in range(STEPS):
+            rows = slice(i * CHUNK, (i + 1) * CHUNK)
+            d_attn = jnp.dot(kvall[rows, lanes], cot_pad, preferred_element_type=F32)
+            e_low = e_buf[rows, :]
+            slopes = (e_low.astype(F32) * (d_attn - row_dot)).astype(BF)
+            k_t = kvall[rows, lanes].T[:HEAD, :]
+            dq = dq + jnp.dot(k_t, slopes, preferred_element_type=F32)
+            dkv[rows, lanes] = (
+                jnp.dot(slopes, q_side, preferred_element_type=F32)
+                + jnp.dot(e_low, cot_side, preferred_element_type=F32)
+            ).astype(BF)
+        dq_ref[head_rows, :] = (dq * HEAD**-0.5).astype(BF)
+        d_far.append(go(dkv.at[far_there, lanes], r1.at[0, :, lanes], ss.at[0, h], rs.at[0, h], me.other_core()))
+        d_own.append(go(dkv.at[own_there, lanes], r1.at[1, :, lanes], ss.at[1, h], rs.at[1, h], me.other_core()))
+    pass_sums(OWN - 1)
+    for h in range(OWN):
+        finish(h)
     for c in ctx_copies:
         c.wait_recv()
-    for c in [c_far, c_own, c_x] + ctx_copies:
+    for c in sent:
         c.wait_send()
 
 
-def key_sums(dkv, ctx):
+def attend(q, kv, cot):
     return pl.pallas_call(
-        key_sums_kernel,
+        attention_kernel,
         out_shape=(
+            jax.ShapeDtypeStruct((QW, ROWS), BF),
             jax.ShapeDtypeStruct((ROWS, 2 * QW), BF),
             jax.ShapeDtypeStruct((NY * QW, TOK), BF),
         ),
-        in_specs=[VMEM] * 2,
-        out_specs=(VMEM,) * 2,
+        in_specs=[VMEM] * 3,
+        out_specs=(VMEM,) * 3,
         scratch_shapes=[
+            pltpu.VMEM((SEQ, 2 * QW), BF),
+            pltpu.VMEM((SEQ, 2 * QW), BF),
+            pltpu.VMEM((QW, ROWS), BF),
+            pltpu.VMEM((SEQ, ROWS), F32),
+            pltpu.VMEM((SEQ, ROWS), BF),
             pltpu.VMEM((2, ROWS, 2 * QW), BF),
             pltpu.VMEM((ROWS, 2 * QW), BF),
             pltpu.VMEM((ROWS, 2 * QW), BF),
-            dma(3), dma(3), dma(4), dma(4),
+            dma(3, 3), dma(3, 3), dma(3, 3), dma(3, 3), dma(3, 4), dma(3, 4),
         ],
         compiler_params=pltpu.CompilerParams(
-            collective_id=2, has_side_effects=True, vmem_limit_bytes=48 * 2**20
+            collective_id=1, has_side_effects=True, vmem_limit_bytes=48 * 2**20
         ),
-        name="key_sums",
-    )(dkv, ctx)
+        name="attention",
+    )(q, kv, cot)
 
 
 def sums_kernel(dn_ref, wg_ref, gg_ref, x_ref, gain_ref, dx_ref, wout_ref, gout_ref,
@@ -577,7 +560,7 @@
             dma(4), dma(4), dma(4), dma(4), dma(4, 3), dma(4, 3), dma(8), dma(8), dma(14), dma(14),
         ],
         compiler_params=pltpu.CompilerParams(
-            collective_id=3, has_side_effects=True, vmem_limit_bytes=48 * 2**20
+            collective_id=2, has_side_effects=True, vmem_limit_bytes=48 * 2**20
         ),
         name="sums",
     )(dn, wg, gg, x, gain)
@@ -590,9 +573,7 @@
     normed, weights, cot = gather(x, gain, w_own, d_context[0].T)
     q = lax.dot_general(weights[:QW], normed, (((1,), (1,)), ((), ())), preferred_element_type=F32).astype(BF)
     kv = lax.dot_general(normed, weights[QW:], (((1,), (1,)), ((), ())), preferred_element_type=F32).astype(BF)
-    kv_all = keys(kv)
-    context, d_query, d_kv = attend(kv_all, q, cot)
-    kv_sums, context = key_sums(d_kv, context)
+    d_query, kv_sums, context = attend(q, kv, cot)
     d_proj = jnp.concatenate([d_query.T, kv_sums], axis=1)
     d_normed = jnp.dot(d_proj, weights, preferred_element_type=F32).astype(BF)
     grad = lax.dot_general(d_proj, normed, (((0,), (0,)), ((), ())), preferred_element_type=F32)

time: 145 us -> 132 us (0.910)
  Pallas kernels: 131 us -> 118 us
    pallas_call x3 -> x1, Pallas kernels: 42.3 us -> 29.6 us  [attend(): pl.pallas_call(attention_kernel, out_shape=(jax.ShapeDtypeStruct((QW, ROW...]
where the time goes in v2:
time: 132 us; the launch traced here: 131 us
  Pallas kernels  118 us (89%)
  matrix products  5.78 us (4%)
  local copies, waits for them, and re-layouts  5.46 us (4%)
    pallas_call x1, Pallas kernels, gather(): pl.pallas_call(gather_kernel, out_shape=(jax.ShapeDtypeStruct((ROWS, D),...  45.1 us
    pallas_call x1, Pallas kernels, sums(): pl.pallas_call(sums_kernel, out_shape=(jax.ShapeDtypeStruct((TOK, D), BF)...  43.1 us
    pallas_call x1, Pallas kernels, attend(): pl.pallas_call(attention_kernel, out_shape=(jax.ShapeDtypeStruct((QW, ROW...  29.6 us
    unnamed x11, local copies, waits for them, and re-layouts  3.68 us
    dot_general x1, matrix products, shards(): lax.dot_general(d_proj, normed, (((0,), (0,)), ((), ())), preferred_eleme...  2.68 us

profile of v2, /device:TPU:2, one launch (start us, length us, event | category | flops | bytes accessed | tf_op | source)
XLA Modules:
  0.0 131.2 jit_solution(10836379731246681531)
XLA Ops:
  0.6 0.7 broadcast_in_dim.9.gain_ref
  1.3 0.8 pad.8.w_ref
  2.1 1.1 copy.11
  3.2 0.0 copy-start
  3.2 1.0 copy-done
  4.2 45.1 %gather.1 = (bf16[512,1536]{1,0:T(8,128)(2,1)S(1)}, bf16[576,1536]{1,0:T(8,128)(2,1)S(1)}, bf16[192,512]{1,0:T(8,128)(2,1)S(1)}) custom-call(bf16[128,1536]{1,0:T(8,128)(2,1)S(1)} %bitcast.21, f32[1,1536]{1,0:T(1,128)S(1)} %broadcast_in_dim.9.gain_ref, bf16[144,128]{1,0:T(8,128)(2,1)S(1)} %pad.8.w_ref, bf16[768,128]{1,0:T(8,128)(2,1)S(1)} %bitcast.23), custom_call_target="tpu_custom_call" | custom-call | tf_op jit(solution)/shard_map/gather/pallas_call | solution.py:228
  49.4 0.0 copy-start.2
  49.4 0.7 convolution_convert_fusion.2.q_ref
  50.0 1.0 convolution_convert_fusion.1.kv_ref
  51.0 0.0 copy-done.2
  51.1 29.6 %attention.1 = (bf16[192,512]{1,0:T(8,128)(2,1)S(1)}, bf16[512,384]{1,0:T(8,128)(2,1)S(1)}, bf16[768,128]{1,0:T(8,128)(2,1)S(1)}) custom-call(bf16[192,512]{1,0:T(8,128)(2,1)S(1)} %convolution_convert_fusion.2.q_ref, bf16[512,384]{1,0:T(8,128)(2,1)S(1)} %convolution_convert_fusion.1.kv_ref, bf16[192,512]{1,0:T(8,128)(2,1)S(1)} %get-tuple-element.15.cot_ref), custom_call_target="tpu_custom_call" | custom-call | tf_op jit(solution)/shard_map/attention/pallas_call | solution.py:369
  80.7 0.8 copy.14
  81.5 0.1 copy.12
  81.7 2.7 %multiply_reduce_fusion = (f32[1536]{0:T(1024)S(1)}, bf16[576,1536]{1,0:T(8,128)(2,1)S(1)}) fusion(bf16[576,1536]{1,0:T(8,128)(2,1)S(1)} %get-tuple-element.13, bf16[512,1536]{1,0:T(8,128)(2,1)} %copy-done.2, bf16[512,384]{1,0:T(8,128)(2,1)S(1)} %get-tuple-element.18, bf16[512,192]{1,0:T(8,128)(2,1)S(1)} %bitcast.27), kind=kOutput, calls=%fused_computation | convolution fusion | flops 910686720 | bytes 5707776 | tf_op jit(solution)/shard_map/dot_general | solution.py:579
  84.4 0.0 copy-start.1
  84.4 1.4 %convolution_convert_fusion.dn_ref = bf16[512,1536]{1,0:T(8,128)(2,1)S(1)} fusion(bf16[576,1536]{1,0:T(8,128)(2,1)S(1)} %get-tuple-element.13, bf16[512,384]{1,0:T(8,128)(2,1)S(1)} %get-tuple-element.18, bf16[512,192]{1,0:T(8,128)(2,1)S(1)} %bitcast.28), kind=kOutput, calls=%fused_computation.1 | convolution fusion | flops 907935744 | bytes 3932160 | tf_op jit(solution)/shard_map/dot_general | solution.py:578
  85.8 0.0 copy-start.3
  85.9 43.1 %sums.1 = (bf16[128,1536]{1,0:T(8,128)(2,1)S(1)}, f32[144,128]{1,0:T(8,128)S(1)}, f32[16,128]{1,0:T(8,128)S(1)}) custom-call(bf16[512,1536]{1,0:T(8,128)(2,1)S(1)} %convolution_convert_fusion.dn_ref, bf16[576,1536]{1,0:T(8,128)(2,1)S(1)} %get-tuple-element.31.wg_ref, f32[16,128]{1,0:T(8,128)S(1)} %pad.9.gg_ref, bf16[128,1536]{1,0:T(8,128)(2,1)S(1)} %bitcast.22, ...), custom_call_target="tpu_custom_call" | custom-call | tf_op jit(solution)/shard_map/sums/pallas_call | solution.py:534
  129.0 0.1 reshape.18
  129.1 0.1 reshape.19
  129.2 0.0 copy-done.3
  129.2 0.6 divide_multiply_fusion
  129.8 0.6 multiply_bitcast_fusion
  130.4 0.7 copy.18
  (3 shorter events, 0.0 us)
Async XLA Ops:
  3.2 1.0 copy-start
  49.4 1.7 %copy-start.2 = (bf16[512,1536]{1,0:T(8,128)(2,1)}, bf16[512,1536]{1,0:T(8,128)(2,1)S(1)}, u32[]{:S(2)}) copy-start(bf16[512,1536]{1,0:T(8,128)(2,1)S(1)} %get-tuple-element.14) | copy-start | bytes 4718596
  84.4 1.5 %copy-start.1 = (bf16[1,128,1536]{2,1,0:T(8,128)(2,1)S(1)}, bf16[1,128,1536]{2,1,0:T(8,128)(2,1)}, u32[]{:S(2)}) copy-start(bf16[1,128,1536]{2,1,0:T(8,128)(2,1)} %param.4) | copy-start | bytes 1179652
  85.8 43.3 %copy-start.3 = (bf16[1536]{0:T(1024)(128)(2,1)S(1)}, bf16[1536]{0:T(1024)(128)(2,1)}, u32[]{:S(2)}) copy-start(bf16[1536]{0:T(1024)(128)(2,1)} %param.5) | copy-start | bytes 9220

commit v3 on v2

--- a/solution.py
+++ b/solution.py
@@ -110,6 +110,38 @@
     return jnp.concatenate(parts, axis=1)
 
 
+UNIT = 48
+UNITS = 12
+SHARD = 3
+
+
+def unit_home(u, y):
+    column = (u // 4) * 16 + 4 * y + u % 4
+    d = column // SHARD
+    return column - SHARD * d, d // NZ, d % NZ
+
+
+def shard_unit(me, j):
+    column = (me.x_lo * NZ + me.z) * SHARD + j
+    return (column % 16) // 4, (column // 16) * 4 + column % 4
+
+
+def each_unit(me, here, there):
+    def step(u, carry):
+        slot, x_lo, z = unit_home(u, me.y)
+        if here is not None:
+            pl.when(x_lo == me.x_lo)(lambda: here(u, slot, z))
+        if there is not None:
+            pl.when(x_lo != me.x_lo)(lambda: there(u))
+        return carry
+
+    lax.fori_loop(0, UNITS, step, 0)
+
+
+def unit_rows(u):
+    return rows_at(u * UNIT, UNIT)
+
+
 def wire_row(piece):
     if piece < OWN:
         return piece * HEAD
@@ -117,27 +149,23 @@
     return QW * (1 + which) + head * HEAD
 
 
-def gather_kernel(x_ref, gain_ref, w_ref, cot_ref, nall, wall, cots,
-                  wd, wy, ns, nr, cs, cr, zs, zr, bs, br, ys, yr, gs, gr):
+def gather_kernel(x_ref, gain_ref, w_ref, cot_ref, nall, w_out, cots,
+                  wall, ybuf, ns, nr, cs, cr, ys, yr, zs, zr, xs, xr, ds, dr):
     me = Place()
     y = me.y
+    right, left = me.along_x(1), me.along_x(3)
+    x_at = me.x_hi * 2 + me.x_lo
+    own = lanes_at(me.group * GW, GW)
+    far = lanes_at(me.far_group * GW, GW)
+    hi_left, hi_right = ((x_at + 3) % 4) // 2, ((x_at + 1) % 4) // 2
+    of_left = lanes_at((hi_left * 2 + me.core) * GW, GW)
+    of_right = lanes_at((hi_right * 2 + me.core) * GW, GW)
     partners = (
         [me.along_z(r) for r in range(1, NZ)]
         + [me.along_y(r) for r in range(1, NY)]
-        + [me.beside(), me.mirror(), me.other_core()]
+        + [left, right, me.other_core()]
     )
     ready = greet(partners)
-    own_rows = rows_at((me.x_lo * NZ + me.z) * BLOCK, BLOCK)
-    wd[own_rows, :] = w_ref[...]
-    ready()
-    z_copies, b_copies = [], []
-    for r in range(1, NZ):
-        c = remote(wd.at[own_rows, :], wd.at[own_rows, :], zs.at[r], zr.at[r], me.along_z(r))
-        c.start()
-        z_copies.append(c)
-    c = remote(wd.at[own_rows, :], wd.at[own_rows, :], bs.at[0], br.at[0], me.beside())
-    c.start()
-    b_copies.append(c)
 
     x = x_ref[...].astype(F32)
     centred = x - jnp.mean(x, axis=1, keepdims=True)
@@ -145,11 +173,53 @@
     normed = centred * lax.rsqrt(spread + EPS) * gain_ref[...]
     tok_rows = rows_at(y * TOK, TOK)
     nall[tok_rows, :] = to_grouped(normed).astype(BF)
-    right, left = me.along_y(1), me.along_y(3)
-    n_right = remote(nall.at[tok_rows, :], nall.at[tok_rows, :], ns.at[0], nr.at[0], right)
-    n_left = remote(nall.at[tok_rows, :], nall.at[tok_rows, :], ns.at[1], nr.at[1], left)
-    n_right.start()
-    n_left.start()
+    ready()
+
+    def y_copy(j, to):
+        return remote(w_ref.at[pl.ds(j * UNIT, UNIT), :], ybuf.at[y, j], ys.at[j], yr.at[j, y], me.id(y=to))
+
+    for j in range(SHARD):
+        to, _ = shard_unit(me, j)
+        pl.when(to != y)(lambda: y_copy(j, to).start())
+
+    up, down = me.along_y(1), me.along_y(3)
+    n_up = remote(nall.at[tok_rows, :], nall.at[tok_rows, :], ns.at[0], nr.at[0], up)
+    n_down = remote(nall.at[tok_rows, :], nall.at[tok_rows, :], ns.at[1], nr.at[1], down)
+    n_up.start()
+    n_down.start()
+
+    for j in range(SHARD):
+        to, u = shard_unit(me, j)
+
+        @pl.when(to == y)
+        def _():
+            ybuf[y, j] = w_ref[j * UNIT : (j + 1) * UNIT, :]
+            for r in range(1, NY):
+                k = (y + r) % NY
+                remote(ybuf.at[k, j], ybuf.at[k, j], ys.at[j], yr.at[j, k], me.along_y(r)).wait_recv()
+            parts = [ybuf[k, j][:, :SLAB].astype(F32) for k in range(NY)]
+            wall[unit_rows(u), own] = jnp.concatenate(parts, axis=1).astype(BF)
+
+    def piece(u, lanes):
+        return wall.at[unit_rows(u), lanes]
+
+    def z_copy(u, r):
+        return remote(piece(u, own), piece(u, own), zs.at[u, r], zr.at[u], me.along_z(r))
+
+    def x_copy(u, lanes, kind, to):
+        return remote(piece(u, lanes), piece(u, lanes), xs.at[kind, u], xr.at[kind, u], to)
+
+    def d_copy(u, x_hi, lanes):
+        return remote(piece(u, lanes), piece(u, lanes), ds.at[x_hi, u], dr.at[x_hi, u], me.other_core())
+
+    def push(u, slot, z):
+        @pl.when(z == me.z)
+        def _():
+            for r in (1, 7, 2, 6, 3, 5, 4):
+                z_copy(u, r).start()
+
+    each_unit(me, push, None)
+
     cot_copies = []
     cot_lanes = lanes_at(y * TOK, TOK)
     for r in range(1, NY):
@@ -159,64 +229,79 @@
         cot_copies.append(c)
     cots[:, cot_lanes] = cot_ref[rows_at(y * QW, QW), :]
 
-    for r in (1, 7, 2, 6, 3, 5, 4):
-        z_copies[r - 1].wait_recv()
-        rows = rows_at((me.x_lo * NZ + (me.z + NZ - r) % NZ) * BLOCK, BLOCK)
-        c = remote(wd.at[rows, :], wd.at[rows, :], bs.at[r], br.at[r], me.beside())
-        c.start()
-        b_copies.append(c)
+    def spread_x(u, slot, z):
+        pl.when(z != me.z)(lambda: z_copy(u, 1).wait_recv())
+        x_copy(u, own, 0, right).start()
+        x_copy(u, own, 1, left).start()
+        d_copy(u, me.x_hi, own).start()
+
+    each_unit(me, spread_x, None)
+
     half = TOK // 2
-    from_left = rows_at(((y + 3) % NY) * TOK, half)
-    from_right = rows_at(((y + 1) % NY) * TOK + half, half)
-    n_right.wait_recv()
-    f_right = remote(nall.at[from_left, :], nall.at[from_left, :], ns.at[2], nr.at[2], right)
-    f_right.start()
-    n_left.wait_recv()
-    f_left = remote(nall.at[from_right, :], nall.at[from_right, :], ns.at[3], nr.at[3], left)
-    f_left.start()
-
-    for c in b_copies:
-        c.wait_recv()
-    y_copies = []
-    for r in range(1, NY):
-        to = (y + r) % NY
-        for k in range(3):
-            c = remote(
-                wd.at[rows_at(k * NY * QW + to * QW, QW), :],
-                wy.at[y, pl.ds(k * QW, QW), :],
-                ys.at[r, k],
-                yr.at[r, k],
-                me.along_y(r),
-            )
-            c.start()
-            y_copies.append(c)
-    for k in range(3):
-        wy[y, k * QW : (k + 1) * QW, :] = wd[rows_at(k * NY * QW + y * QW, QW), :]
-    for c in y_copies:
-        c.wait_recv()
-    own = lanes_at(me.group * GW, GW)
-    for piece in range(3 * OWN):
-        row = wire_row(piece)
-        parts = [wy[k, row : row + HEAD, :][:, :SLAB].astype(F32) for k in range(NY)]
-        wall[piece * HEAD : (piece + 1) * HEAD, own] = jnp.concatenate(parts, axis=1).astype(BF)
-    far = lanes_at(me.far_group * GW, GW)
-    g_far = remote(wall.at[:, own], wall.at[:, own], gs.at[0], gr.at[0], me.mirror())
-    g_core = remote(wall.at[:, own], wall.at[:, own], gs.at[1], gr.at[1], me.other_core())
-    g_far.start()
-    g_core.start()
-    g_far.wait_recv()
-    g_pass = remote(wall.at[:, far], wall.at[:, far], gs.at[2], gr.at[2], me.other_core())
-    g_pass.start()
-    g_core.wait_recv()
-    g_pass.wait_recv()
-    f_right.wait_recv()
-    f_left.wait_recv()
+    from_down = rows_at(((y + 3) % NY) * TOK, half)
+    from_up = rows_at(((y + 1) % NY) * TOK + half, half)
+    n_up.wait_recv()
+    f_up = remote(nall.at[from_down, :], nall.at[from_down, :], ns.at[2], nr.at[2], up)
+    f_up.start()
+    n_down.wait_recv()
+    f_down = remote(nall.at[from_up, :], nall.at[from_up, :], ns.at[3], nr.at[3], down)
+    f_down.start()
+
+    def relay(u):
+        x_copy(u, of_left, 0, right).wait_recv()
+        pl.when(u % 2 == 0)(lambda: x_copy(u, of_left, 2, right).start())
+        d_copy(u, hi_left, of_left).start()
+        x_copy(u, of_right, 1, left).wait_recv()
+        pl.when(u % 2 == 1)(lambda: x_copy(u, of_right, 2, left).start())
+        d_copy(u, hi_right, of_right).start()
+
+    each_unit(me, None, relay)
+
+    def last(u, slot, z):
+        x_copy(u, far, 2, right).wait_recv()
+        d_copy(u, 1 - me.x_hi, far).start()
+
+    each_unit(me, last, None)
+
+    def drain(u, carry):
+        for x_hi in range(2):
+            lanes = lanes_at((x_hi * 2 + 1 - me.core) * GW, GW)
+            d_copy(u, x_hi, lanes).wait_recv()
+        return carry
+
+    lax.fori_loop(0, UNITS, drain, 0)
+    for p in range(3 * OWN):
+        row = wire_row(p)
+        w_out[p * HEAD : (p + 1) * HEAD, :] = wall[row : row + HEAD, :]
+    f_up.wait_recv()
+    f_down.wait_recv()
     for c in cot_copies:
         c.wait_recv()
-    for c in (
-        z_copies + b_copies + y_copies + cot_copies
-        + [n_right, n_left, f_right, f_left, g_far, g_core, g_pass]
-    ):
+
+    def sent_here(u, slot, z):
+        @pl.when(z == me.z)
+        def _():
+            for r in range(1, NZ):
+                z_copy(u, r).wait_send()
+
+        x_copy(u, own, 0, right).wait_send()
+        x_copy(u, own, 1, left).wait_send()
+
+    def sent_there(u):
+        x_copy(u, own, 2, right).wait_send()
+
+    each_unit(me, sent_here, sent_there)
+
+    def sent_core(u, carry):
+        for x_hi in range(2):
+            d_copy(u, x_hi, own).wait_send()
+        return carry
+
+    lax.fori_loop(0, UNITS, sent_core, 0)
+    for j in range(SHARD):
+        to, _ = shard_unit(me, j)
+        pl.when(to != y)(lambda: y_copy(j, to).wait_send())
+    for c in cot_copies + [n_up, n_down, f_up, f_down]:
         c.wait_send()
 
 
@@ -235,10 +320,10 @@
         in_specs=[VMEM] * 4,
         out_specs=(VMEM,) * 3,
         scratch_shapes=[
-            pltpu.VMEM((16 * BLOCK, 128), BF),
-            pltpu.VMEM((NY, PW, 128), BF),
-            dma(4), dma(4), dma(4), dma(4), dma(8), dma(8), dma(8), dma(8),
-            dma(4, 3), dma(4, 3), dma(3), dma(3),
+            pltpu.VMEM((PW, D), BF),
+            pltpu.VMEM((NY, SHARD, UNIT, 128), BF),
+            dma(4), dma(4), dma(4), dma(4), dma(3), dma(3, 4), dma(12, 8), dma(12),
+            dma(3, 12), dma(3, 12), dma(2, 12), dma(2, 12),
         ],
         compiler_params=pltpu.CompilerParams(
             collective_id=0, has_side_effects=True, vmem_limit_bytes=48 * 2**20
@@ -394,11 +479,14 @@
 
 
 def sums_kernel(dn_ref, wg_ref, gg_ref, x_ref, gain_ref, dx_ref, wout_ref, gout_ref,
-                half_r, to_right, to_left, full_r, wr1, s1, wr2, wyo, wd, wb, wz, zbuf,
+                half_r, to_up, to_down, full_r, s1, wr1, wr2, mid, zout, zbuf, yout,
                 gcore, gy, gx, gz,
-                ns, nr, ws, wr, ys, yr, zs, zr, gs, gr):
+                ns, nr, ws, wr, xs, xr, zs, zr, ys, yr, gs, gr):
     me = Place()
     y = me.y
+    right, left = me.along_x(1), me.along_x(3)
+    x_at = me.x_hi * 2 + me.x_lo
+    hi_left, hi_right = ((x_at + 3) % 4) // 2, ((x_at + 1) % 4) // 2
     partners = (
         [me.along_z(r) for r in range(1, NZ)]
         + [me.along_y(r) for r in range(1, NY)]
@@ -415,122 +503,177 @@
         sent.append(c)
         return c
 
-    def group(x_hi, core):
-        return lanes_at((x_hi * 2 + core) * GW, GW)
-
-    other = 1 - me.core
-    w_far = go(wg_ref.at[:, group(1 - me.x_hi, other)], wr1.at[0], ws.at[0], wr.at[0], me.other_core())
-    w_own = go(wg_ref.at[:, group(me.x_hi, other)], wr1.at[1], ws.at[1], wr.at[1], me.other_core())
+    part = PW // 4
+    w_core = []
+    for k in range(4):
+        rows = pl.ds(k * part, part)
+        for x_hi in range(2):
+            there = lanes_at((x_hi * 2 + 1 - me.core) * GW, GW)
+            w_core.append(go(wg_ref.at[rows, there], wr1.at[x_hi, rows, :], ws.at[x_hi, k], wr.at[x_hi, k], me.other_core()))
     half = TOK // 2
-    right, left = me.along_y(1), me.along_y(3)
+    up, down = me.along_y(1), me.along_y(3)
     opposite = ((y + 2) % NY) * TOK
-    h_right = go(dn_ref.at[rows_at(opposite, half), :], half_r.at[0], ns.at[0], nr.at[0], right)
-    h_left = go(dn_ref.at[rows_at(opposite + half, half), :], half_r.at[1], ns.at[1], nr.at[1], left)
+    h_up = go(dn_ref.at[rows_at(opposite, half), :], half_r.at[0], ns.at[0], nr.at[0], up)
+    h_down = go(dn_ref.at[rows_at(opposite + half, half), :], half_r.at[1], ns.at[1], nr.at[1], down)
     gcore[me.core] = gg_ref[...]
     g_core = go(gg_ref, gcore.at[me.core], gs.at[0], gr.at[0], me.other_core())
 
-    w_far.wait_recv()
-    s1[...] = (wg_ref[:, group(1 - me.x_hi, me.core)].astype(F32) + wr1[0].astype(F32)).astype(BF)
-    w_x = go(s1, wr2, ws.at[2], wr.at[2], me.mirror())
-
-    h_right.wait_recv()
-    block = rows_at(((y + 1) % NY) * TOK, half)
-    rest = rows_at(((y + 1) % NY) * TOK + half, half)
-    to_right[:half, :] = (dn_ref[block, :].astype(F32) + half_r[0].astype(F32)).astype(BF)
-    to_right[half:, :] = dn_ref[rest, :]
-    f_right = go(to_right, full_r.at[0], ns.at[2], nr.at[2], right)
-    h_left.wait_recv()
-    block = rows_at(((y + 3) % NY) * TOK, half)
-    rest = rows_at(((y + 3) % NY) * TOK + half, half)
-    to_left[:half, :] = dn_ref[block, :]
-    to_left[half:, :] = (dn_ref[rest, :].astype(F32) + half_r[1].astype(F32)).astype(BF)
-    f_left = go(to_left, full_r.at[1], ns.at[3], nr.at[3], left)
+    def x_copy(u, src, dst, kind, to):
+        return remote(src, dst, xs.at[kind, u], xr.at[kind, u], to)
+
+    def to_opposite(u, slot, z):
+        src = s1.at[1 - me.x_hi, unit_rows(u), :]
+        dst = wr2.at[0, unit_rows(u), :]
+        pl.when(u % 2 == 0)(lambda: x_copy(u, src, dst, 0, right).start())
+        pl.when(u % 2 == 1)(lambda: x_copy(u, src, dst, 0, left).start())
+
+    for k in range(4):
+        rows = slice(k * part, (k + 1) * part)
+        for x_hi in range(2):
+            w_core[2 * k + x_hi].wait_recv()
+            here = lanes_at((x_hi * 2 + me.core) * GW, GW)
+            s1[x_hi, rows, :] = (wg_ref[rows, here].astype(F32) + wr1[x_hi, rows, :].astype(F32)).astype(BF)
+
+        def first(u, carry):
+            _, x_lo, _ = unit_home(u, y)
+            pl.when(x_lo == me.x_lo)(lambda: to_opposite(u, 0, 0))
+            return carry
+
+        lax.fori_loop(k * SHARD, (k + 1) * SHARD, first, 0)
 
     g_core.wait_recv()
     gy[y] = gcore[0] + gcore[1]
     g_y = [go(gy.at[y], gy.at[y], gs.at[r], gr.at[r], me.along_y(r)) for r in range(1, NY)]
 
-    w_own.wait_recv()
-    w_x.wait_recv()
-    for piece in range(3 * OWN):
-        rows = slice(piece * HEAD, (piece + 1) * HEAD)
-        dense = wg_ref[rows, group(me.x_hi, me.core)].astype(F32) + wr1[1, rows, :].astype(F32) + wr2[rows, :].astype(F32)
-        row = wire_row(piece)
-        for k in range(NY):
-            part = dense[:, k * SLAB : (k + 1) * SLAB]
-            part = jnp.concatenate([part, jnp.zeros((HEAD, 128 - SLAB), F32)], axis=1)
-            wyo[k, row : row + HEAD, :] = part.astype(BF)
-    w_y = []
-    for r in range(1, NY):
-        to = (y + r) % NY
-        for k in range(3):
-            w_y.append(go(
-                wyo.at[to, pl.ds(k * QW, QW), :],
-                wd.at[rows_at(k * NY * QW + y * QW, QW), :],
-                ys.at[r, k], yr.at[r, k], me.along_y(r),
-            ))
-    for k in range(3):
-        wd[rows_at(k * NY * QW + y * QW, QW), :] = wyo[y, k * QW : (k + 1) * QW, :]
+    def pass_on(u):
+        rows = unit_rows(u)
+        pl.when(u % 2 == 0)(lambda: x_copy(u, s1.at[hi_left, rows, :], wr2.at[2, rows, :], 2, left).start())
+        pl.when(u % 2 == 1)(lambda: x_copy(u, s1.at[hi_right, rows, :], wr2.at[1, rows, :], 1, right).start())
+        x_copy(u, s1.at[0, rows, :], wr2.at[0, rows, :], 0, right).wait_recv()
+
+        @pl.when(u % 2 == 0)
+        def _():
+            mid[rows, :] = (s1[hi_right, rows, :].astype(F32) + wr2[0, rows, :].astype(F32)).astype(BF)
+            x_copy(u, mid.at[rows, :], wr2.at[1, rows, :], 1, right).start()
+
+        @pl.when(u % 2 == 1)
+        def _():
+            mid[rows, :] = (s1[hi_left, rows, :].astype(F32) + wr2[0, rows, :].astype(F32)).astype(BF)
+            x_copy(u, mid.at[rows, :], wr2.at[2, rows, :], 2, left).start()
+
+    each_unit(me, None, pass_on)
+
+    h_up.wait_recv()
+    block = rows_at(((y + 1) % NY) * TOK, half)
+    rest = rows_at(((y + 1) % NY) * TOK + half, half)
+    to_up[:half, :] = (dn_ref[block, :].astype(F32) + half_r[0].astype(F32)).astype(BF)
+    to_up[half:, :] = dn_ref[rest, :]
+    f_up = go(to_up, full_r.at[0], ns.at[2], nr.at[2], up)
+    h_down.wait_recv()
+    block = rows_at(((y + 3) % NY) * TOK, half)
+    rest = rows_at(((y + 3) % NY) * TOK + half, half)
+    to_down[:half, :] = dn_ref[block, :]
+    to_down[half:, :] = (dn_ref[rest, :].astype(F32) + half_r[1].astype(F32)).astype(BF)
+    f_down = go(to_down, full_r.at[1], ns.at[3], nr.at[3], down)
+
+    def z_copy(u, slot, z):
+        distance = (z + NZ - me.z) % NZ
+        return remote(
+            zout.at[unit_rows(u), :], zbuf.at[slot, distance], zs.at[u], zr.at[slot, distance],
+            me.id(z=z),
+        )
+
+    def over_x(u, slot, z):
+        rows = unit_rows(u)
+        x_copy(u, s1.at[0, rows, :], wr2.at[1, rows, :], 1, right).wait_recv()
+        x_copy(u, s1.at[0, rows, :], wr2.at[2, rows, :], 2, left).wait_recv()
+        zout[rows, :] = (
+            s1[me.x_hi, rows, :].astype(F32) + wr2[1, rows, :].astype(F32) + wr2[2, rows, :].astype(F32)
+        ).astype(BF)
+        pl.when(z != me.z)(lambda: z_copy(u, slot, z).start())
+
+    each_unit(me, over_x, None)
 
     for c in g_y:
         c.wait_recv()
-    x_at = me.x_hi * 2 + me.x_lo
     gx[x_at] = gy[0] + gy[1] + gy[2] + gy[3]
     g_x = [go(gx.at[x_at], gx.at[x_at], gs.at[3 + r], gr.at[3 + r], me.along_x(r)) for r in range(1, 4)]
 
-    for c in w_y:
-        c.wait_recv()
-    span = NZ * BLOCK
-    w_b = go(wd.at[rows_at((1 - me.x_lo) * span, span), :], wb, ws.at[3], wr.at[3], me.beside())
-
-    for c in g_x:
-        c.wait_recv()
-    gz[me.z] = gx[0] + gx[1] + gx[2] + gx[3]
-    g_z = [go(gz.at[me.z], gz.at[me.z], gs.at[6 + r], gr.at[6 + r], me.along_z(r)) for r in range(1, NZ)]
-
-    f_right.wait_recv()
-    f_left.wait_recv()
-    d_normed = (
-        dn_ref[rows_at(y * TOK, TOK), :].astype(F32) + full_r[0].astype(F32) + full_r[1].astype(F32)
-    )
-    d_normed = to_natural(d_normed)
     x = x_ref[...].astype(F32)
     centred = x - jnp.mean(x, axis=1, keepdims=True)
     spread = jnp.mean(centred * centred, axis=1, keepdims=True)
     scale = lax.rsqrt(spread + EPS)
     hat = centred * scale
-    inner = d_normed * gain_ref[...]
-    first = jnp.mean(inner, axis=1, keepdims=True)
+    f_up.wait_recv()
+    f_down.wait_recv()
+    d_normed = (
+        dn_ref[rows_at(y * TOK, TOK), :].astype(F32) + full_r[0].astype(F32) + full_r[1].astype(F32)
+    )
+    inner = to_natural(d_normed) * gain_ref[...]
+    first_mean = jnp.mean(inner, axis=1, keepdims=True)
     second = jnp.mean(inner * hat, axis=1, keepdims=True)
-    dx_ref[...] = (scale * (inner - first - hat * second)).astype(BF)
-
-    w_b.wait_recv()
-    for k in range(NZ):
-        at = rows_at(me.x_lo * span + k * BLOCK, BLOCK)
-        wz[k * BLOCK : (k + 1) * BLOCK, :] = (
-            wd[at, :].astype(F32) + wb[k * BLOCK : (k + 1) * BLOCK, :].astype(F32)
-        ).astype(BF)
-    w_z = []
-    for r in range(1, NZ):
-        to = (me.z + r) % NZ
-        w_z.append(go(wz.at[rows_at(to * BLOCK, BLOCK), :], zbuf.at[r], zs.at[r], zr.at[r], me.along_z(r)))
+    dx_ref[...] = (scale * (inner - first_mean - hat * second)).astype(BF)
+
+    for c in g_x:
+        c.wait_recv()
+    gz[me.z] = gx[0] + gx[1] + gx[2] + gx[3]
+    g_z = [go(gz.at[me.z], gz.at[me.z], gs.at[6 + r], gr.at[6 + r], me.along_z(r)) for r in range(1, NZ)]
+
+    def y_copy(j, to):
+        return remote(yout.at[j, to], wout_ref.at[pl.ds(j * UNIT, UNIT), :], ys.at[j, to], yr.at[j], me.id(y=to))
+
+    for j in range(SHARD):
+        holder, u = shard_unit(me, j)
+
+        @pl.when(holder == y)
+        def _():
+            total = zout[unit_rows(u), :].astype(F32)
+            for r in range(1, NZ):
+                remote(zbuf.at[j, r], zbuf.at[j, r], zs.at[u], zr.at[j, r], me.along_z(r)).wait_recv()
+                total = total + zbuf[j, r].astype(F32)
+            for k in range(NY):
+                rows = total[:, k * SLAB : (k + 1) * SLAB]
+                rows = jnp.concatenate([rows, jnp.zeros((UNIT, 128 - SLAB), F32)], axis=1)
+                yout[j, k] = rows
+            for r in range(1, NY):
+                y_copy(j, (y + r) % NY).start()
+            wout_ref[j * UNIT : (j + 1) * UNIT, :] = yout[j, y]
+
     for c in g_z:
         c.wait_recv()
     total = gz[0]
     for k in range(1, NZ):
         total = total + gz[k]
     gout_ref[...] = total
-    total = wz[rows_at(me.z * BLOCK, BLOCK), :].astype(F32)
-    for r in range(1, NZ):
-        w_z[r - 1].wait_recv()
-        total = total + zbuf[r].astype(F32)
-    wout_ref[...] = total
+
+    for j in range(SHARD):
+        holder, u = shard_unit(me, j)
+
+        @pl.when(holder != y)
+        def _():
+            y_copy(j, y).wait_recv()
+
+        @pl.when(holder == y)
+        def _():
+            for r in range(1, NY):
+                y_copy(j, (y + r) % NY).wait_send()
+
+    def sent_here(u, slot, z):
+        rows = unit_rows(u)
+        x_copy(u, mid.at[rows, :], wr2.at[0, rows, :], 0, right).wait_send()
+        pl.when(z != me.z)(lambda: z_copy(u, slot, z).wait_send())
+
+    def sent_there(u):
+        rows = unit_rows(u)
+        x_copy(u, mid.at[rows, :], wr2.at[1, rows, :], 1, right).wait_send()
+        x_copy(u, mid.at[rows, :], wr2.at[2, rows, :], 2, left).wait_send()
+
+    each_unit(me, sent_here, sent_there)
     for c in sent:
         c.wait_send()
 
 
 def sums(dn, wg, gg, x, gain):
-    span = NZ * BLOCK
     return pl.pallas_call(
         sums_kernel,
         out_shape=(
@@ -546,18 +689,18 @@
             pltpu.VMEM((TOK, D), BF),
             pltpu.VMEM((2, TOK, D), BF),
             pltpu.VMEM((2, PW, GW), BF),
+            pltpu.VMEM((2, PW, GW), BF),
+            pltpu.VMEM((3, PW, GW), BF),
             pltpu.VMEM((PW, GW), BF),
             pltpu.VMEM((PW, GW), BF),
-            pltpu.VMEM((NY, PW, 128), BF),
-            pltpu.VMEM((2 * span, 128), BF),
-            pltpu.VMEM((span, 128), BF),
-            pltpu.VMEM((span, 128), BF),
-            pltpu.VMEM((NZ, BLOCK, 128), BF),
+            pltpu.VMEM((SHARD, NZ, UNIT, GW), BF),
+            pltpu.VMEM((SHARD, NY, UNIT, 128), F32),
             pltpu.VMEM((2, 16, 128), F32),
             pltpu.VMEM((NY, 16, 128), F32),
             pltpu.VMEM((4, 16, 128), F32),
             pltpu.VMEM((NZ, 16, 128), F32),
-            dma(4), dma(4), dma(4), dma(4), dma(4, 3), dma(4, 3), dma(8), dma(8), dma(14), dma(14),
+            dma(4), dma(4), dma(2, 4), dma(2, 4), dma(3, 12), dma(3, 12), dma(12), dma(3, 8),
+            dma(3, 4), dma(3), dma(14), dma(14),
         ],
         compiler_params=pltpu.CompilerParams(
             collective_id=2, has_side_effects=True, vmem_limit_bytes=48 * 2**20
@@ -574,12 +717,15 @@
     q = lax.dot_general(weights[:QW], normed, (((1,), (1,)), ((), ())), preferred_element_type=F32).astype(BF)
     kv = lax.dot_general(normed, weights[QW:], (((1,), (1,)), ((), ())), preferred_element_type=F32).astype(BF)
     d_query, kv_sums, context = attend(q, kv, cot)
-    d_proj = jnp.concatenate([d_query.T, kv_sums], axis=1)
-    d_normed = jnp.dot(d_proj, weights, preferred_element_type=F32).astype(BF)
+    d_query = d_query.T
+    d_proj = jnp.concatenate([d_query, kv_sums], axis=1)
+    d_normed = jnp.dot(d_proj, weights, preferred_element_type=F32)
+    gain_terms = jnp.sum(d_normed * normed.astype(F32), axis=0)
+    by_head = [kv_sums[:, h * HEAD : (h + 1) * HEAD] for h in (0, 2, 4, 1, 3, 5)]
+    d_proj = jnp.concatenate([d_query] + by_head, axis=1)
     grad = lax.dot_general(d_proj, normed, (((0,), (0,)), ((), ())), preferred_element_type=F32)
-    gain_terms = jnp.sum(grad * weights.astype(F32), axis=0)
     gain_terms = jnp.pad(gain_terms.reshape(12, 128), ((0, 4), (0, 0)))
-    d_tokens, weight_sums, gain_sums = sums(d_normed, grad.astype(BF), gain_terms, x, gain)
+    d_tokens, weight_sums, gain_sums = sums(d_normed.astype(BF), grad.astype(BF), gain_terms, x, gain)
     factor = 1.0 / math.sqrt(16 * SEQ)
     weight_grad = weight_sums[:, :SLAB].T * factor
     gain_grad = gain_sums[:12].reshape(2, 2, NY, SLAB).transpose(0, 2, 1, 3).reshape(D)

time: 132 us -> 119 us (0.902)
  Pallas kernels: 118 us -> 101 us
  local copies, waits for them, and re-layouts: 5.46 us -> 8.34 us
  matrix products: 5.78 us -> 7.25 us
    pallas_call x1, Pallas kernels: 45.1 us -> 33.4 us  [gather(): pl.pallas_call(gather_kernel, out_shape=(jax.ShapeDtypeStruct((ROWS, D),...]
    pallas_call x1, Pallas kernels: 43.1 us -> 35.9 us  [sums(): pl.pallas_call(sums_kernel, out_shape=(jax.ShapeDtypeStruct((TOK, D), BF)...]
    pallas_call x1, Pallas kernels: 29.6 us -> 31.3 us  [attend(): pl.pallas_call(attention_kernel, out_shape=(jax.ShapeDtypeStruct((QW, ROW...]
    dot_general x1, matrix products: 1.44 us -> 3.03 us  [shards(): d_normed = jnp.dot(d_proj, weights, preferred_element_type=F32)]
    unnamed x11 -> x15, local copies, waits for them, and re-layouts: 3.68 us -> 3.73 us
where the time goes in v3:
time: 119 us; the launch traced here: 118 us
  Pallas kernels  101 us (85%)
  local copies, waits for them, and re-layouts  8.34 us (7%)
  matrix products  7.25 us (6%)
  other arithmetic  1.25 us (1%)
    pallas_call x1, Pallas kernels, sums(): pl.pallas_call(sums_kernel, out_shape=(jax.ShapeDtypeStruct((TOK, D), BF)...  35.9 us
    pallas_call x1, Pallas kernels, gather(): pl.pallas_call(gather_kernel, out_shape=(jax.ShapeDtypeStruct((ROWS, D),...  33.4 us
    pallas_call x1, Pallas kernels, attend(): pl.pallas_call(attention_kernel, out_shape=(jax.ShapeDtypeStruct((QW, ROW...  31.3 us
    unnamed x15, local copies, waits for them, and re-layouts  3.73 us
    dot_general x1, matrix products, shards(): d_normed = jnp.dot(d_proj, weights, preferred_element_type=F32)  3.03 us
    dot_general x1, matrix products, shards(): lax.dot_general(d_proj, normed, (((0,), (0,)), ((), ())), preferred_eleme...  2.56 us

profile of v3, /device:TPU:2, one launch (start us, length us, event | category | flops | bytes accessed | tf_op | source)
XLA Modules:
  0.0 118.1 jit_solution(14654865388811180914)
XLA Ops:
  0.6 0.7 broadcast_in_dim.9.gain_ref
  1.3 0.8 pad.8.w_ref
  2.1 1.1 copy.11
  3.2 0.0 copy-start
  3.2 1.0 copy-done
  4.2 33.4 %gather.1 = (bf16[512,1536]{1,0:T(8,128)(2,1)S(1)}, bf16[576,1536]{1,0:T(8,128)(2,1)S(1)}, bf16[192,512]{1,0:T(8,128)(2,1)S(1)}) custom-call(bf16[128,1536]{1,0:T(8,128)(2,1)S(1)} %bitcast.22, f32[1,1536]{1,0:T(1,128)S(1)} %broadcast_in_dim.9.gain_ref, bf16[144,128]{1,0:T(8,128)(2,1)S(1)} %pad.8.w_ref, bf16[768,128]{1,0:T(8,128)(2,1)S(1)} %bitcast.24), custom_call_target="tpu_custom_call" | custom-call | tf_op jit(solution)/shard_map/gather/pallas_call | solution.py:313
  37.6 0.7 convolution_convert_fusion.2.q_ref
  38.3 1.0 convolution_convert_fusion.1.kv_ref
  39.3 31.3 %attention.1 = (bf16[192,512]{1,0:T(8,128)(2,1)S(1)}, bf16[512,384]{1,0:T(8,128)(2,1)S(1)}, bf16[768,128]{1,0:T(8,128)(2,1)S(1)}) custom-call(bf16[192,512]{1,0:T(8,128)(2,1)S(1)} %convolution_convert_fusion.2.q_ref, bf16[512,384]{1,0:T(8,128)(2,1)S(1)} %convolution_convert_fusion.1.kv_ref, bf16[192,512]{1,0:T(8,128)(2,1)S(1)} %get-tuple-element.15.cot_ref), custom_call_target="tpu_custom_call" | custom-call | tf_op jit(solution)/shard_map/attention/pallas_call | solution.py:454
  70.5 0.8 copy.14
  71.4 0.8 copy.12
  72.2 3.0 %multiply_reduce_fusion = (f32[1536]{0:T(1024)S(1)}, bf16[512,1536]{1,0:T(8,128)(2,1)S(1)}) fusion(bf16[512,1536]{1,0:T(8,128)(2,1)S(1)} %get-tuple-element.14, bf16[576,1536]{1,0:T(8,128)(2,1)} %copy-done.2, bf16[512,384]{1,0:T(8,128)(2,1)S(1)} %get-tuple-element.18, bf16[512,192]{1,0:T(8,128)(2,1)} %bitcast.28), kind=kOutput, calls=%fused_computation | convolution fusion | flops 910293504 | bytes 5511168 | tf_op jit(solution)/shard_map/dot_general | solution.py:722
  75.2 0.0 copy-start.4
  75.3 0.9 fusion.7
  76.1 0.1 copy-done.4
  76.2 1.2 %concatenate.7 = bf16[512,576]{1,0:T(8,128)(2,1)S(1)} concatenate(bf16[512,192]{1,0:T(8,128)(2,1)S(1)} %bitcast.29, bf16[512,64]{1,0:T(8,128)(2,1)} %get-tuple-element.37, bf16[512,64]{1,0:T(8,128)(2,1)} %get-tuple-element.36, bf16[512,64]{1,0:T(8,128)(2,1)S(1)} %get-tuple-element.35, bf16[512,64]{1,0:T(8,128)(2,1)S(1)} %get-tuple-element.34, ...), dimensions={1} | concatenate | bytes 1179648 | tf_op jit(solution)/shard_map/concatenate | solution.py:725
  77.4 0.0 copy-start.1
  77.5 2.6 %convolution_convert_fusion.wg_ref = bf16[576,1536]{1,0:T(8,128)(2,1)S(1)} fusion(bf16[512,576]{1,0:T(8,128)(2,1)S(1)} %concatenate.7, bf16[512,1536]{1,0:T(8,128)(2,1)} %copy-done.3), kind=kOutput, calls=%fused_computation.1 | convolution fusion | flops 906854400 | bytes 3932160 | tf_op jit(solution)/shard_map/dot_general | solution.py:726
  80.0 35.9 %sums.1 = (bf16[128,1536]{1,0:T(8,128)(2,1)S(1)}, f32[144,128]{1,0:T(8,128)S(1)}, f32[16,128]{1,0:T(8,128)S(1)}) custom-call(bf16[512,1536]{1,0:T(8,128)(2,1)S(1)} %get-tuple-element.31.dn_ref, bf16[576,1536]{1,0:T(8,128)(2,1)S(1)} %convolution_convert_fusion.wg_ref, f32[16,128]{1,0:T(8,128)S(1)} %pad.9.gg_ref, bf16[128,1536]{1,0:T(8,128)(2,1)S(1)} %bitcast.23, ...), custom_call_target="tpu_custom_call" | custom-call | tf_op jit(solution)/shard_map/sums/pallas_call | solution.py:677
  116.0 0.1 reshape.18
  116.0 0.1 reshape.19
  116.1 0.6 divide_multiply_fusion
  116.7 0.6 multiply_bitcast_fusion
  117.4 0.7 copy.18
  (9 shorter events, 0.0 us)
Async XLA Ops:
  3.2 1.0 copy-start
  37.6 1.7 %copy-start.2 = (bf16[576,1536]{1,0:T(8,128)(2,1)}, bf16[576,1536]{1,0:T(8,128)(2,1)S(1)}, u32[]{:S(2)}) copy-start(bf16[576,1536]{1,0:T(8,128)(2,1)S(1)} %get-tuple-element.13) | copy-start | bytes 5308420
  37.6 34.6 %copy-start.3 = (bf16[512,1536]{1,0:T(8,128)(2,1)}, bf16[512,1536]{1,0:T(8,128)(2,1)S(1)}, u32[]{:S(2)}) copy-start(bf16[512,1536]{1,0:T(8,128)(2,1)S(1)} %get-tuple-element.14) | copy-start | bytes 4718596
  75.2 1.0 copy-start.4
  77.4 2.6 %copy-start.1 = (bf16[1,128,1536]{2,1,0:T(8,128)(2,1)S(1)}, bf16[1,128,1536]{2,1,0:T(8,128)(2,1)}, u32[]{:S(2)}) copy-start(bf16[1,128,1536]{2,1,0:T(8,128)(2,1)} %param.4) | copy-start | bytes 1179652
  80.0 36.1 %copy-start.5 = (bf16[1536]{0:T(1024)(128)(2,1)S(1)}, bf16[1536]{0:T(1024)(128)(2,1)}, u32[]{:S(2)}) copy-start(bf16[1536]{0:T(1024)(128)(2,1)} %param.5) | copy-start | bytes 9220

commit v4 on v3

v4 whole, which is shorter than its diff:
```python
import functools
import math

import jax
import jax.numpy as jnp
from jax import lax
from jax.experimental import pallas as pl
from jax.experimental.pallas import tpu as pltpu
from jax.sharding import PartitionSpec as P

MESH = pl.DeviceIdType.MESH
BF = jnp.bfloat16
F32 = jnp.float32

D = 1536
HEAD = 64
OWN = 3
TOK = 128
NY = 4
NZ = 8
NA = 4
ROWS = NY * TOK
SEQ = NA * ROWS
QW = OWN * HEAD
PW = 3 * QW
SLAB = 96
BLOCK = 144
GW = NY * SLAB
EPS = 1e-05
VMEM = pl.BlockSpec(memory_space=pltpu.VMEM)


class Place:
    def __init__(self):
        d, s = lax.axis_index("dp"), lax.axis_index("sp")
        self.x_lo, self.z = d // NZ, d % NZ
        self.x_hi, self.y, self.core = s // 8, (s // 2) % NY, s % 2
        self.group = self.x_hi * 2 + self.core
        self.far_group = (1 - self.x_hi) * 2 + self.core

    def id(self, x_hi=None, x_lo=None, y=None, z=None, core=None):
        x_hi = self.x_hi if x_hi is None else x_hi
        x_lo = self.x_lo if x_lo is None else x_lo
        y = self.y if y is None else y
        z = self.z if z is None else z
        core = self.core if core is None else core
        return {"dp": x_lo * NZ + z, "sp": x_hi * 8 + y * 2 + core}

    def other_core(self):
        return self.id(core=1 - self.core)

    def mirror(self):
        return self.id(x_hi=1 - self.x_hi, x_lo=1 - self.x_lo)

    def beside(self):
        return self.id(x_lo=1 - self.x_lo)

    def far(self):
        return self.id(x_hi=1 - self.x_hi)

    def along_y(self, step):
        return self.id(y=(self.y + step) % NY)

    def along_z(self, step):
        return self.id(z=(self.z + step) % NZ)

    def along_x(self, step):
        x = (self.x_hi * 2 + self.x_lo + step) % 4
        return self.id(x_hi=x // 2, x_lo=x % 2)


def greet(partners):
    barrier = pltpu.get_barrier_semaphore()
    for partner in partners:
        pl.semaphore_signal(barrier, inc=1, device_id=partner, device_id_type=MESH)
    return functools.partial(pl.semaphore_wait, barrier, len(partners))


def remote(src, dst, send, recv, partner):
    return pltpu.make_async_remote_copy(
        src_ref=src, dst_ref=dst, send_sem=send, recv_sem=recv, device_id=partner, device_id_type=MESH
    )


def rows_at(start, size):
    return pl.ds(pl.multiple_of(start, 16), size)


def lanes_at(start, size):
    return pl.ds(pl.multiple_of(start, 128), size)


def to_grouped(wide):
    parts = []
    for x_hi in range(2):
        for core in range(2):
            for y in range(NY):
                s = x_hi * 8 + y * 2 + core
                parts.append(wide[:, s * SLAB : (s + 1) * SLAB])
    return jnp.concatenate(parts, axis=1)


def to_natural(wide):
    parts = []
    for x_hi in range(2):
        for y in range(NY):
            for core in range(2):
                s = (x_hi * 2 + core) * NY + y
                parts.append(wide[:, s * SLAB : (s + 1) * SLAB])
    return jnp.concatenate(parts, axis=1)


UNIT = 48
UNITS = 12
SHARD = 3


def unit_home(u, y):
    column = (u // 4) * 16 + 4 * y + u % 4
    d = column // SHARD
    return column - SHARD * d, d // NZ, d % NZ


def shard_unit(me, j):
    column = (me.x_lo * NZ + me.z) * SHARD + j
    return (column % 16) // 4, (column // 16) * 4 + column % 4


ALL = ((0, UNITS),)


def each_unit(me, here, there, spans=ALL):
    def step(u, carry):
        slot, x_lo, z = unit_home(u, me.y)
        if here is not None:
            pl.when(x_lo == me.x_lo)(lambda: here(u, slot, z))
        if there is not None:
            pl.when(x_lo != me.x_lo)(lambda: there(u))
        return carry

    for first, end in spans:
        lax.fori_loop(first, end, step, 0)


def unit_rows(u):
    return rows_at(u * UNIT, UNIT)


def gather_phase(me, ready, load, x_ref, gain_ref, w_ref, cot_ref, nall, wall, cots,
                 cot_t, ybuf, ns, nr, cs, cr, ys, yr, zs, zr, xs, xr, ds, dr):
    y = me.y
    right, left = me.along_x(1), me.along_x(3)
    x_at = me.x_hi * 2 + me.x_lo
    own = lanes_at(me.group * GW, GW)
    far = lanes_at(me.far_group * GW, GW)
    hi_left, hi_right = ((x_at + 3) % 4) // 2, ((x_at + 1) % 4) // 2
    of_left = lanes_at((hi_left * 2 + me.core) * GW, GW)
    of_right = lanes_at((hi_right * 2 + me.core) * GW, GW)
    load(w_ref)
    ready()

    def y_copy(j, to):
        return remote(w_ref.at[pl.ds(j * UNIT, UNIT), :], ybuf.at[y, j], ys.at[j], yr.at[j, y], me.id(y=to))

    for j in range(SHARD):
        to, _ = shard_unit(me, j)
        pl.when(to != y)(lambda: y_copy(j, to).start())

    load(x_ref)
    load(gain_ref)
    x = x_ref[...].astype(F32)
    centred = x - jnp.mean(x, axis=1, keepdims=True)
    spread = jnp.mean(centred * centred, axis=1, keepdims=True)
    normed = centred * lax.rsqrt(spread + EPS) * gain_ref[...].astype(F32)
    tok_rows = rows_at(y * TOK, TOK)
    nall[tok_rows, :] = to_grouped(normed).astype(BF)
    up, down = me.along_y(1), me.along_y(3)
    n_up = remote(nall.at[tok_rows, :], nall.at[tok_rows, :], ns.at[0], nr.at[0], up)
    n_down = remote(nall.at[tok_rows, :], nall.at[tok_rows, :], ns.at[1], nr.at[1], down)
    n_up.start()
    n_down.start()

    for j in range(SHARD):
        to, u = shard_unit(me, j)

        @pl.when(to == y)
        def _():
            ybuf[y, j] = w_ref[j * UNIT : (j + 1) * UNIT, :]
            for r in range(1, NY):
                k = (y + r) % NY
                remote(ybuf.at[k, j], ybuf.at[k, j], ys.at[j], yr.at[j, k], me.along_y(r)).wait_recv()
            parts = [ybuf[k, j][:, :SLAB].astype(F32) for k in range(NY)]
            wall[unit_rows(u), own] = jnp.concatenate(parts, axis=1).astype(BF)

    def piece(u, lanes):
        return wall.at[unit_rows(u), lanes]

    def z_copy(u, r):
        return remote(piece(u, own), piece(u, own), zs.at[u, r], zr.at[u], me.along_z(r))

    def x_copy(u, lanes, kind, to):
        return remote(piece(u, lanes), piece(u, lanes), xs.at[kind, u], xr.at[kind, u], to)

    def push(u, slot, z):
        @pl.when(z == me.z)
        def _():
            for r in (1, 7, 2, 6, 3, 5, 4):
                z_copy(u, r).start()

    each_unit(me, push, None)

    cot_copies = []
    load(cot_ref)
    cot_t[...] = cot_ref[...].T
    cot_lanes = lanes_at(y * TOK, TOK)
    for r in range(1, NY):
        to = (y + r) % NY
        c = remote(cot_t.at[rows_at(to * QW, QW), :], cots.at[:, cot_lanes], cs.at[r], cr.at[r], me.along_y(r))
        c.start()
        cot_copies.append(c)
    cots[:, cot_lanes] = cot_t[rows_at(y * QW, QW), :]

    def spread_x(u, slot, z):
        pl.when(z != me.z)(lambda: z_copy(u, 1).wait_recv())
        x_copy(u, own, 0, right).start()
        x_copy(u, own, 1, left).start()

    each_unit(me, spread_x, None)

    half = TOK // 2
    from_down = rows_at(((y + 3) % NY) * TOK, half)
    from_up = rows_at(((y + 1) % NY) * TOK + half, half)
    n_up.wait_recv()
    f_up = remote(nall.at[from_down, :], nall.at[from_down, :], ns.at[2], nr.at[2], up)
    f_up.start()
    n_down.wait_recv()
    f_down = remote(nall.at[from_up, :], nall.at[from_up, :], ns.at[3], nr.at[3], down)
    f_down.start()

    def relay(u):
        x_copy(u, of_left, 0, right).wait_recv()
        pl.when(u % 2 == 0)(lambda: x_copy(u, of_left, 2, right).start())
        x_copy(u, of_right, 1, left).wait_recv()
        pl.when(u % 2 == 1)(lambda: x_copy(u, of_right, 2, left).start())

    each_unit(me, None, relay)

    def last(u, slot, z):
        x_copy(u, far, 2, right).wait_recv()

    each_unit(me, last, None)

    core_copies = []
    for x_hi in range(2):
        lanes = lanes_at((x_hi * 2 + me.core) * GW, GW)
        c = remote(wall.at[:, lanes], wall.at[:, lanes], ds.at[x_hi], dr.at[x_hi], me.other_core())
        c.start()
        core_copies.append(c)
    for c in core_copies:
        c.wait_recv()
    f_up.wait_recv()
    f_down.wait_recv()
    for c in cot_copies:
        c.wait_recv()

    def sent_here(u, slot, z):
        @pl.when(z == me.z)
        def _():
            for r in range(1, NZ):
                z_copy(u, r).wait_send()

        x_copy(u, own, 0, right).wait_send()
        x_copy(u, own, 1, left).wait_send()

    def sent_there(u):
        x_copy(u, own, 2, right).wait_send()

    each_unit(me, sent_here, sent_there)

    for j in range(SHARD):
        to, _ = shard_unit(me, j)
        pl.when(to != y)(lambda: y_copy(j, to).wait_send())
    for c in cot_copies + core_copies + [n_up, n_down, f_up, f_down]:
        c.wait_send()


def dma(*shape):
    return pltpu.SemaphoreType.DMA(shape)


FACTOR = 1.0 / math.sqrt(16 * SEQ)
CHUNK = 256
STEPS = SEQ // CHUNK
EARLY = ((0, 6), (8, 10))
LATE = ((6, 8), (10, 12))


def block_kernel(x_hbm, gain_hbm, w_hbm, cot_hbm, ctx_ref, dx_ref, wout_ref, gout_ref,
                 x_ref, gain_ref, shard_ref, d_ctx, n_ref, w_ref, cot_ref, cot_t, ybuf, ls,
                 *rest):
    me = Place()
    y = me.y
    partners = (
        [me.along_z(r) for r in range(1, NZ)]
        + [me.along_y(r) for r in range(1, NY)]
        + [me.along_x(r) for r in range(1, 4)]
        + [me.other_core()]
    )
    ready = greet(partners)
    loads = {}
    for k, (src, dst) in enumerate(
        ((w_hbm, shard_ref), (x_hbm, x_ref), (gain_hbm, gain_ref), (cot_hbm, d_ctx))
    ):
        c = pltpu.make_async_copy(src, dst, ls.at[k])
        c.start()
        loads[id(dst)] = c
    gather_phase(
        me, ready, lambda ref: loads[id(ref)].wait(), x_ref, gain_ref, shard_ref, d_ctx,
        n_ref, w_ref, cot_ref, cot_t, ybuf, *rest[:12],
    )
    back_phase(
        me, n_ref, w_ref, cot_ref, x_ref, gain_ref, ctx_ref, dx_ref, wout_ref, gout_ref, *rest[12:]
    )


def back_phase(me, n_ref, w_ref, cot_ref, x_ref, gain_ref, ctx_ref, dx_ref, wout_ref, gout_ref,
               wuse, kvall, dkv, ctx_own, ctx_out, dq_ref, dq_own, out_ref, s_buf, e_buf, r1, mid, r2,
               ks, kr, ss, rs, cs, cr,
               dn_ref, wg_ref, gg_ref, w_sums,
               half_r, to_up, to_down, full_r, s1, wr1, wr2, w_mid, zout, zbuf, yout,
               gcore, gy, gx, gz,
               ns, nr, ws, wr, xs, xr, zs, zr, ys, yr, gs, gr):
    y = me.y
    own = rows_at(me.group * ROWS, ROWS)
    far = rows_at(me.far_group * ROWS, ROWS)
    own_there = rows_at((me.x_hi * 2 + 1 - me.core) * ROWS, ROWS)
    far_there = rows_at(((1 - me.x_hi) * 2 + 1 - me.core) * ROWS, ROWS)
    mine = y * QW
    sent = []

    def go(*args):
        c = remote(*args)
        c.start()
        sent.append(c)
        return c

    def head_lanes(h):
        return slice(h * 128, (h + 1) * 128)

    nt = (((1,), (1,)), ((), ()))
    k_far, k_core = [], []
    for h in range(OWN):
        lanes = head_lanes(h)
        for which in range(2):
            row = QW * (1 + which) + h * HEAD
            wuse[h * 128 + which * HEAD : h * 128 + (which + 1) * HEAD, :] = w_ref[row : row + HEAD, :]
        kvall[own, lanes] = lax.dot_general(n_ref[...], wuse[lanes, :], nt, preferred_element_type=F32).astype(BF)
        k_far.append(go(kvall.at[own, lanes], kvall.at[own, lanes], ks.at[0, h], kr.at[0, h], me.far()))
        k_core.append(go(kvall.at[own, lanes], kvall.at[own, lanes], ks.at[1, h], kr.at[1, h], me.other_core()))
    queries = lax.dot_general(w_ref[:QW, :], n_ref[...], nt, preferred_element_type=F32).astype(BF)
    k_pass = []
    d_far, d_own, d_x, ctx_copies = [], [], [], []

    def pass_keys(h):
        k_far[h].wait_recv()
        k_pass.append(go(kvall.at[far, head_lanes(h)], kvall.at[far, head_lanes(h)], ks.at[2, h], kr.at[2, h], me.other_core()))

    def pass_sums(h):
        lanes = head_lanes(h)
        d_far[h].wait_recv()
        mid[:, lanes] = (dkv[far, lanes].astype(F32) + r1[0, :, lanes].astype(F32)).astype(BF)
        d_x.append(go(mid.at[:, lanes], r2.at[:, lanes], ss.at[2, h], rs.at[2, h], me.far()))

    def finish(h):
        lanes = head_lanes(h)
        d_own[h].wait_recv()
        d_x[h].wait_recv()
        out_ref[:, lanes] = (
            dkv[own, lanes].astype(F32) + r1[1, :, lanes].astype(F32) + r2[:, lanes].astype(F32)
        ).astype(BF)

    pass_keys(0)
    zeros = jnp.zeros((HEAD, ROWS), BF)
    for h in range(OWN):
        lanes = head_lanes(h)
        head_rows = slice(h * HEAD, (h + 1) * HEAD)
        q = queries[head_rows, :] * jnp.asarray(HEAD**-0.5, BF)
        q_pad = jnp.concatenate([q, zeros], axis=0)
        k_core[h].wait_recv()
        k_pass[h].wait_recv()
        top = jnp.full((8, ROWS), -jnp.inf, F32)
        for i in range(STEPS):
            rows = slice(i * CHUNK, (i + 1) * CHUNK)
            s = jnp.dot(kvall[rows, lanes], q_pad, preferred_element_type=F32)
            s_buf[rows, :] = s
            top = jnp.maximum(top, jnp.max(s.reshape(CHUNK // 8, 8, ROWS), axis=0))
        top = jnp.max(top, axis=0, keepdims=True)
        total = jnp.zeros((8, ROWS), F32)
        ctx = jnp.zeros((HEAD, ROWS), F32)
        for i in range(STEPS):
            rows = slice(i * CHUNK, (i + 1) * CHUNK)
            e = jnp.exp(s_buf[rows, :] - top)
            total = total + jnp.sum(e.reshape(CHUNK // 8, 8, ROWS), axis=0)
            e_low = e.astype(BF)
            e_buf[rows, :] = e_low
            v_t = kvall[rows, lanes].T[HEAD:, :]
            ctx = ctx + jnp.dot(v_t, e_low, preferred_element_type=F32)
        inverse = 1.0 / jnp.sum(total, axis=0, keepdims=True)
        ctx = ctx * inverse
        ctx_own[head_rows, :] = ctx.astype(BF)
        rows_there = rows_at(mine + h * HEAD, HEAD)
        for r in range(1, NY):
            to = lanes_at(((y + r) % NY) * TOK, TOK)
            ctx_copies.append(go(ctx_own.at[head_rows, to], ctx_out.at[rows_there, :], cs.at[h, r], cr.at[h, r], me.along_y(r)))
        ctx_out[rows_there, :] = ctx_own[head_rows, lanes_at(y * TOK, TOK)]
        if h + 1 < OWN:
            pass_keys(h + 1)
        if h > 0:
            pass_sums(h - 1)
        cot = (cot_ref[head_rows, :].astype(F32) * inverse).astype(BF)
        row_dot = jnp.sum(cot.astype(F32) * ctx, axis=0, keepdims=True)
        cot_pad = jnp.concatenate([zeros, cot], axis=0)
        q_side = q_pad.T
        cot_side = cot_pad.T
        dq = jnp.zeros((HEAD, ROWS), F32)
        for i in range(STEPS):
            rows = slice(i * CHUNK, (i + 1) * CHUNK)
            d_attn = jnp.dot(kvall[rows, lanes], cot_pad, preferred_element_type=F32)
            e_low = e_buf[rows, :]
            slopes = (e_low.astype(F32) * (d_attn - row_dot)).astype(BF)
            k_t = kvall[rows, lanes].T[:HEAD, :]
            dq = dq + jnp.dot(k_t, slopes, preferred_element_type=F32)
            dkv[rows, lanes] = (
                jnp.dot(slopes, q_side, preferred_element_type=F32)
                + jnp.dot(e_low, cot_side, preferred_element_type=F32)
            ).astype(BF)
        dq_ref[head_rows, :] = (dq * HEAD**-0.5).astype(BF)
        d_far.append(go(dkv.at[far_there, lanes], r1.at[0, :, lanes], ss.at[0, h], rs.at[0, h], me.other_core()))
        d_own.append(go(dkv.at[own_there, lanes], r1.at[1, :, lanes], ss.at[1, h], rs.at[1, h], me.other_core()))
    right, left = me.along_x(1), me.along_x(3)
    x_at = me.x_hi * 2 + me.x_lo
    hi_left, hi_right = ((x_at + 3) % 4) // 2, ((x_at + 1) % 4) // 2
    half = TOK // 2
    up, down = me.along_y(1), me.along_y(3)
    opposite = (y + 2) % NY

    def weight_rows(h):
        rows = jnp.dot(out_ref[:, head_lanes(h)].T, n_ref[...], preferred_element_type=F32).astype(BF)
        for which in range(2):
            row = QW * (1 + which) + h * HEAD
            wg_ref[row : row + HEAD, :] = rows[which * HEAD : (which + 1) * HEAD, :]

    w_core = []

    def to_core(first, size):
        rows = pl.ds(first, size)
        k = len(w_core) // 2
        for x_hi in range(2):
            there = lanes_at((x_hi * 2 + 1 - me.core) * GW, GW)
            w_core.append(go(wg_ref.at[rows, there], wr1.at[x_hi, rows, :], ws.at[x_hi, k], wr.at[x_hi, k], me.other_core()))

    def from_core(k, first, size):
        rows = slice(first, first + size)
        for x_hi in range(2):
            w_core[2 * k + x_hi].wait_recv()
            here = lanes_at((x_hi * 2 + me.core) * GW, GW)
            s1[x_hi, rows, :] = (wg_ref[rows, here].astype(F32) + wr1[x_hi, rows, :].astype(F32)).astype(BF)

    def x_copy(u, src, dst, kind, to):
        return remote(src, dst, xs.at[kind, u], xr.at[kind, u], to)

    def to_opposite(u, slot, z):
        src = s1.at[1 - me.x_hi, unit_rows(u), :]
        dst = wr2.at[0, unit_rows(u), :]
        pl.when(u % 2 == 0)(lambda: x_copy(u, src, dst, 0, right).start())
        pl.when(u % 2 == 1)(lambda: x_copy(u, src, dst, 0, left).start())

    def pass_on(u):
        rows = unit_rows(u)
        pl.when(u % 2 == 0)(lambda: x_copy(u, s1.at[hi_left, rows, :], wr2.at[2, rows, :], 2, left).start())
        pl.when(u % 2 == 1)(lambda: x_copy(u, s1.at[hi_right, rows, :], wr2.at[1, rows, :], 1, right).start())
        x_copy(u, s1.at[0, rows, :], wr2.at[0, rows, :], 0, right).wait_recv()

        @pl.when(u % 2 == 0)
        def _():
            w_mid[rows, :] = (s1[hi_right, rows, :].astype(F32) + wr2[0, rows, :].astype(F32)).astype(BF)
            x_copy(u, w_mid.at[rows, :], wr2.at[1, rows, :], 1, right).start()

        @pl.when(u % 2 == 1)
        def _():
            w_mid[rows, :] = (s1[hi_left, rows, :].astype(F32) + wr2[0, rows, :].astype(F32)).astype(BF)
            x_copy(u, w_mid.at[rows, :], wr2.at[2, rows, :], 2, left).start()


    def z_copy(u, slot, z):
        distance = (z + NZ - me.z) % NZ
        return remote(
            zout.at[unit_rows(u), :], zbuf.at[slot, distance], zs.at[u], zr.at[slot, distance],
            me.id(z=z),
        )

    def over_x(u, slot, z):
        rows = unit_rows(u)
        x_copy(u, s1.at[0, rows, :], wr2.at[1, rows, :], 1, right).wait_recv()
        x_copy(u, s1.at[0, rows, :], wr2.at[2, rows, :], 2, left).wait_recv()
        zout[rows, :] = (
            s1[me.x_hi, rows, :].astype(F32) + wr2[1, rows, :].astype(F32) + wr2[2, rows, :].astype(F32)
        ).astype(BF)
        pl.when(z != me.z)(lambda: z_copy(u, slot, z).start())


    wg_ref[:QW, :] = jnp.dot(dq_ref[...], n_ref[...], preferred_element_type=F32).astype(BF)
    pass_sums(OWN - 1)
    for h in range(OWN - 1):
        finish(h)
        weight_rows(h)
    to_core(0, 288)
    to_core(384, 96)
    from_core(0, 0, 288)
    from_core(1, 384, 96)
    each_unit(me, to_opposite, None, EARLY)
    finish(OWN - 1)
    dq_own[...] = dq_ref[...].T
    gain_terms = jnp.zeros((8, D), F32)
    for r in (2, 1, 3, 0):
        at = (y + r) % NY
        rows = rows_at(at * TOK, TOK)
        first_rows = rows_at(at * TOK, half)
        rest_rows = rows_at(at * TOK + half, half)
        part = jnp.dot(dq_own[rows, :], w_ref[:QW, :], preferred_element_type=F32) + jnp.dot(
            out_ref[rows, :], wuse[...], preferred_element_type=F32
        )
        dn_ref[rows, :] = part.astype(BF)
        if r == 2:
            h_up = go(dn_ref.at[first_rows, :], half_r.at[0], ns.at[0], nr.at[0], up)
            h_down = go(dn_ref.at[rest_rows, :], half_r.at[1], ns.at[1], nr.at[1], down)
            weight_rows(OWN - 1)
            to_core(288, 96)
            to_core(480, 96)
        terms = part * n_ref[rows, :].astype(F32)
        gain_terms = gain_terms + jnp.sum(terms.reshape(TOK // 8, 8, D), axis=0)
    gain_terms = jnp.sum(gain_terms, axis=0, keepdims=True)
    gg_ref[...] = jnp.zeros((16, 128), F32)
    for k in range(D // 128):
        gg_ref[k : k + 1, :] = gain_terms[:, k * 128 : (k + 1) * 128]
    gcore[me.core] = gg_ref[...]
    g_core = go(gg_ref, gcore.at[me.core], gs.at[0], gr.at[0], me.other_core())
    from_core(2, 288, 96)
    from_core(3, 480, 96)
    each_unit(me, to_opposite, None, LATE)
    each_unit(me, None, pass_on, EARLY)
    g_core.wait_recv()
    gy[y] = gcore[0] + gcore[1]
    g_y = [go(gy.at[y], gy.at[y], gs.at[r], gr.at[r], me.along_y(r)) for r in range(1, NY)]
    each_unit(me, None, pass_on, LATE)
    each_unit(me, over_x, None, EARLY)
    h_up.wait_recv()
    block = rows_at(((y + 1) % NY) * TOK, half)
    rest = rows_at(((y + 1) % NY) * TOK + half, half)
    to_up[:half, :] = (dn_ref[block, :].astype(F32) + half_r[0].astype(F32)).astype(BF)
    to_up[half:, :] = dn_ref[rest, :]
    f_up = go(to_up, full_r.at[0], ns.at[2], nr.at[2], up)
    h_down.wait_recv()
    block = rows_at(((y + 3) % NY) * TOK, half)
    rest = rows_at(((y + 3) % NY) * TOK + half, half)
    to_down[:half, :] = dn_ref[block, :]
    to_down[half:, :] = (dn_ref[rest, :].astype(F32) + half_r[1].astype(F32)).astype(BF)
    f_down = go(to_down, full_r.at[1], ns.at[3], nr.at[3], down)

    for c in g_y:
        c.wait_recv()
    gx[x_at] = gy[0] + gy[1] + gy[2] + gy[3]
    g_x = [go(gx.at[x_at], gx.at[x_at], gs.at[3 + r], gr.at[3 + r], me.along_x(r)) for r in range(1, 4)]

    each_unit(me, over_x, None, LATE)
    for c in g_x:
        c.wait_recv()
    gz[me.z] = gx[0] + gx[1] + gx[2] + gx[3]
    g_z = [go(gz.at[me.z], gz.at[me.z], gs.at[6 + r], gr.at[6 + r], me.along_z(r)) for r in range(1, NZ)]

    def y_copy(j, to):
        return remote(yout.at[j, to], w_sums.at[pl.ds(j * UNIT, UNIT), :], ys.at[j, to], yr.at[j], me.id(y=to))

    for j in range(SHARD):
        holder, u = shard_unit(me, j)

        @pl.when(holder == y)
        def _():
            total = zout[unit_rows(u), :].astype(F32)
            for r in range(1, NZ):
                remote(zbuf.at[j, r], zbuf.at[j, r], zs.at[u], zr.at[j, r], me.along_z(r)).wait_recv()
                total = total + zbuf[j, r].astype(F32)
            for k in range(NY):
                rows = total[:, k * SLAB : (k + 1) * SLAB]
                rows = jnp.concatenate([rows, jnp.zeros((UNIT, 128 - SLAB), F32)], axis=1)
                yout[j, k] = rows
            for r in range(1, NY):
                y_copy(j, (y + r) % NY).start()
            w_sums[j * UNIT : (j + 1) * UNIT, :] = yout[j, y]

    x = x_ref[...].astype(F32)
    centred = x - jnp.mean(x, axis=1, keepdims=True)
    spread = jnp.mean(centred * centred, axis=1, keepdims=True)
    scale = lax.rsqrt(spread + EPS)
    hat = centred * scale
    f_up.wait_recv()
    f_down.wait_recv()
    d_normed = (
        dn_ref[rows_at(y * TOK, TOK), :].astype(F32) + full_r[0].astype(F32) + full_r[1].astype(F32)
    )
    inner = to_natural(d_normed) * gain_ref[...].astype(F32)
    first_mean = jnp.mean(inner, axis=1, keepdims=True)
    second = jnp.mean(inner * hat, axis=1, keepdims=True)
    dx_ref[...] = (scale * (inner - first_mean - hat * second)).astype(BF)

    for c in g_z:
        c.wait_recv()
    total = gz[0]
    for k in range(1, NZ):
        total = total + gz[k]
    total = jnp.concatenate([total[k : k + 1, :] for k in range(D // 128)], axis=1)
    gout_ref[...] = to_natural(total) / gain_ref[...].astype(F32) * FACTOR

    for j in range(SHARD):
        holder, u = shard_unit(me, j)

        @pl.when(holder != y)
        def _():
            y_copy(j, y).wait_recv()

        @pl.when(holder == y)
        def _():
            for r in range(1, NY):
                y_copy(j, (y + r) % NY).wait_send()

    wout_ref[...] = w_sums[...][:, :SLAB] * FACTOR
    for c in ctx_copies:
        c.wait_recv()
    ctx_ref[...] = ctx_out[...].T

    def sent_here(u, slot, z):
        rows = unit_rows(u)
        x_copy(u, w_mid.at[rows, :], wr2.at[0, rows, :], 0, right).wait_send()
        pl.when(z != me.z)(lambda: z_copy(u, slot, z).wait_send())

    def sent_there(u):
        rows = unit_rows(u)
        x_copy(u, w_mid.at[rows, :], wr2.at[1, rows, :], 1, right).wait_send()
        x_copy(u, w_mid.at[rows, :], wr2.at[2, rows, :], 2, left).wait_send()

    each_unit(me, sent_here, sent_there)
    for c in sent:
        c.wait_send()


def block(x, gain, w, cot):
    return pl.pallas_call(
        block_kernel,
        out_shape=(
            jax.ShapeDtypeStruct((TOK, NY * QW), BF),
            jax.ShapeDtypeStruct((TOK, D), BF),
            jax.ShapeDtypeStruct((BLOCK, SLAB), F32),
            jax.ShapeDtypeStruct((1, D), F32),
        ),
        in_specs=[pl.BlockSpec(memory_space=pl.ANY)] * 4,
        out_specs=(VMEM,) * 4,
        scratch_shapes=[
            pltpu.VMEM((TOK, D), BF),
            pltpu.VMEM((1, D), BF),
            pltpu.VMEM((BLOCK, 128), BF),
            pltpu.VMEM((TOK, NY * QW), BF),
            pltpu.VMEM((ROWS, D), BF),
            pltpu.VMEM((PW, D), BF),
            pltpu.VMEM((QW, ROWS), BF),
            pltpu.VMEM((NY * QW, TOK), BF),
            pltpu.VMEM((NY, SHARD, UNIT, 128), BF),
            dma(4),
            dma(4), dma(4), dma(4), dma(4), dma(3), dma(3, 4), dma(12, 8), dma(12),
            dma(3, 12), dma(3, 12), dma(2), dma(2),
            pltpu.VMEM((2 * QW, D), BF),
            pltpu.VMEM((SEQ, 2 * QW), BF),
            pltpu.VMEM((SEQ, 2 * QW), BF),
            pltpu.VMEM((QW, ROWS), BF),
            pltpu.VMEM((NY * QW, TOK), BF),
            pltpu.VMEM((QW, ROWS), BF),
            pltpu.VMEM((ROWS, QW), BF),
            pltpu.VMEM((ROWS, 2 * QW), BF),
            pltpu.VMEM((SEQ, ROWS), F32),
            pltpu.VMEM((SEQ, ROWS), BF),
            pltpu.VMEM((2, ROWS, 2 * QW), BF),
            pltpu.VMEM((ROWS, 2 * QW), BF),
            pltpu.VMEM((ROWS, 2 * QW), BF),
            dma(3, 3), dma(3, 3), dma(3, 3), dma(3, 3), dma(3, 4), dma(3, 4),
            pltpu.VMEM((ROWS, D), BF),
            pltpu.VMEM((PW, D), BF),
            pltpu.VMEM((16, 128), F32),
            pltpu.VMEM((BLOCK, 128), F32),
            pltpu.VMEM((2, TOK // 2, D), BF),
            pltpu.VMEM((TOK, D), BF),
            pltpu.VMEM((TOK, D), BF),
            pltpu.VMEM((2, TOK, D), BF),
            pltpu.VMEM((2, PW, GW), BF),
            pltpu.VMEM((2, PW, GW), BF),
            pltpu.VMEM((3, PW, GW), BF),
            pltpu.VMEM((PW, GW), BF),
            pltpu.VMEM((PW, GW), BF),
            pltpu.VMEM((SHARD, NZ, UNIT, GW), BF),
            pltpu.VMEM((SHARD, NY, UNIT, 128), F32),
            pltpu.VMEM((2, 16, 128), F32),
            pltpu.VMEM((NY, 16, 128), F32),
            pltpu.VMEM((4, 16, 128), F32),
            pltpu.VMEM((NZ, 16, 128), F32),
            dma(4), dma(4), dma(2, 4), dma(2, 4), dma(3, 12), dma(3, 12), dma(12), dma(3, 8),
            dma(3, 4), dma(3), dma(14), dma(14),
        ],
        compiler_params=pltpu.CompilerParams(
            collective_id=0, has_side_effects=True, vmem_limit_bytes=56 * 2**20
        ),
        name="block",
    )(x, gain, w, cot)


def shards(tokens, norm_gain, qkv_weight, d_context):
    x, gain = tokens[0], norm_gain[None, :]
    w = jnp.pad(qkv_weight.T, ((0, 0), (0, 128 - SLAB)))
    context, d_tokens, weight_grad, gain_grad = block(x, gain, w, d_context[0])
    return (context[None], d_tokens[None], weight_grad.T, gain_grad.reshape(D))


def solution(mesh):
    in_specs = (P("dp", "sp", None), P(), P("sp", "dp"), P("dp", "sp", None))
    out_specs = (P("dp", "sp", None), P("dp", "sp", None), P("sp", "dp"), P())
    return jax.shard_map(shards, mesh=mesh, in_specs=in_specs, out_specs=out_specs, check_vma=False)
```

time: 119 us -> 106 us (0.89)
  matrix products: 7.25 us -> 0 us
  Pallas kernels: 101 us -> 98 us
  local copies, waits for them, and re-layouts: 8.34 us -> 5.85 us
    dot_general x4 -> x0, matrix products: 7.25 us -> none  [the longest x1 3.03 us: shards(): d_normed = jnp.dot(d_proj, weights, preferred_element_type=F32)]
    pallas_call x3 -> x1, Pallas kernels: 101 us -> 98 us  [block(): pl.pallas_call(block_kernel, out_shape=(jax.ShapeDtypeStruct((TOK, NY * Q...]
    pallas_call x0 -> x1, other arithmetic: none -> 1.36 us  [block(): pl.pallas_call(block_kernel, out_shape=(jax.ShapeDtypeStruct((TOK, NY * Q...]
    mul x2 -> x0, other arithmetic: 1.25 us -> none  [the longest x1 0.64 us: shards(): weight_grad = weight_sums[:, :SLAB].T * factor]
    concatenate x1 -> x0, local copies, waits for them, and re-layouts: 1.24 us -> none  [shards(): d_proj = jnp.concatenate([d_query] + by_head, axis=1)]
    unnamed x15 -> x9, local copies, waits for them, and re-layouts: 3.73 us -> 3.86 us
where the time goes in v4:
time: 106 us
  Pallas kernels  98 us (92%)
  local copies, waits for them, and re-layouts  5.85 us (6%)
  other arithmetic  1.36 us (1%)
    pallas_call x1, Pallas kernels, block(): pl.pallas_call(block_kernel, out_shape=(jax.ShapeDtypeStruct((TOK, NY * Q...  98 us
    unnamed x9, local copies, waits for them, and re-layouts  3.86 us

profile of v4, /device:TPU:2, one launch (start us, length us, event | category | flops | bytes accessed | tf_op | source)
XLA Modules:
  0.0 105.8 jit_solution(6107555102835101496)
XLA Ops:
  0.6 0.0 copy-start.2
  0.6 0.7 copy-done.2
  1.3 0.6 broadcast_in_dim.9.gain_hbm
  1.9 1.4 %pad.4.w_hbm = bf16[144,128]{1,0:T(8,128)(2,1)} pad(bf16[144,96]{1,0:T(8,128)(2,1)} %bitcast.11, bf16[]{:T(256)} %constant.2.clone.1), padding=0_0x0_32 | pad | bytes 64514 | tf_op jit(solution)/shard_map/jit(_pad)/pad | solution.py:725
  3.3 98.0 %block.1 = (bf16[128,768]{1,0:T(8,128)(2,1)}, bf16[128,1536]{1,0:T(8,128)(2,1)}, f32[144,96]{1,0:T(8,128)}, f32[1,1536]{1,0:T(1,128)}) custom-call(bf16[128,1536]{1,0:T(8,128)(2,1)} %bitcast.6, bf16[1,1536]{1,0:T(2,128)(2,1)} %broadcast_in_dim.9.gain_hbm, bf16[144,128]{1,0:T(8,128)(2,1)} %pad.4.w_hbm, bf16[128,768]{1,0:T(8,128)(2,1)} %bitcast.8), custom_call_target="tpu_custom_call" | custom-call | tf_op jit(solution)/shard_map/block/pallas_call | solution.py:657
  101.3 0.0 copy-start
  101.3 1.4 %reduce = f32[1536]{0:T(1024)} reduce(f32[1,1536]{1,0:T(1,128)} %get-tuple-element.11, f32[]{:T(128)} %constant.7), dimensions={0}, to_apply=%get-tuple-element.11.reduce_sub_computation | reduce | bytes 12292 | tf_op jit(solution)/shard_map/block/pallas_call | solution.py:657
  102.6 1.6 %copy.11 = bf16[1,128,768]{2,1,0:T(8,128)(2,1)} copy(bf16[1,128,768]{2,1,0:T(8,128)(2,1)} %bitcast.9) | data formatting | bytes 393216
  104.3 0.0 copy-done
  104.3 0.0 copy-start.1
  104.3 0.7 copy.12
  105.0 0.2 copy-done.1
  105.2 0.6 copy.13
Async XLA Ops:
  0.6 0.7 copy-start.2
  101.3 3.0 %copy-start = (bf16[128,1536]{1,0:T(8,128)(2,1)S(1)}, bf16[128,1536]{1,0:T(8,128)(2,1)}, u32[]{:S(2)}) copy-start(bf16[128,1536]{1,0:T(8,128)(2,1)} %get-tuple-element.9) | copy-start | bytes 1179652
  104.3 0.9 copy-start.1

commit v5 on v4

--- a/solution.py
+++ b/solution.py
@@ -46,6 +46,20 @@
         core = self.core if core is None else core
         return {"dp": x_lo * NZ + z, "sp": x_hi * 8 + y * 2 + core}
 
+    def find_units(self):
+        self.homes, self.sends = [], []
+        for j in range(SHARD):
+            y, u = shard_unit(self, j)
+            x_lo, z = unit_home(u, y)
+            self.homes.append(self.id(x_lo=x_lo, z=z, y=y))
+            self.sends.append((y != self.y) | (x_lo != self.x_lo) | (z != self.z))
+        self.has, self.unit = unit_at(self.x_lo, self.z, self.y)
+        volume, self.place = unit_source(self.unit, self.y)
+        elsewhere = volume != self.x_lo * NZ + self.z
+        self.sources = [self.id(x_lo=volume // NZ, z=volume % NZ, y=k) for k in range(NY)]
+        self.gets = [self.has & ((self.y != k) | elsewhere) for k in range(NY)]
+        self.keeps = [self.has & (self.y == k) & jnp.logical_not(elsewhere) for k in range(NY)]
+
     def other_core(self):
         return self.id(core=1 - self.core)
 
@@ -69,11 +83,28 @@
         return self.id(x_hi=x // 2, x_lo=x % 2)
 
 
-def greet(partners):
+def greet(me):
     barrier = pltpu.get_barrier_semaphore()
+    partners = (
+        [me.along_z(r) for r in range(1, NZ)]
+        + [me.along_y(r) for r in range(1, NY)]
+        + [me.along_x(r) for r in range(1, 4)]
+        + [me.other_core()]
+    )
+
+    def tell(partner):
+        pl.semaphore_signal(barrier, inc=1, device_id=partner, device_id_type=MESH)
+
     for partner in partners:
-        pl.semaphore_signal(barrier, inc=1, device_id=partner, device_id_type=MESH)
-    return functools.partial(pl.semaphore_wait, barrier, len(partners))
+        tell(partner)
+    count = jnp.int32(len(partners))
+    for j in range(SHARD):
+        pl.when(me.sends[j])(lambda: tell(me.homes[j]))
+        count = count + me.sends[j].astype(jnp.int32)
+    for k in range(NY):
+        pl.when(me.gets[k])(lambda: tell(me.sources[k]))
+        count = count + me.gets[k].astype(jnp.int32)
+    return functools.partial(pl.semaphore_wait, barrier, count)
 
 
 def remote(src, dst, send, recv, partner):
@@ -115,10 +146,22 @@
 SHARD = 3
 
 
+def unit_source(u, y):
+    column = (u // 4) * 16 + 4 * y + u % 4
+    return column // SHARD, column % SHARD
+
+
 def unit_home(u, y):
-    column = (u // 4) * 16 + 4 * y + u % 4
-    d = column // SHARD
-    return column - SHARD * d, d // NZ, d % NZ
+    return u % 2, ((16 * (u // 4) + 4 * y) // SHARD + (u % 4) // 2) % NZ
+
+
+def unit_at(x_lo, z, y):
+    found, unit = jnp.int32(0), jnp.int32(0)
+    for k in range(SHARD):
+        for h in range(2):
+            hit = (((16 * k + 4 * y) // SHARD + h) % NZ == z).astype(jnp.int32)
+            found, unit = found + hit, unit + hit * (4 * k + 2 * h)
+    return found > 0, unit + x_lo
 
 
 def shard_unit(me, j):
@@ -126,14 +169,11 @@
     return (column % 16) // 4, (column // 16) * 4 + column % 4
 
 
-ALL = ((0, UNITS),)
-
-
-def each_unit(me, here, there, spans=ALL):
+def each_unit(me, here, there, spans):
     def step(u, carry):
-        slot, x_lo, z = unit_home(u, me.y)
+        x_lo, z = unit_home(u, me.y)
         if here is not None:
-            pl.when(x_lo == me.x_lo)(lambda: here(u, slot, z))
+            pl.when(x_lo == me.x_lo)(lambda: here(u, z))
         if there is not None:
             pl.when(x_lo != me.x_lo)(lambda: there(u))
         return carry
@@ -142,12 +182,22 @@
         lax.fori_loop(first, end, step, 0)
 
 
+def near_first(me, x_lo, act):
+    def step(n, carry):
+        r = jnp.where(n % 2 == 1, (n + 1) // 2, (NZ - n // 2) % NZ)
+        has, u = unit_at(x_lo, (me.z + NZ - r) % NZ, me.y)
+        pl.when(has)(lambda: act(r, u))
+        return carry
+
+    lax.fori_loop(0, NZ, step, 0)
+
+
 def unit_rows(u):
     return rows_at(u * UNIT, UNIT)
 
 
-def gather_phase(me, ready, load, x_ref, gain_ref, w_ref, cot_ref, nall, wall, cots,
-                 cot_t, ybuf, ns, nr, cs, cr, ys, yr, zs, zr, xs, xr, ds, dr):
+def gather_phase(me, ready, load, x_ref, gain_ref, raw_ref, cot_ref, nall, wall, cots,
+                 w_ref, cot_t, ybuf, ns, nr, cs, cr, ys, yr, zs, zr, xs, xr, ds, dr):
     y = me.y
     right, left = me.along_x(1), me.along_x(3)
     x_at = me.x_hi * 2 + me.x_lo
@@ -156,15 +206,15 @@
     hi_left, hi_right = ((x_at + 3) % 4) // 2, ((x_at + 1) % 4) // 2
     of_left = lanes_at((hi_left * 2 + me.core) * GW, GW)
     of_right = lanes_at((hi_right * 2 + me.core) * GW, GW)
-    load(w_ref)
+    load(raw_ref)
+    w_ref[...] = jnp.concatenate([raw_ref[...], jnp.zeros((BLOCK, 128 - SLAB), BF)], axis=1)
     ready()
 
-    def y_copy(j, to):
-        return remote(w_ref.at[pl.ds(j * UNIT, UNIT), :], ybuf.at[y, j], ys.at[j], yr.at[j, y], me.id(y=to))
+    def y_copy(j):
+        return remote(w_ref.at[pl.ds(j * UNIT, UNIT), :], ybuf.at[y], ys.at[j], yr.at[y], me.homes[j])
 
     for j in range(SHARD):
-        to, _ = shard_unit(me, j)
-        pl.when(to != y)(lambda: y_copy(j, to).start())
+        pl.when(me.sends[j])(lambda: y_copy(j).start())
 
     load(x_ref)
     load(gain_ref)
@@ -180,34 +230,31 @@
     n_up.start()
     n_down.start()
 
-    for j in range(SHARD):
-        to, u = shard_unit(me, j)
-
-        @pl.when(to == y)
+    for k in range(NY):
+        pl.when(me.gets[k])(lambda: remote(ybuf.at[k], ybuf.at[k], ys.at[0], yr.at[k], me.sources[k]).wait_recv())
+
+        @pl.when(me.keeps[k])
         def _():
-            ybuf[y, j] = w_ref[j * UNIT : (j + 1) * UNIT, :]
-            for r in range(1, NY):
-                k = (y + r) % NY
-                remote(ybuf.at[k, j], ybuf.at[k, j], ys.at[j], yr.at[j, k], me.along_y(r)).wait_recv()
-            parts = [ybuf[k, j][:, :SLAB].astype(F32) for k in range(NY)]
-            wall[unit_rows(u), own] = jnp.concatenate(parts, axis=1).astype(BF)
+            ybuf[k] = w_ref[rows_at(me.place * UNIT, UNIT), :]
+
+    @pl.when(me.has)
+    def _():
+        parts = [ybuf[k][:, :SLAB].astype(F32) for k in range(NY)]
+        wall[unit_rows(me.unit), own] = jnp.concatenate(parts, axis=1).astype(BF)
 
     def piece(u, lanes):
         return wall.at[unit_rows(u), lanes]
 
     def z_copy(u, r):
-        return remote(piece(u, own), piece(u, own), zs.at[u, r], zr.at[u], me.along_z(r))
-
-    def x_copy(u, lanes, kind, to):
-        return remote(piece(u, lanes), piece(u, lanes), xs.at[kind, u], xr.at[kind, u], to)
-
-    def push(u, slot, z):
-        @pl.when(z == me.z)
-        def _():
-            for r in (1, 7, 2, 6, 3, 5, 4):
-                z_copy(u, r).start()
-
-    each_unit(me, push, None)
+        return remote(piece(u, own), piece(u, own), zs.at[r], zr.at[r], me.along_z(r))
+
+    def x_copy(u, r, lanes, kind, to):
+        return remote(piece(u, lanes), piece(u, lanes), xs.at[kind, r], xr.at[kind, r], to)
+
+    @pl.when(me.has)
+    def _():
+        for r in (1, 7, 2, 6, 3, 5, 4):
+            z_copy(me.unit, r).start()
 
     cot_copies = []
     load(cot_ref)
@@ -220,12 +267,12 @@
         cot_copies.append(c)
     cots[:, cot_lanes] = cot_t[rows_at(y * QW, QW), :]
 
-    def spread_x(u, slot, z):
-        pl.when(z != me.z)(lambda: z_copy(u, 1).wait_recv())
-        x_copy(u, own, 0, right).start()
-        x_copy(u, own, 1, left).start()
-
-    each_unit(me, spread_x, None)
+    def spread_x(r, u):
+        pl.when(r != 0)(lambda: z_copy(u, r).wait_recv())
+        x_copy(u, r, own, 0, right).start()
+        x_copy(u, r, own, 1, left).start()
+
+    near_first(me, me.x_lo, spread_x)
 
     half = TOK // 2
     from_down = rows_at(((y + 3) % NY) * TOK, half)
@@ -237,18 +284,14 @@
     f_down = remote(nall.at[from_up, :], nall.at[from_up, :], ns.at[3], nr.at[3], down)
     f_down.start()
 
-    def relay(u):
-        x_copy(u, of_left, 0, right).wait_recv()
-        pl.when(u % 2 == 0)(lambda: x_copy(u, of_left, 2, right).start())
-        x_copy(u, of_right, 1, left).wait_recv()
-        pl.when(u % 2 == 1)(lambda: x_copy(u, of_right, 2, left).start())
-
-    each_unit(me, None, relay)
-
-    def last(u, slot, z):
-        x_copy(u, far, 2, right).wait_recv()
-
-    each_unit(me, last, None)
+    def relay(r, u):
+        x_copy(u, r, of_left, 0, right).wait_recv()
+        pl.when((u // 2) % 2 == 0)(lambda: x_copy(u, r, of_left, 2, right).start())
+        x_copy(u, r, of_right, 1, left).wait_recv()
+        pl.when((u // 2) % 2 == 1)(lambda: x_copy(u, r, of_right, 2, left).start())
+
+    near_first(me, 1 - me.x_lo, relay)
+    near_first(me, me.x_lo, lambda r, u: x_copy(u, r, far, 2, right).wait_recv())
 
     core_copies = []
     for x_hi in range(2):
@@ -263,23 +306,19 @@
     for c in cot_copies:
         c.wait_recv()
 
-    def sent_here(u, slot, z):
-        @pl.when(z == me.z)
-        def _():
-            for r in range(1, NZ):
-                z_copy(u, r).wait_send()
-
-        x_copy(u, own, 0, right).wait_send()
-        x_copy(u, own, 1, left).wait_send()
-
-    def sent_there(u):
-        x_copy(u, own, 2, right).wait_send()
-
-    each_unit(me, sent_here, sent_there)
-
+    @pl.when(me.has)
+    def _():
+        for r in range(1, NZ):
+            z_copy(me.unit, r).wait_send()
+
+    def sent_here(r, u):
+        x_copy(u, r, own, 0, right).wait_send()
+        x_copy(u, r, own, 1, left).wait_send()
+
+    near_first(me, me.x_lo, sent_here)
+    near_first(me, 1 - me.x_lo, lambda r, u: x_copy(u, r, own, 2, right).wait_send())
     for j in range(SHARD):
-        to, _ = shard_unit(me, j)
-        pl.when(to != y)(lambda: y_copy(j, to).wait_send())
+        pl.when(me.sends[j])(lambda: y_copy(j).wait_send())
     for c in cot_copies + core_copies + [n_up, n_down, f_up, f_down]:
         c.wait_send()
 
@@ -290,23 +329,17 @@
 
 FACTOR = 1.0 / math.sqrt(16 * SEQ)
 CHUNK = 256
-STEPS = SEQ // CHUNK
 EARLY = ((0, 6), (8, 10))
 LATE = ((6, 8), (10, 12))
 
 
 def block_kernel(x_hbm, gain_hbm, w_hbm, cot_hbm, ctx_ref, dx_ref, wout_ref, gout_ref,
-                 x_ref, gain_ref, shard_ref, d_ctx, n_ref, w_ref, cot_ref, cot_t, ybuf, ls,
+                 x_ref, gain_ref, shard_ref, d_ctx, n_ref, w_ref, cot_ref, w_pad, cot_t, ybuf, ls,
                  *rest):
     me = Place()
     y = me.y
-    partners = (
-        [me.along_z(r) for r in range(1, NZ)]
-        + [me.along_y(r) for r in range(1, NY)]
-        + [me.along_x(r) for r in range(1, 4)]
-        + [me.other_core()]
-    )
-    ready = greet(partners)
+    me.find_units()
+    ready = greet(me)
     loads = {}
     for k, (src, dst) in enumerate(
         ((w_hbm, shard_ref), (x_hbm, x_ref), (gain_hbm, gain_ref), (cot_hbm, d_ctx))
@@ -316,7 +349,7 @@
         loads[id(dst)] = c
     gather_phase(
         me, ready, lambda ref: loads[id(ref)].wait(), x_ref, gain_ref, shard_ref, d_ctx,
-        n_ref, w_ref, cot_ref, cot_t, ybuf, *rest[:12],
+        n_ref, w_ref, cot_ref, w_pad, cot_t, ybuf, *rest[:12],
     )
     back_phase(
         me, n_ref, w_ref, cot_ref, x_ref, gain_ref, ctx_ref, dx_ref, wout_ref, gout_ref, *rest[12:]
@@ -333,8 +366,17 @@
     y = me.y
     own = rows_at(me.group * ROWS, ROWS)
     far = rows_at(me.far_group * ROWS, ROWS)
-    own_there = rows_at((me.x_hi * 2 + 1 - me.core) * ROWS, ROWS)
-    far_there = rows_at(((1 - me.x_hi) * 2 + 1 - me.core) * ROWS, ROWS)
+    near = me.x_hi * 2 + 1 - me.core
+    beyond = (1 - me.x_hi) * 2 + 1 - me.core
+    own_there = rows_at(near * ROWS, ROWS)
+    far_there = rows_at(beyond * ROWS, ROWS)
+    groups = (me.group, near, me.far_group, beyond)
+
+    def chunks(at):
+        for i in range(ROWS // CHUNK):
+            here = at * ROWS + i * CHUNK
+            yield rows_at(groups[at] * ROWS + i * CHUNK, CHUNK), slice(here, here + CHUNK)
+
     mine = y * QW
     sent = []
 
@@ -379,32 +421,35 @@
             dkv[own, lanes].astype(F32) + r1[1, :, lanes].astype(F32) + r2[:, lanes].astype(F32)
         ).astype(BF)
 
-    pass_keys(0)
     zeros = jnp.zeros((HEAD, ROWS), BF)
     for h in range(OWN):
         lanes = head_lanes(h)
         head_rows = slice(h * HEAD, (h + 1) * HEAD)
         q = queries[head_rows, :] * jnp.asarray(HEAD**-0.5, BF)
         q_pad = jnp.concatenate([q, zeros], axis=0)
-        k_core[h].wait_recv()
-        k_pass[h].wait_recv()
         top = jnp.full((8, ROWS), -jnp.inf, F32)
-        for i in range(STEPS):
-            rows = slice(i * CHUNK, (i + 1) * CHUNK)
-            s = jnp.dot(kvall[rows, lanes], q_pad, preferred_element_type=F32)
-            s_buf[rows, :] = s
-            top = jnp.maximum(top, jnp.max(s.reshape(CHUNK // 8, 8, ROWS), axis=0))
+        for at in range(NA):
+            if at == 1:
+                k_core[h].wait_recv()
+            if at == 2 and h == 0:
+                pass_keys(0)
+            if at == 3:
+                k_pass[h].wait_recv()
+            for keys, rows in chunks(at):
+                s = jnp.dot(kvall[keys, lanes], q_pad, preferred_element_type=F32)
+                s_buf[rows, :] = s
+                top = jnp.maximum(top, jnp.max(s.reshape(CHUNK // 8, 8, ROWS), axis=0))
         top = jnp.max(top, axis=0, keepdims=True)
         total = jnp.zeros((8, ROWS), F32)
         ctx = jnp.zeros((HEAD, ROWS), F32)
-        for i in range(STEPS):
-            rows = slice(i * CHUNK, (i + 1) * CHUNK)
-            e = jnp.exp(s_buf[rows, :] - top)
-            total = total + jnp.sum(e.reshape(CHUNK // 8, 8, ROWS), axis=0)
-            e_low = e.astype(BF)
-            e_buf[rows, :] = e_low
-            v_t = kvall[rows, lanes].T[HEAD:, :]
-            ctx = ctx + jnp.dot(v_t, e_low, preferred_element_type=F32)
+        for at in range(NA):
+            for keys, rows in chunks(at):
+                e = jnp.exp(s_buf[rows, :] - top)
+                total = total + jnp.sum(e.reshape(CHUNK // 8, 8, ROWS), axis=0)
+                e_low = e.astype(BF)
+                e_buf[rows, :] = e_low
+                v_t = kvall[keys, lanes].T[HEAD:, :]
+                ctx = ctx + jnp.dot(v_t, e_low, preferred_element_type=F32)
         inverse = 1.0 / jnp.sum(total, axis=0, keepdims=True)
         ctx = ctx * inverse
         ctx_own[head_rows, :] = ctx.astype(BF)
@@ -423,20 +468,25 @@
         q_side = q_pad.T
         cot_side = cot_pad.T
         dq = jnp.zeros((HEAD, ROWS), F32)
-        for i in range(STEPS):
-            rows = slice(i * CHUNK, (i + 1) * CHUNK)
-            d_attn = jnp.dot(kvall[rows, lanes], cot_pad, preferred_element_type=F32)
-            e_low = e_buf[rows, :]
-            slopes = (e_low.astype(F32) * (d_attn - row_dot)).astype(BF)
-            k_t = kvall[rows, lanes].T[:HEAD, :]
-            dq = dq + jnp.dot(k_t, slopes, preferred_element_type=F32)
-            dkv[rows, lanes] = (
-                jnp.dot(slopes, q_side, preferred_element_type=F32)
-                + jnp.dot(e_low, cot_side, preferred_element_type=F32)
-            ).astype(BF)
+        for at in (3, 2, 1, 0):
+            for keys, rows in chunks(at):
+                d_attn = jnp.dot(kvall[keys, lanes], cot_pad, preferred_element_type=F32)
+                e_low = e_buf[rows, :]
+                slopes = (e_low.astype(F32) * (d_attn - row_dot)).astype(BF)
+                k_t = kvall[keys, lanes].T[:HEAD, :]
+                dq = dq + jnp.dot(k_t, slopes, preferred_element_type=F32)
+                dkv[keys, lanes] = (
+                    jnp.dot(slopes, q_side, preferred_element_type=F32)
+                    + jnp.dot(e_low, cot_side, preferred_element_type=F32)
+                ).astype(BF)
+            if at == 3:
+                d_far.append(go(dkv.at[far_there, lanes], r1.at[0, :, lanes], ss.at[0, h], rs.at[0, h], me.other_core()))
+            if at == 1:
+                d_own.append(go(dkv.at[own_there, lanes], r1.at[1, :, lanes], ss.at[1, h], rs.at[1, h], me.other_core()))
         dq_ref[head_rows, :] = (dq * HEAD**-0.5).astype(BF)
-        d_far.append(go(dkv.at[far_there, lanes], r1.at[0, :, lanes], ss.at[0, h], rs.at[0, h], me.other_core()))
-        d_own.append(go(dkv.at[own_there, lanes], r1.at[1, :, lanes], ss.at[1, h], rs.at[1, h], me.other_core()))
+        if h == OWN - 1:
+            pass_sums(h)
+
     right, left = me.along_x(1), me.along_x(3)
     x_at = me.x_hi * 2 + me.x_lo
     hi_left, hi_right = ((x_at + 3) % 4) // 2, ((x_at + 1) % 4) // 2
@@ -469,48 +519,44 @@
     def x_copy(u, src, dst, kind, to):
         return remote(src, dst, xs.at[kind, u], xr.at[kind, u], to)
 
-    def to_opposite(u, slot, z):
+    def to_opposite(u, z):
         src = s1.at[1 - me.x_hi, unit_rows(u), :]
         dst = wr2.at[0, unit_rows(u), :]
-        pl.when(u % 2 == 0)(lambda: x_copy(u, src, dst, 0, right).start())
-        pl.when(u % 2 == 1)(lambda: x_copy(u, src, dst, 0, left).start())
+        pl.when((u // 2) % 2 == 0)(lambda: x_copy(u, src, dst, 0, right).start())
+        pl.when((u // 2) % 2 == 1)(lambda: x_copy(u, src, dst, 0, left).start())
 
     def pass_on(u):
         rows = unit_rows(u)
-        pl.when(u % 2 == 0)(lambda: x_copy(u, s1.at[hi_left, rows, :], wr2.at[2, rows, :], 2, left).start())
-        pl.when(u % 2 == 1)(lambda: x_copy(u, s1.at[hi_right, rows, :], wr2.at[1, rows, :], 1, right).start())
+        pl.when((u // 2) % 2 == 0)(lambda: x_copy(u, s1.at[hi_left, rows, :], wr2.at[2, rows, :], 2, left).start())
+        pl.when((u // 2) % 2 == 1)(lambda: x_copy(u, s1.at[hi_right, rows, :], wr2.at[1, rows, :], 1, right).start())
         x_copy(u, s1.at[0, rows, :], wr2.at[0, rows, :], 0, right).wait_recv()
 
-        @pl.when(u % 2 == 0)
+        @pl.when((u // 2) % 2 == 0)
         def _():
             w_mid[rows, :] = (s1[hi_right, rows, :].astype(F32) + wr2[0, rows, :].astype(F32)).astype(BF)
             x_copy(u, w_mid.at[rows, :], wr2.at[1, rows, :], 1, right).start()
 
-        @pl.when(u % 2 == 1)
+        @pl.when((u // 2) % 2 == 1)
         def _():
             w_mid[rows, :] = (s1[hi_left, rows, :].astype(F32) + wr2[0, rows, :].astype(F32)).astype(BF)
             x_copy(u, w_mid.at[rows, :], wr2.at[2, rows, :], 2, left).start()
 
 
-    def z_copy(u, slot, z):
+    def z_copy(u, z):
         distance = (z + NZ - me.z) % NZ
-        return remote(
-            zout.at[unit_rows(u), :], zbuf.at[slot, distance], zs.at[u], zr.at[slot, distance],
-            me.id(z=z),
-        )
-
-    def over_x(u, slot, z):
+        return remote(zout.at[unit_rows(u), :], zbuf.at[distance], zs.at[u], zr.at[distance], me.id(z=z))
+
+    def over_x(u, z):
         rows = unit_rows(u)
         x_copy(u, s1.at[0, rows, :], wr2.at[1, rows, :], 1, right).wait_recv()
         x_copy(u, s1.at[0, rows, :], wr2.at[2, rows, :], 2, left).wait_recv()
         zout[rows, :] = (
             s1[me.x_hi, rows, :].astype(F32) + wr2[1, rows, :].astype(F32) + wr2[2, rows, :].astype(F32)
         ).astype(BF)
-        pl.when(z != me.z)(lambda: z_copy(u, slot, z).start())
+        pl.when(z != me.z)(lambda: z_copy(u, z).start())
 
 
     wg_ref[:QW, :] = jnp.dot(dq_ref[...], n_ref[...], preferred_element_type=F32).astype(BF)
-    pass_sums(OWN - 1)
     for h in range(OWN - 1):
         finish(h)
         weight_rows(h)
@@ -552,8 +598,6 @@
     g_core.wait_recv()
     gy[y] = gcore[0] + gcore[1]
     g_y = [go(gy.at[y], gy.at[y], gs.at[r], gr.at[r], me.along_y(r)) for r in range(1, NY)]
-    each_unit(me, None, pass_on, LATE)
-    each_unit(me, over_x, None, EARLY)
     h_up.wait_recv()
     block = rows_at(((y + 1) % NY) * TOK, half)
     rest = rows_at(((y + 1) % NY) * TOK + half, half)
@@ -567,6 +611,8 @@
     to_down[half:, :] = (dn_ref[rest, :].astype(F32) + half_r[1].astype(F32)).astype(BF)
     f_down = go(to_down, full_r.at[1], ns.at[3], nr.at[3], down)
 
+    each_unit(me, None, pass_on, LATE)
+    each_unit(me, over_x, None, EARLY)
     for c in g_y:
         c.wait_recv()
     gx[x_at] = gy[0] + gy[1] + gy[2] + gy[3]
@@ -578,25 +624,27 @@
     gz[me.z] = gx[0] + gx[1] + gx[2] + gx[3]
     g_z = [go(gz.at[me.z], gz.at[me.z], gs.at[6 + r], gr.at[6 + r], me.along_z(r)) for r in range(1, NZ)]
 
-    def y_copy(j, to):
-        return remote(yout.at[j, to], w_sums.at[pl.ds(j * UNIT, UNIT), :], ys.at[j, to], yr.at[j], me.id(y=to))
-
-    for j in range(SHARD):
-        holder, u = shard_unit(me, j)
-
-        @pl.when(holder == y)
+    own_place = rows_at(me.place * UNIT, UNIT)
+
+    def y_copy(k):
+        return remote(yout.at[k], w_sums.at[own_place, :], ys.at[k], yr.at[me.place], me.sources[k])
+
+    @pl.when(me.has)
+    def _():
+        total = zout[unit_rows(me.unit), :].astype(F32)
+        for r in range(1, NZ):
+            remote(zbuf.at[r], zbuf.at[r], zs.at[0], zr.at[r], me.along_z(r)).wait_recv()
+            total = total + zbuf[r].astype(F32)
+        for k in range(NY):
+            part = total[:, k * SLAB : (k + 1) * SLAB]
+            yout[k] = jnp.concatenate([part, jnp.zeros((UNIT, 128 - SLAB), F32)], axis=1)
+
+    for k in range(NY):
+        pl.when(me.gets[k])(lambda: y_copy(k).start())
+
+        @pl.when(me.keeps[k])
         def _():
-            total = zout[unit_rows(u), :].astype(F32)
-            for r in range(1, NZ):
-                remote(zbuf.at[j, r], zbuf.at[j, r], zs.at[u], zr.at[j, r], me.along_z(r)).wait_recv()
-                total = total + zbuf[j, r].astype(F32)
-            for k in range(NY):
-                rows = total[:, k * SLAB : (k + 1) * SLAB]
-                rows = jnp.concatenate([rows, jnp.zeros((UNIT, 128 - SLAB), F32)], axis=1)
-                yout[j, k] = rows
-            for r in range(1, NY):
-                y_copy(j, (y + r) % NY).start()
-            w_sums[j * UNIT : (j + 1) * UNIT, :] = yout[j, y]
+            w_sums[own_place, :] = yout[k]
 
     x = x_ref[...].astype(F32)
     centred = x - jnp.mean(x, axis=1, keepdims=True)
@@ -622,33 +670,28 @@
     gout_ref[...] = to_natural(total) / gain_ref[...].astype(F32) * FACTOR
 
     for j in range(SHARD):
-        holder, u = shard_unit(me, j)
-
-        @pl.when(holder != y)
-        def _():
-            y_copy(j, y).wait_recv()
-
-        @pl.when(holder == y)
-        def _():
-            for r in range(1, NY):
-                y_copy(j, (y + r) % NY).wait_send()
-
+        rows = pl.ds(j * UNIT, UNIT)
+        pl.when(me.sends[j])(
+            lambda: remote(w_sums.at[rows, :], w_sums.at[rows, :], ys.at[0], yr.at[j], me.homes[j]).wait_recv()
+        )
+    for k in range(NY):
+        pl.when(me.gets[k])(lambda: y_copy(k).wait_send())
     wout_ref[...] = w_sums[...][:, :SLAB] * FACTOR
     for c in ctx_copies:
         c.wait_recv()
     ctx_ref[...] = ctx_out[...].T
 
-    def sent_here(u, slot, z):
+    def sent_here(u, z):
         rows = unit_rows(u)
         x_copy(u, w_mid.at[rows, :], wr2.at[0, rows, :], 0, right).wait_send()
-        pl.when(z != me.z)(lambda: z_copy(u, slot, z).wait_send())
+        pl.when(z != me.z)(lambda: z_copy(u, z).wait_send())
 
     def sent_there(u):
         rows = unit_rows(u)
         x_copy(u, w_mid.at[rows, :], wr2.at[1, rows, :], 1, right).wait_send()
         x_copy(u, w_mid.at[rows, :], wr2.at[2, rows, :], 2, left).wait_send()
 
-    each_unit(me, sent_here, sent_there)
+    each_unit(me, sent_here, sent_there, ((0, UNITS),))
     for c in sent:
         c.wait_send()
 
@@ -667,16 +710,17 @@
         scratch_shapes=[
             pltpu.VMEM((TOK, D), BF),
             pltpu.VMEM((1, D), BF),
-            pltpu.VMEM((BLOCK, 128), BF),
+            pltpu.VMEM((BLOCK, SLAB), BF),
             pltpu.VMEM((TOK, NY * QW), BF),
             pltpu.VMEM((ROWS, D), BF),
             pltpu.VMEM((PW, D), BF),
             pltpu.VMEM((QW, ROWS), BF),
+            pltpu.VMEM((BLOCK, 128), BF),
             pltpu.VMEM((NY * QW, TOK), BF),
-            pltpu.VMEM((NY, SHARD, UNIT, 128), BF),
+            pltpu.VMEM((NY, UNIT, 128), BF),
             dma(4),
-            dma(4), dma(4), dma(4), dma(4), dma(3), dma(3, 4), dma(12, 8), dma(12),
-            dma(3, 12), dma(3, 12), dma(2), dma(2),
+            dma(4), dma(4), dma(4), dma(4), dma(3), dma(4), dma(8), dma(8),
+            dma(3, 8), dma(3, 8), dma(2), dma(2),
             pltpu.VMEM((2 * QW, D), BF),
             pltpu.VMEM((SEQ, 2 * QW), BF),
             pltpu.VMEM((SEQ, 2 * QW), BF),
@@ -704,14 +748,14 @@
             pltpu.VMEM((3, PW, GW), BF),
             pltpu.VMEM((PW, GW), BF),
             pltpu.VMEM((PW, GW), BF),
-            pltpu.VMEM((SHARD, NZ, UNIT, GW), BF),
-            pltpu.VMEM((SHARD, NY, UNIT, 128), F32),
+            pltpu.VMEM((NZ, UNIT, GW), BF),
+            pltpu.VMEM((NY, UNIT, 128), F32),
             pltpu.VMEM((2, 16, 128), F32),
             pltpu.VMEM((NY, 16, 128), F32),
             pltpu.VMEM((4, 16, 128), F32),
             pltpu.VMEM((NZ, 16, 128), F32),
-            dma(4), dma(4), dma(2, 4), dma(2, 4), dma(3, 12), dma(3, 12), dma(12), dma(3, 8),
-            dma(3, 4), dma(3), dma(14), dma(14),
+            dma(4), dma(4), dma(2, 4), dma(2, 4), dma(3, 12), dma(3, 12), dma(12), dma(8),
+            dma(4), dma(3), dma(14), dma(14),
         ],
         compiler_params=pltpu.CompilerParams(
             collective_id=0, has_side_effects=True, vmem_limit_bytes=56 * 2**20
@@ -722,8 +766,7 @@
 
 def shards(tokens, norm_gain, qkv_weight, d_context):
     x, gain = tokens[0], norm_gain[None, :]
-    w = jnp.pad(qkv_weight.T, ((0, 0), (0, 128 - SLAB)))
-    context, d_tokens, weight_grad, gain_grad = block(x, gain, w, d_context[0])
+    context, d_tokens, weight_grad, gain_grad = block(x, gain, qkv_weight.T, d_context[0])
     return (context[None], d_tokens[None], weight_grad.T, gain_grad.reshape(D))
 
 

time: 106 us -> 92.1 us (0.87)
  Pallas kernels: 98 us -> 85.4 us
  local copies, waits for them, and re-layouts: 5.85 us -> 4.46 us
    pallas_call x1, Pallas kernels: 98 us -> 85.4 us  [block(): pl.pallas_call(block_kernel, out_shape=(jax.ShapeDtypeStruct((TOK, NY * Q...]
    pad x1 -> x0, local copies, waits for them, and re-layouts: 1.39 us -> none  [shards(): w = jnp.pad(qkv_weight.T, ((0, 0), (0, 128 - SLAB)))]
where the time goes in v5:
time: 92.1 us; the launch traced here: 91.9 us
  Pallas kernels  85.4 us (93%)
  local copies, waits for them, and re-layouts  4.46 us (5%)
  other arithmetic  1.36 us (1%)
    pallas_call x1, Pallas kernels, block(): pl.pallas_call(block_kernel, out_shape=(jax.ShapeDtypeStruct((TOK, NY * Q...  85.4 us
    unnamed x9, local copies, waits for them, and re-layouts  3.86 us

profile of v5, /device:TPU:2, one launch (start us, length us, event | category | flops | bytes accessed | tf_op | source)
XLA Modules:
  0.0 91.9 jit_solution(15041550373090756462)
XLA Ops:
  0.6 0.0 copy-start.2
  0.6 0.7 copy-done.2
  1.3 0.6 broadcast_in_dim.9.gain_hbm
  1.9 85.4 %block.1 = (bf16[128,768]{1,0:T(8,128)(2,1)}, bf16[128,1536]{1,0:T(8,128)(2,1)}, f32[144,96]{1,0:T(8,128)}, f32[1,1536]{1,0:T(1,128)}) custom-call(bf16[128,1536]{1,0:T(8,128)(2,1)} %bitcast.6, bf16[1,1536]{1,0:T(2,128)(2,1)} %broadcast_in_dim.9.gain_hbm, bf16[144,96]{1,0:T(8,128)(2,1)} %bitcast.11, bf16[128,768]{1,0:T(8,128)(2,1)} %bitcast.8), custom_call_target="tpu_custom_call" | custom-call | tf_op jit(solution)/shard_map/block/pallas_call | solution.py:700
  87.3 0.0 copy-start
  87.3 1.4 %reduce = f32[1536]{0:T(1024)} reduce(f32[1,1536]{1,0:T(1,128)} %get-tuple-element.11, f32[]{:T(128)} %constant.2), dimensions={0}, to_apply=%get-tuple-element.11.reduce_sub_computation | reduce | bytes 12292 | tf_op jit(solution)/shard_map/block/pallas_call | solution.py:700
  88.7 1.6 %copy.11 = bf16[1,128,768]{2,1,0:T(8,128)(2,1)} copy(bf16[1,128,768]{2,1,0:T(8,128)(2,1)} %bitcast.9) | data formatting | bytes 393216
  90.3 0.0 copy-done
  90.3 0.0 copy-start.1
  90.3 0.7 copy.12
  91.0 0.2 copy-done.1
  91.2 0.6 copy.13
Async XLA Ops:
  0.6 0.7 copy-start.2
  87.3 3.0 %copy-start = (bf16[128,1536]{1,0:T(8,128)(2,1)S(1)}, bf16[128,1536]{1,0:T(8,128)(2,1)}, u32[]{:S(2)}) copy-start(bf16[128,1536]{1,0:T(8,128)(2,1)} %get-tuple-element.9) | copy-start | bytes 1179652
  90.3 0.9 %copy-start.1 = (f32[144,96]{1,0:T(8,128)S(1)}, f32[144,96]{1,0:T(8,128)}, u32[]{:S(2)}) copy-start(f32[144,96]{1,0:T(8,128)} %get-tuple-element.10) | copy-start | bytes 165892

commit v6 on v5

--- a/solution.py
+++ b/solution.py
@@ -182,14 +182,14 @@
         lax.fori_loop(first, end, step, 0)
 
 
-def near_first(me, x_lo, act):
+def near_first(me, x_lo, act, first=0, end=NZ):
     def step(n, carry):
         r = jnp.where(n % 2 == 1, (n + 1) // 2, (NZ - n // 2) % NZ)
         has, u = unit_at(x_lo, (me.z + NZ - r) % NZ, me.y)
         pl.when(has)(lambda: act(r, u))
         return carry
 
-    lax.fori_loop(0, NZ, step, 0)
+    lax.fori_loop(first, end, step, 0)
 
 
 def unit_rows(u):
@@ -225,11 +225,16 @@
     tok_rows = rows_at(y * TOK, TOK)
     nall[tok_rows, :] = to_grouped(normed).astype(BF)
     up, down = me.along_y(1), me.along_y(3)
-    n_up = remote(nall.at[tok_rows, :], nall.at[tok_rows, :], ns.at[0], nr.at[0], up)
-    n_down = remote(nall.at[tok_rows, :], nall.at[tok_rows, :], ns.at[1], nr.at[1], down)
-    n_up.start()
-    n_down.start()
-
+    half = TOK // 2
+    low, high = rows_at(y * TOK, half), rows_at(y * TOK + half, half)
+
+    def n_copy(rows, k, to):
+        c = remote(nall.at[rows, :], nall.at[rows, :], ns.at[k], nr.at[k], to)
+        c.start()
+        return c
+
+    n_up, n_down = n_copy(low, 0, up), n_copy(high, 1, down)
+    n_rest = [n_copy(high, 4, up), n_copy(low, 5, down)]
     for k in range(NY):
         pl.when(me.gets[k])(lambda: remote(ybuf.at[k], ybuf.at[k], ys.at[0], yr.at[k], me.sources[k]).wait_recv())
 
@@ -272,17 +277,14 @@
         x_copy(u, r, own, 0, right).start()
         x_copy(u, r, own, 1, left).start()
 
-    near_first(me, me.x_lo, spread_x)
-
-    half = TOK // 2
+    near_first(me, me.x_lo, spread_x, 0, 3)
     from_down = rows_at(((y + 3) % NY) * TOK, half)
     from_up = rows_at(((y + 1) % NY) * TOK + half, half)
     n_up.wait_recv()
-    f_up = remote(nall.at[from_down, :], nall.at[from_down, :], ns.at[2], nr.at[2], up)
-    f_up.start()
+    f_up = n_copy(from_down, 2, up)
     n_down.wait_recv()
-    f_down = remote(nall.at[from_up, :], nall.at[from_up, :], ns.at[3], nr.at[3], down)
-    f_down.start()
+    f_down = n_copy(from_up, 3, down)
+    near_first(me, me.x_lo, spread_x, 3, NZ)
 
     def relay(r, u):
         x_copy(u, r, of_left, 0, right).wait_recv()
@@ -301,8 +303,8 @@
         core_copies.append(c)
     for c in core_copies:
         c.wait_recv()
-    f_up.wait_recv()
-    f_down.wait_recv()
+    for c in n_rest + [f_up, f_down]:
+        c.wait_recv()
     for c in cot_copies:
         c.wait_recv()
 
@@ -319,7 +321,7 @@
     near_first(me, 1 - me.x_lo, lambda r, u: x_copy(u, r, own, 2, right).wait_send())
     for j in range(SHARD):
         pl.when(me.sends[j])(lambda: y_copy(j).wait_send())
-    for c in cot_copies + core_copies + [n_up, n_down, f_up, f_down]:
+    for c in cot_copies + core_copies + n_rest + [n_up, n_down, f_up, f_down]:
         c.wait_send()
 
 
@@ -460,8 +462,6 @@
         ctx_out[rows_there, :] = ctx_own[head_rows, lanes_at(y * TOK, TOK)]
         if h + 1 < OWN:
             pass_keys(h + 1)
-        if h > 0:
-            pass_sums(h - 1)
         cot = (cot_ref[head_rows, :].astype(F32) * inverse).astype(BF)
         row_dot = jnp.sum(cot.astype(F32) * ctx, axis=0, keepdims=True)
         cot_pad = jnp.concatenate([zeros, cot], axis=0)
@@ -483,9 +483,8 @@
                 d_far.append(go(dkv.at[far_there, lanes], r1.at[0, :, lanes], ss.at[0, h], rs.at[0, h], me.other_core()))
             if at == 1:
                 d_own.append(go(dkv.at[own_there, lanes], r1.at[1, :, lanes], ss.at[1, h], rs.at[1, h], me.other_core()))
+                pass_sums(h)
         dq_ref[head_rows, :] = (dq * HEAD**-0.5).astype(BF)
-        if h == OWN - 1:
-            pass_sums(h)
 
     right, left = me.along_x(1), me.along_x(3)
     x_at = me.x_hi * 2 + me.x_lo
@@ -525,6 +524,15 @@
         pl.when((u // 2) % 2 == 0)(lambda: x_copy(u, src, dst, 0, right).start())
         pl.when((u // 2) % 2 == 1)(lambda: x_copy(u, src, dst, 0, left).start())
 
+    def straight(u):
+        rows = unit_rows(u)
+        x_copy(u, s1.at[hi_left, rows, :], wr2.at[2, rows, :], 2, left).start()
+        x_copy(u, s1.at[hi_right, rows, :], wr2.at[1, rows, :], 1, right).start()
+
+    def straight_opposite(u, z):
+        rows = unit_rows(u)
+        x_copy(u, s1.at[1 - me.x_hi, rows, :], wr2.at[0, rows, :], 0, me.far()).start()
+
     def pass_on(u):
         rows = unit_rows(u)
         pl.when((u // 2) % 2 == 0)(lambda: x_copy(u, s1.at[hi_left, rows, :], wr2.at[2, rows, :], 2, left).start())
@@ -552,6 +560,16 @@
         x_copy(u, s1.at[0, rows, :], wr2.at[2, rows, :], 2, left).wait_recv()
         zout[rows, :] = (
             s1[me.x_hi, rows, :].astype(F32) + wr2[1, rows, :].astype(F32) + wr2[2, rows, :].astype(F32)
+        ).astype(BF)
+        pl.when(z != me.z)(lambda: z_copy(u, z).start())
+
+    def over_x_straight(u, z):
+        rows = unit_rows(u)
+        for kind in range(3):
+            x_copy(u, s1.at[0, rows, :], wr2.at[kind, rows, :], kind, right).wait_recv()
+        zout[rows, :] = (
+            s1[me.x_hi, rows, :].astype(F32) + wr2[0, rows, :].astype(F32)
+            + wr2[1, rows, :].astype(F32) + wr2[2, rows, :].astype(F32)
         ).astype(BF)
         pl.when(z != me.z)(lambda: z_copy(u, z).start())
 
@@ -583,6 +601,10 @@
             weight_rows(OWN - 1)
             to_core(288, 96)
             to_core(480, 96)
+        if r == 1:
+            f_rest = [go(dn_ref.at[rest_rows, :], full_r.at[0, pl.ds(half, half), :], ns.at[4], nr.at[4], up)]
+        if r == 3:
+            f_rest.append(go(dn_ref.at[first_rows, :], full_r.at[1, pl.ds(0, half), :], ns.at[5], nr.at[5], down))
         terms = part * n_ref[rows, :].astype(F32)
         gain_terms = gain_terms + jnp.sum(terms.reshape(TOK // 8, 8, D), axis=0)
     gain_terms = jnp.sum(gain_terms, axis=0, keepdims=True)
@@ -600,16 +622,12 @@
     g_y = [go(gy.at[y], gy.at[y], gs.at[r], gr.at[r], me.along_y(r)) for r in range(1, NY)]
     h_up.wait_recv()
     block = rows_at(((y + 1) % NY) * TOK, half)
-    rest = rows_at(((y + 1) % NY) * TOK + half, half)
-    to_up[:half, :] = (dn_ref[block, :].astype(F32) + half_r[0].astype(F32)).astype(BF)
-    to_up[half:, :] = dn_ref[rest, :]
-    f_up = go(to_up, full_r.at[0], ns.at[2], nr.at[2], up)
+    to_up[...] = (dn_ref[block, :].astype(F32) + half_r[0].astype(F32)).astype(BF)
+    f_up = go(to_up, full_r.at[0, pl.ds(0, half), :], ns.at[2], nr.at[2], up)
     h_down.wait_recv()
-    block = rows_at(((y + 3) % NY) * TOK, half)
-    rest = rows_at(((y + 3) % NY) * TOK + half, half)
-    to_down[:half, :] = dn_ref[block, :]
-    to_down[half:, :] = (dn_ref[rest, :].astype(F32) + half_r[1].astype(F32)).astype(BF)
-    f_down = go(to_down, full_r.at[1], ns.at[3], nr.at[3], down)
+    block = rows_at(((y + 3) % NY) * TOK + half, half)
+    to_down[...] = (dn_ref[block, :].astype(F32) + half_r[1].astype(F32)).astype(BF)
+    f_down = go(to_down, full_r.at[1, pl.ds(half, half), :], ns.at[3], nr.at[3], down)
 
     each_unit(me, None, pass_on, LATE)
     each_unit(me, over_x, None, EARLY)
@@ -651,8 +669,8 @@
     spread = jnp.mean(centred * centred, axis=1, keepdims=True)
     scale = lax.rsqrt(spread + EPS)
     hat = centred * scale
-    f_up.wait_recv()
-    f_down.wait_recv()
+    for c in f_rest + [f_up, f_down]:
+        c.wait_recv()
     d_normed = (
         dn_ref[rows_at(y * TOK, TOK), :].astype(F32) + full_r[0].astype(F32) + full_r[1].astype(F32)
     )
@@ -719,7 +737,7 @@
             pltpu.VMEM((NY * QW, TOK), BF),
             pltpu.VMEM((NY, UNIT, 128), BF),
             dma(4),
-            dma(4), dma(4), dma(4), dma(4), dma(3), dma(4), dma(8), dma(8),
+            dma(6), dma(6), dma(4), dma(4), dma(3), dma(4), dma(8), dma(8),
             dma(3, 8), dma(3, 8), dma(2), dma(2),
             pltpu.VMEM((2 * QW, D), BF),
             pltpu.VMEM((SEQ, 2 * QW), BF),
@@ -740,8 +758,8 @@
             pltpu.VMEM((16, 128), F32),
             pltpu.VMEM((BLOCK, 128), F32),
             pltpu.VMEM((2, TOK // 2, D), BF),
-            pltpu.VMEM((TOK, D), BF),
-            pltpu.VMEM((TOK, D), BF),
+            pltpu.VMEM((TOK // 2, D), BF),
+            pltpu.VMEM((TOK // 2, D), BF),
             pltpu.VMEM((2, TOK, D), BF),
             pltpu.VMEM((2, PW, GW), BF),
             pltpu.VMEM((2, PW, GW), BF),
@@ -754,7 +772,7 @@
             pltpu.VMEM((NY, 16, 128), F32),
             pltpu.VMEM((4, 16, 128), F32),
             pltpu.VMEM((NZ, 16, 128), F32),
-            dma(4), dma(4), dma(2, 4), dma(2, 4), dma(3, 12), dma(3, 12), dma(12), dma(8),
+            dma(6), dma(6), dma(2, 4), dma(2, 4), dma(3, 12), dma(3, 12), dma(12), dma(8),
             dma(4), dma(3), dma(14), dma(14),
         ],
         compiler_params=pltpu.CompilerParams(
@@ -764,10 +782,28 @@
     )(x, gain, w, cot)
 
 
+def hand_over_kernel(a, b, c, g, a_out, b_out, c_out, g_out):
+    a_out[...] = a[...]
+    b_out[...] = b[...]
+    c_out[...] = c[...]
+    g_out[...] = g[...].reshape(D)
+
+
+def hand_over(*arrays):
+    shapes = [jax.ShapeDtypeStruct(v.shape, v.dtype) for v in arrays[:3]]
+    return pl.pallas_call(
+        hand_over_kernel,
+        out_shape=tuple(shapes) + (jax.ShapeDtypeStruct((D,), F32),),
+        in_specs=[VMEM] * 4,
+        out_specs=(VMEM,) * 4,
+        name="hand_over",
+    )(*arrays)
+
+
 def shards(tokens, norm_gain, qkv_weight, d_context):
-    x, gain = tokens[0], norm_gain[None, :]
-    context, d_tokens, weight_grad, gain_grad = block(x, gain, qkv_weight.T, d_context[0])
-    return (context[None], d_tokens[None], weight_grad.T, gain_grad.reshape(D))
+    outputs = block(tokens[0], norm_gain[None, :], qkv_weight.T, d_context[0])
+    context, d_tokens, weight_grad, gain_grad = hand_over(*outputs)
+    return (context[None], d_tokens[None], weight_grad.T, gain_grad)
 
 
 def solution(mesh):

time: 92.1 us -> 89.6 us (0.973)
  local copies, waits for them, and re-layouts: 4.46 us -> 1.28 us
  Pallas kernels: 85.4 us -> 87.5 us
  other arithmetic: 1.36 us -> 0 us
    unnamed x9 -> x2, local copies, waits for them, and re-layouts: 3.86 us -> 0.68 us
    pallas_call x0 -> x1, Pallas kernels: none -> 1.96 us  [hand_over(): pl.pallas_call(hand_over_kernel, out_shape=tuple(shapes) + (jax.ShapeDtyp...]
    pallas_call x1 -> x0, other arithmetic: 1.36 us -> none  [block(): pl.pallas_call(block_kernel, out_shape=(jax.ShapeDtypeStruct((TOK, NY * Q...]
where the time goes in v6:
time: 89.6 us; the launch traced here: 89.5 us
  Pallas kernels  87.5 us (98%)
  local copies, waits for them, and re-layouts  1.28 us (1%)
    pallas_call x1, Pallas kernels, block(): pl.pallas_call(block_kernel, out_shape=(jax.ShapeDtypeStruct((TOK, NY * Q...  85.6 us
    pallas_call x1, Pallas kernels, hand_over(): pl.pallas_call(hand_over_kernel, out_shape=tuple(shapes) + (jax.ShapeDtyp...  1.96 us

profile of v6, /device:TPU:2, one launch (start us, length us, event | category | flops | bytes accessed | tf_op | source)
XLA Modules:
  0.0 89.5 jit_solution(1456905491597580737)
XLA Ops:
  0.6 0.0 copy-start
  0.6 0.7 copy-done
  1.3 0.6 broadcast_in_dim.9.gain_hbm
  1.9 85.6 %block.1 = (bf16[128,768]{1,0:T(8,128)(2,1)}, bf16[128,1536]{1,0:T(8,128)(2,1)}, f32[144,96]{1,0:T(8,128)}, f32[1,1536]{1,0:T(1,128)}) custom-call(bf16[128,1536]{1,0:T(8,128)(2,1)} %bitcast.6, bf16[1,1536]{1,0:T(2,128)(2,1)} %broadcast_in_dim.9.gain_hbm, bf16[144,96]{1,0:T(8,128)(2,1)} %bitcast.8, bf16[128,768]{1,0:T(8,128)(2,1)} %bitcast.7), custom_call_target="tpu_custom_call" | custom-call | tf_op jit(solution)/shard_map/block/pallas_call | solution.py:718
  87.5 2.0 %hand_over.1 = (bf16[128,768]{1,0:T(8,128)(2,1)}, bf16[128,1536]{1,0:T(8,128)(2,1)}, f32[144,96]{1,0:T(8,128)}, f32[1536]{0:T(1024)}) custom-call(bf16[128,768]{1,0:T(8,128)(2,1)} %get-tuple-element.12.a, bf16[128,1536]{1,0:T(8,128)(2,1)} %get-tuple-element.13.b, f32[144,96]{1,0:T(8,128)} %get-tuple-element.14.c, f32[1,1536]{1,0:T(1,128)} %get-tuple-element.15.g), custom_call_target="tpu_custom_call" | custom-call | tf_op jit(solution)/shard_map/hand_over/pallas_call | solution.py:794
Async XLA Ops:
  0.6 0.7 copy-start

commit v7 on v6

--- a/solution.py
+++ b/solution.py
@@ -53,7 +53,8 @@
             x_lo, z = unit_home(u, y)
             self.homes.append(self.id(x_lo=x_lo, z=z, y=y))
             self.sends.append((y != self.y) | (x_lo != self.x_lo) | (z != self.z))
-        self.has, self.unit = unit_at(self.x_lo, self.z, self.y)
+        self.starts = [((16 * k + 4 * self.y) // SHARD) % NZ for k in range(SHARD)]
+        self.has, self.unit = unit_at(self.x_lo, self.z, self.starts)
         volume, self.place = unit_source(self.unit, self.y)
         elsewhere = volume != self.x_lo * NZ + self.z
         self.sources = [self.id(x_lo=volume // NZ, z=volume % NZ, y=k) for k in range(NY)]
@@ -155,11 +156,12 @@
     return u % 2, ((16 * (u // 4) + 4 * y) // SHARD + (u % 4) // 2) % NZ
 
 
-def unit_at(x_lo, z, y):
+def unit_at(x_lo, z, starts):
     found, unit = jnp.int32(0), jnp.int32(0)
     for k in range(SHARD):
+        ahead = z - starts[k]
         for h in range(2):
-            hit = (((16 * k + 4 * y) // SHARD + h) % NZ == z).astype(jnp.int32)
+            hit = ((ahead == h) | (ahead == h - NZ)).astype(jnp.int32)
             found, unit = found + hit, unit + hit * (4 * k + 2 * h)
     return found > 0, unit + x_lo
 
@@ -171,7 +173,9 @@
 
 def each_unit(me, here, there, spans):
     def step(u, carry):
-        x_lo, z = unit_home(u, me.y)
+        k, i = u // 4, u % 4
+        z = jnp.where(k == 0, me.starts[0], jnp.where(k == 1, me.starts[1], me.starts[2])) + i // 2
+        x_lo, z = i % 2, jnp.where(z >= NZ, z - NZ, z)
         if here is not None:
             pl.when(x_lo == me.x_lo)(lambda: here(u, z))
         if there is not None:
@@ -185,7 +189,8 @@
 def near_first(me, x_lo, act, first=0, end=NZ):
     def step(n, carry):
         r = jnp.where(n % 2 == 1, (n + 1) // 2, (NZ - n // 2) % NZ)
-        has, u = unit_at(x_lo, (me.z + NZ - r) % NZ, me.y)
+        z = me.z - r
+        has, u = unit_at(x_lo, jnp.where(z < 0, z + NZ, z), me.starts)
         pl.when(has)(lambda: act(r, u))
         return carry
 
@@ -217,7 +222,6 @@
         pl.when(me.sends[j])(lambda: y_copy(j).start())
 
     load(x_ref)
-    load(gain_ref)
     x = x_ref[...].astype(F32)
     centred = x - jnp.mean(x, axis=1, keepdims=True)
     spread = jnp.mean(centred * centred, axis=1, keepdims=True)
@@ -308,21 +312,24 @@
     for c in cot_copies:
         c.wait_recv()
 
-    @pl.when(me.has)
-    def _():
-        for r in range(1, NZ):
-            z_copy(me.unit, r).wait_send()
-
-    def sent_here(r, u):
-        x_copy(u, r, own, 0, right).wait_send()
-        x_copy(u, r, own, 1, left).wait_send()
-
-    near_first(me, me.x_lo, sent_here)
-    near_first(me, 1 - me.x_lo, lambda r, u: x_copy(u, r, own, 2, right).wait_send())
-    for j in range(SHARD):
-        pl.when(me.sends[j])(lambda: y_copy(j).wait_send())
-    for c in cot_copies + core_copies + n_rest + [n_up, n_down, f_up, f_down]:
-        c.wait_send()
+    def drain():
+        @pl.when(me.has)
+        def _():
+            for r in range(1, NZ):
+                z_copy(me.unit, r).wait_send()
+
+        def sent_here(r, u):
+            x_copy(u, r, own, 0, right).wait_send()
+            x_copy(u, r, own, 1, left).wait_send()
+
+        near_first(me, me.x_lo, sent_here)
+        near_first(me, 1 - me.x_lo, lambda r, u: x_copy(u, r, own, 2, right).wait_send())
+        for j in range(SHARD):
+            pl.when(me.sends[j])(lambda: y_copy(j).wait_send())
+        for c in cot_copies + core_copies + n_rest + [n_up, n_down, f_up, f_down]:
+            c.wait_send()
+
+    return drain
 
 
 def dma(*shape):
@@ -335,30 +342,31 @@
 LATE = ((6, 8), (10, 12))
 
 
-def block_kernel(x_hbm, gain_hbm, w_hbm, cot_hbm, ctx_ref, dx_ref, wout_ref, gout_ref,
+def block_kernel(x_hbm, gain_in, w_hbm, cot_hbm, ctx_ref, dx_ref, wout_ref, gout_ref,
                  x_ref, gain_ref, shard_ref, d_ctx, n_ref, w_ref, cot_ref, w_pad, cot_t, ybuf, ls,
                  *rest):
     me = Place()
     y = me.y
     me.find_units()
     ready = greet(me)
+    gain_ref[...] = gain_in[...].astype(F32).reshape(1, D)
     loads = {}
     for k, (src, dst) in enumerate(
-        ((w_hbm, shard_ref), (x_hbm, x_ref), (gain_hbm, gain_ref), (cot_hbm, d_ctx))
+        ((w_hbm, shard_ref), (x_hbm, x_ref), (cot_hbm, d_ctx))
     ):
         c = pltpu.make_async_copy(src, dst, ls.at[k])
         c.start()
         loads[id(dst)] = c
-    gather_phase(
+    drain = gather_phase(
         me, ready, lambda ref: loads[id(ref)].wait(), x_ref, gain_ref, shard_ref, d_ctx,
         n_ref, w_ref, cot_ref, w_pad, cot_t, ybuf, *rest[:12],
     )
     back_phase(
-        me, n_ref, w_ref, cot_ref, x_ref, gain_ref, ctx_ref, dx_ref, wout_ref, gout_ref, *rest[12:]
+        me, drain, n_ref, w_ref, cot_ref, x_ref, gain_ref, ctx_ref, dx_ref, wout_ref, gout_ref, *rest[12:]
     )
 
 
-def back_phase(me, n_ref, w_ref, cot_ref, x_ref, gain_ref, ctx_ref, dx_ref, wout_ref, gout_ref,
+def back_phase(me, drain, n_ref, w_ref, cot_ref, x_ref, gain_ref, ctx_ref, dx_ref, wout_ref, gout_ref,
                wuse, kvall, dkv, ctx_own, ctx_out, dq_ref, dq_own, out_ref, s_buf, e_buf, r1, mid, r2,
                ks, kr, ss, rs, cs, cr,
                dn_ref, wg_ref, gg_ref, w_sums,
@@ -424,29 +432,38 @@
         ).astype(BF)
 
     zeros = jnp.zeros((HEAD, ROWS), BF)
+    q_pads, tops = [], []
+
+    def score(h, at):
+        for keys, rows in chunks(at):
+            s = jnp.dot(kvall[keys, head_lanes(h)], q_pads[h], preferred_element_type=F32)
+            s_buf[h, rows, :] = s
+            tops[h] = jnp.maximum(tops[h], jnp.max(s.reshape(CHUNK // 8, 8, ROWS), axis=0))
+
+    for h in range(OWN):
+        q = queries[h * HEAD : (h + 1) * HEAD, :] * jnp.asarray(HEAD**-0.5, BF)
+        q_pads.append(jnp.concatenate([q, zeros], axis=0))
+        tops.append(jnp.full((8, ROWS), -jnp.inf, F32))
+        score(h, 0)
+    for h in range(OWN):
+        k_core[h].wait_recv()
+        score(h, 1)
+    drain()
+    pass_keys(0)
     for h in range(OWN):
         lanes = head_lanes(h)
         head_rows = slice(h * HEAD, (h + 1) * HEAD)
-        q = queries[head_rows, :] * jnp.asarray(HEAD**-0.5, BF)
-        q_pad = jnp.concatenate([q, zeros], axis=0)
-        top = jnp.full((8, ROWS), -jnp.inf, F32)
-        for at in range(NA):
-            if at == 1:
-                k_core[h].wait_recv()
-            if at == 2 and h == 0:
-                pass_keys(0)
-            if at == 3:
-                k_pass[h].wait_recv()
-            for keys, rows in chunks(at):
-                s = jnp.dot(kvall[keys, lanes], q_pad, preferred_element_type=F32)
-                s_buf[rows, :] = s
-                top = jnp.maximum(top, jnp.max(s.reshape(CHUNK // 8, 8, ROWS), axis=0))
+        q_pad = q_pads[h]
+        score(h, 2)
+        k_pass[h].wait_recv()
+        score(h, 3)
+        top = tops[h]
         top = jnp.max(top, axis=0, keepdims=True)
         total = jnp.zeros((8, ROWS), F32)
         ctx = jnp.zeros((HEAD, ROWS), F32)
         for at in range(NA):
             for keys, rows in chunks(at):
-                e = jnp.exp(s_buf[rows, :] - top)
+                e = jnp.exp(s_buf[h, rows, :] - top)
                 total = total + jnp.sum(e.reshape(CHUNK // 8, 8, ROWS), axis=0)
                 e_low = e.astype(BF)
                 e_buf[rows, :] = e_low
@@ -584,6 +601,9 @@
     from_core(1, 384, 96)
     each_unit(me, to_opposite, None, EARLY)
     finish(OWN - 1)
+    weight_rows(OWN - 1)
+    to_core(288, 96)
+    to_core(480, 96)
     dq_own[...] = dq_ref[...].T
     gain_terms = jnp.zeros((8, D), F32)
     for r in (2, 1, 3, 0):
@@ -598,9 +618,6 @@
         if r == 2:
             h_up = go(dn_ref.at[first_rows, :], half_r.at[0], ns.at[0], nr.at[0], up)
             h_down = go(dn_ref.at[rest_rows, :], half_r.at[1], ns.at[1], nr.at[1], down)
-            weight_rows(OWN - 1)
-            to_core(288, 96)
-            to_core(480, 96)
         if r == 1:
             f_rest = [go(dn_ref.at[rest_rows, :], full_r.at[0, pl.ds(half, half), :], ns.at[4], nr.at[4], up)]
         if r == 3:
@@ -723,11 +740,11 @@
             jax.ShapeDtypeStruct((BLOCK, SLAB), F32),
             jax.ShapeDtypeStruct((1, D), F32),
         ),
-        in_specs=[pl.BlockSpec(memory_space=pl.ANY)] * 4,
+        in_specs=[pl.BlockSpec(memory_space=m) for m in (pl.ANY, pltpu.VMEM, pl.ANY, pl.ANY)],
         out_specs=(VMEM,) * 4,
         scratch_shapes=[
             pltpu.VMEM((TOK, D), BF),
-            pltpu.VMEM((1, D), BF),
+            pltpu.VMEM((1, D), F32),
             pltpu.VMEM((BLOCK, SLAB), BF),
             pltpu.VMEM((TOK, NY * QW), BF),
             pltpu.VMEM((ROWS, D), BF),
@@ -747,7 +764,7 @@
             pltpu.VMEM((QW, ROWS), BF),
             pltpu.VMEM((ROWS, QW), BF),
             pltpu.VMEM((ROWS, 2 * QW), BF),
-            pltpu.VMEM((SEQ, ROWS), F32),
+            pltpu.VMEM((OWN, SEQ, ROWS), F32),
             pltpu.VMEM((SEQ, ROWS), BF),
             pltpu.VMEM((2, ROWS, 2 * QW), BF),
             pltpu.VMEM((ROWS, 2 * QW), BF),
@@ -801,7 +818,7 @@
 
 
 def shards(tokens, norm_gain, qkv_weight, d_context):
-    outputs = block(tokens[0], norm_gain[None, :], qkv_weight.T, d_context[0])
+    outputs = block(tokens[0], norm_gain, qkv_weight.T, d_context[0])
     context, d_tokens, weight_grad, gain_grad = hand_over(*outputs)
     return (context[None], d_tokens[None], weight_grad.T, gain_grad)
 

time: 89.6 us -> 87 us (0.971)
  Pallas kernels: 87.5 us -> 86.2 us
  local copies, waits for them, and re-layouts: 1.28 us -> 0 us
    pallas_call x1, Pallas kernels: 85.6 us -> 84.3 us  [block(): pl.pallas_call(block_kernel, out_shape=(jax.ShapeDtypeStruct((TOK, NY * Q...]
where the time goes in v7:
time: 87 us; the launch traced here: 86.9 us
  Pallas kernels  86.2 us (99%)
    pallas_call x1, Pallas kernels, block(): pl.pallas_call(block_kernel, out_shape=(jax.ShapeDtypeStruct((TOK, NY * Q...  84.3 us
    pallas_call x1, Pallas kernels, hand_over(): pl.pallas_call(hand_over_kernel, out_shape=tuple(shapes) + (jax.ShapeDtyp...  1.96 us

profile of v7, /device:TPU:2, one launch (start us, length us, event | category | flops | bytes accessed | tf_op | source)
XLA Modules:
  0.0 86.9 jit_solution(7724047405853518718)
XLA Ops:
  0.6 84.3 %block.1 = (bf16[128,768]{1,0:T(8,128)(2,1)}, bf16[128,1536]{1,0:T(8,128)(2,1)}, f32[144,96]{1,0:T(8,128)}, f32[1,1536]{1,0:T(1,128)}) custom-call(bf16[128,1536]{1,0:T(8,128)(2,1)} %bitcast.6, bf16[1536]{0:T(1024)(128)(2,1)} %gain_in.1, bf16[144,96]{1,0:T(8,128)(2,1)} %bitcast.8, bf16[128,768]{1,0:T(8,128)(2,1)} %bitcast.7), custom_call_target="tpu_custom_call" | custom-call | tf_op jit(solution)/shard_map/block/pallas_call | solution.py:735
  84.9 2.0 %hand_over.1 = (bf16[128,768]{1,0:T(8,128)(2,1)}, bf16[128,1536]{1,0:T(8,128)(2,1)}, f32[144,96]{1,0:T(8,128)}, f32[1536]{0:T(1024)}) custom-call(bf16[128,768]{1,0:T(8,128)(2,1)} %get-tuple-element.12.a, bf16[128,1536]{1,0:T(8,128)(2,1)} %get-tuple-element.13.b, f32[144,96]{1,0:T(8,128)} %get-tuple-element.14.c, f32[1,1536]{1,0:T(1,128)} %get-tuple-element.15.g), custom_call_target="tpu_custom_call" | custom-call | tf_op jit(solution)/shard_map/hand_over/pallas_call | solution.py:811

commit v8 on v7

--- a/solution.py
+++ b/solution.py
@@ -704,6 +704,24 @@
     total = jnp.concatenate([total[k : k + 1, :] for k in range(D // 128)], axis=1)
     gout_ref[...] = to_natural(total) / gain_ref[...].astype(F32) * FACTOR
 
+    for c in ctx_copies:
+        c.wait_recv()
+    ctx_ref[...] = ctx_out[...].T
+
+    def sent_here(u, z):
+        rows = unit_rows(u)
+        x_copy(u, w_mid.at[rows, :], wr2.at[0, rows, :], 0, right).wait_send()
+        pl.when(z != me.z)(lambda: z_copy(u, z).wait_send())
+
+    def sent_there(u):
+        rows = unit_rows(u)
+        x_copy(u, w_mid.at[rows, :], wr2.at[1, rows, :], 1, right).wait_send()
+        x_copy(u, w_mid.at[rows, :], wr2.at[2, rows, :], 2, left).wait_send()
+
+    each_unit(me, sent_here, sent_there, ((0, UNITS),))
+    for c in sent:
+        c.wait_send()
+
     for j in range(SHARD):
         rows = pl.ds(j * UNIT, UNIT)
         pl.when(me.sends[j])(
@@ -712,23 +730,6 @@
     for k in range(NY):
         pl.when(me.gets[k])(lambda: y_copy(k).wait_send())
     wout_ref[...] = w_sums[...][:, :SLAB] * FACTOR
-    for c in ctx_copies:
-        c.wait_recv()
-    ctx_ref[...] = ctx_out[...].T
-
-    def sent_here(u, z):
-        rows = unit_rows(u)
-        x_copy(u, w_mid.at[rows, :], wr2.at[0, rows, :], 0, right).wait_send()
-        pl.when(z != me.z)(lambda: z_copy(u, z).wait_send())
-
-    def sent_there(u):
-        rows = unit_rows(u)
-        x_copy(u, w_mid.at[rows, :], wr2.at[1, rows, :], 1, right).wait_send()
-        x_copy(u, w_mid.at[rows, :], wr2.at[2, rows, :], 2, left).wait_send()
-
-    each_unit(me, sent_here, sent_there, ((0, UNITS),))
-    for c in sent:
-        c.wait_send()
 
 
 def block(x, gain, w, cot):

time: 87 us -> 86.5 us (level)
  no operation moved by 1% of the time
where the time goes in v8:
time: 86.5 us; the launch traced here: 86.4 us
  Pallas kernels  85.7 us (99%)
    pallas_call x1, Pallas kernels, block(): pl.pallas_call(block_kernel, out_shape=(jax.ShapeDtypeStruct((TOK, NY * Q...  83.8 us
    pallas_call x1, Pallas kernels, hand_over(): pl.pallas_call(hand_over_kernel, out_shape=tuple(shapes) + (jax.ShapeDtyp...  1.96 us

profile of v8, /device:TPU:2, one launch (start us, length us, event | category | flops | bytes accessed | tf_op | source)
XLA Modules:
  0.0 86.4 jit_solution(1333192548780705384)
XLA Ops:
  0.6 83.8 %block.1 = (bf16[128,768]{1,0:T(8,128)(2,1)}, bf16[128,1536]{1,0:T(8,128)(2,1)}, f32[144,96]{1,0:T(8,128)}, f32[1,1536]{1,0:T(1,128)}) custom-call(bf16[128,1536]{1,0:T(8,128)(2,1)} %bitcast.6, bf16[1536]{0:T(1024)(128)(2,1)} %gain_in.1, bf16[144,96]{1,0:T(8,128)(2,1)} %bitcast.8, bf16[128,768]{1,0:T(8,128)(2,1)} %bitcast.7), custom_call_target="tpu_custom_call" | custom-call | tf_op jit(solution)/shard_map/block/pallas_call | solution.py:736
  84.4 2.0 %hand_over.1 = (bf16[128,768]{1,0:T(8,128)(2,1)}, bf16[128,1536]{1,0:T(8,128)(2,1)}, f32[144,96]{1,0:T(8,128)}, f32[1536]{0:T(1024)}) custom-call(bf16[128,768]{1,0:T(8,128)(2,1)} %get-tuple-element.12.a, bf16[128,1536]{1,0:T(8,128)(2,1)} %get-tuple-element.13.b, f32[144,96]{1,0:T(8,128)} %get-tuple-element.14.c, f32[1,1536]{1,0:T(1,128)} %get-tuple-element.15.g), custom_call_target="tpu_custom_call" | custom-call | tf_op jit(solution)/shard_map/hand_over/pallas_call | solution.py:812
